TPU v7x, 512 devices: a whole 4x8x8 slice. The times are simulated.
512 devices in a mesh: outer: 32 (over z, y_hi), inner: 16 (over x, y_lo, core).
Axes of the slice: x: 4, y: 8 (y_hi: 4, y_lo: 2; y = y_hi * 2 + y_lo), z: 8, core: 2. Of those that a mesh axis runs over, the one named last changes fastest.
Arguments:
- queries: bfloat16 [131072, 256], P(('outer', 'inner')), may hold values from -24 to 24, as said below
- keys: bfloat16 [131072, 256], P(('outer', 'inner')), may hold values from -24 to 24, as said below
- values: bfloat16 [131072, 256], P(('outer', 'inner')), may hold values from -6 to 6
- grad_out: bfloat16 [131072, 256], P(('outer', 'inner')), may hold values from -6 to 6
- group_lengths: int32 [256], replicated, may hold values from 1 to 1024, 131072 in all
Outputs:
- grad_queries: bfloat16 [131072, 256], P(('outer', 'inner'))
- grad_keys: bfloat16 [131072, 256], P(('outer', 'inner'))
- grad_values: bfloat16 [131072, 256], P(('outer', 'inner'))
Inputs may be any that keep to these rules, and one draw needn't show every extreme that they name: `queries`: shown draw: independent entries; scores of order one. `keys`: shown draw: independent entries.
All inputs are finite; a program needn't handle non-finite values.
Results may differ from a plain program's by a relative error of at most 0.017.
Values may be sent and summed in bfloat16 or wider, within the bound.
No kernel may reach another device: no remote copies, remote signals or barrier semaphores. Data moves between devices by JAX's collectives and lax.ppermute only.
A program may use at most 64 MiB of HBM per device.

v0:
```python
import math

import jax
import jax.numpy as jnp
from jax import lax
from jax.sharding import PartitionSpec as P

HEADS = 2
CTX = 2


def passed_along(value, axis, steps):
    count = lax.axis_size(axis)
    first, last = (max(0, -steps), min(count, count - steps))
    return lax.ppermute(value, axis, [(source, source + steps) for source in range(first, last)])


def shifted(block, axis, distance):
    devices = range(lax.axis_size(axis))
    route = [((i - distance) % len(devices), i) for i in devices]
    return lax.ppermute(block, axis, route)


def group_of(pos, ends):
    return jnp.sum((ends[None, :] <= pos[:, None]).astype(jnp.int32), axis=1)


def allowed_pairs(qpos, kpos, ends, total):
    cq = group_of(qpos, ends)
    ck = group_of(kpos, ends)
    valid = (qpos < total)[:, None] & ((kpos >= 0) & (kpos < total))[None, :]
    return valid & (ck[None, :] <= cq[:, None]) & (ck[None, :] >= cq[:, None] - CTX)


def split_heads(block):
    return block.reshape(block.shape[0], HEADS, block.shape[1] // HEADS)


def score_block(q_rows, k_rows, scale):
    return (
        jnp.einsum(
            "qhd,khd->hqk",
            split_heads(q_rows),
            split_heads(k_rows),
            preferred_element_type=jnp.float32,
        )
        * scale
    )


def stats_update(top, total, q_rows, k_rows, mask, scale):
    scores = score_block(q_rows, k_rows, scale)
    block_top = jnp.max(jnp.where(mask[None], scores, -jnp.inf), axis=2)
    new_top = jnp.maximum(top, block_top)
    new_total = total * jnp.exp(top - new_top) + jnp.sum(
        jnp.where(mask[None], jnp.exp(scores - new_top[:, :, None]), 0.0), axis=2
    )
    return (new_top, new_total)


def output_term(q_rows, lse, k_rows, v_rows, mask, scale):
    scores = score_block(q_rows, k_rows, scale)
    probs = jnp.where(mask[None], jnp.exp(scores - lse[:, :, None]), 0.0).astype(jnp.bfloat16)
    return jnp.einsum(
        "hqk,khd->qhd", probs, split_heads(v_rows), preferred_element_type=jnp.float32
    )


def grad_terms(q_rows, g_rows, lse, delta, k_rows, v_rows, mask, scale):
    scores = score_block(q_rows, k_rows, scale)
    probs = jnp.where(mask[None], jnp.exp(scores - lse[:, :, None]), 0.0)
    probs_b = probs.astype(jnp.bfloat16)
    g_three = split_heads(g_rows)
    dprobs = jnp.einsum(
        "qhd,khd->hqk", g_three, split_heads(v_rows), preferred_element_type=jnp.float32
    )
    dscores = (probs * (dprobs - delta[:, :, None])).astype(jnp.bfloat16)
    dv_term = jnp.einsum("hqk,qhd->khd", probs_b, g_three, preferred_element_type=jnp.float32)
    dk_term = (
        jnp.einsum("hqk,qhd->khd", dscores, split_heads(q_rows), preferred_element_type=jnp.float32)
        * scale
    )
    dq_term = (
        jnp.einsum("hqk,khd->qhd", dscores, split_heads(k_rows), preferred_element_type=jnp.float32)
        * scale
    )
    return (
        dq_term.reshape(q_rows.shape[0], -1),
        dk_term.reshape(k_rows.shape[0], -1),
        dv_term.reshape(k_rows.shape[0], -1),
    )


def per_device(queries, keys, values, grad_out, group_lengths):
    rows = queries.shape[0]
    width = queries.shape[1]
    devices = lax.axis_size(("outer", "inner"))
    reach = 3 * lax.axis_size("inner") // 4
    total = rows * devices
    here = lax.axis_index(("outer", "inner"))
    scale = 1.0 / math.sqrt(width // HEADS)
    ends = jnp.cumsum(group_lengths)
    offsets = jnp.arange(rows, dtype=jnp.int32)
    own_pos = here * rows + offsets

    def key_positions(step):
        return (here - step) * rows + offsets

    own_mask = allowed_pairs(own_pos, own_pos, ends, total)
    start_top = jnp.full((HEADS, rows), -jnp.inf, jnp.float32)
    start_total = jnp.zeros((HEADS, rows), jnp.float32)
    top, total_sum = stats_update(start_top, start_total, queries, keys, own_mask, scale)

    def stats_step(step, carry):
        k_rows, top, total_sum = carry
        k_rows = passed_along(k_rows, ("outer", "inner"), 1)
        mask = allowed_pairs(own_pos, key_positions(step), ends, total)
        top, total_sum = stats_update(top, total_sum, queries, k_rows, mask, scale)
        return (k_rows, top, total_sum)

    _, top, total_sum = lax.fori_loop(1, reach + 1, stats_step, (keys, top, total_sum))
    lse = top + jnp.log(total_sum)
    output = output_term(queries, lse, keys, values, own_mask, scale)

    def output_step(step, carry):
        k_rows, v_rows, output = carry
        k_rows, v_rows = passed_along((k_rows, v_rows), ("outer", "inner"), 1)
        mask = allowed_pairs(own_pos, key_positions(step), ends, total)
        return (k_rows, v_rows, output + output_term(queries, lse, k_rows, v_rows, mask, scale))

    _, _, output = lax.fori_loop(1, reach + 1, output_step, (keys, values, output))
    delta = jnp.einsum("qhd,qhd->hq", split_heads(grad_out).astype(jnp.float32), output)
    dq_own, dk_own, dv_own = grad_terms(
        queries, grad_out, lse, delta, keys, values, own_mask, scale
    )

    def key_step(step, carry):
        k_rows, v_rows, dk_sum, dv_sum, dq_sum = carry
        k_rows, v_rows = passed_along((k_rows, v_rows), ("outer", "inner"), 1)
        dk_sum, dv_sum = shifted((dk_sum, dv_sum), ("outer", "inner"), 1)
        mask = allowed_pairs(own_pos, key_positions(step), ends, total)
        dq_term, dk_term, dv_term = grad_terms(
            queries, grad_out, lse, delta, k_rows, v_rows, mask, scale
        )
        return (k_rows, v_rows, dk_sum + dk_term, dv_sum + dv_term, dq_sum + dq_term)

    _, _, dk_sum, dv_sum, grad_q = lax.fori_loop(
        1, reach + 1, key_step, (keys, values, dk_own, dv_own, dq_own)
    )
    grad_k, grad_v = (
        shifted(dk_sum.astype(jnp.bfloat16), ("outer", "inner"), -reach).astype(dk_sum.dtype),
        shifted(dv_sum.astype(jnp.bfloat16), ("outer", "inner"), -reach).astype(dv_sum.dtype),
    )
    return (grad_q.astype(jnp.bfloat16), grad_k.astype(jnp.bfloat16), grad_v.astype(jnp.bfloat16))


def solution(mesh):
    placed = (
        P(("outer", "inner"), None),
        P(("outer", "inner"), None),
        P(("outer", "inner"), None),
        P(("outer", "inner"), None),
        P(),
    )
    return jax.shard_map(
        per_device,
        mesh=mesh,
        in_specs=placed,
        out_specs=(
            P(("outer", "inner"), None),
            P(("outer", "inner"), None),
            P(("outer", "inner"), None),
        ),
        check_vma=False,
    )
```

profile of v0, /device:TPU:247, one launch (start us, length us, event | category | flops | bytes accessed | tf_op | source)
XLA Modules:
  0.0 579.8 jit_solution(13424487249719471418)
XLA Ops:
  4.8 125.6 %while.64 = (s32[]{:T(128)}, bf16[256,256]{0,1:T(8,128)(2,1)S(1)}, f32[2,256]{1,0:T(2,128)S(1)}, f32[2,256]{1,0:T(2,128)S(1)}, s32[]{:T(128)}, /*index=5*/s32[25...) while((s32[]{:T(128)}, bf16[256,256]{0,1:T(8,128)(2,1)S(1)}, ...), condition=%wide.region_10.11_spmd.clone, body=%wide.region_5.10_spmd.clone.sunk | while | flops 35064580 | bytes 2333877 | solution.py:121
  24.1 6.3 %collective-permute-start = (bf16[256,256]{0,1:T(8,128)(2,1)S(1)}, bf16[256,256]{0,1:T(8,128)(2,1)S(1)}, u32[]{:S(2)}, u32[]{:S(2)}) collective-permute-start(bf16[256,256]{0,1:T(8,128)(2,1)S(1)} %get-tuple-element.1273), channel_id=1, source_target_pairs={{0,1},{1,2},{2,3},{3,4},{4,5},{5,6},{6,7},{7,8},{8,9},{9,10},{10,1... | collective-permute-start | bytes 393224 | tf_op jit(solution)/shard_map/while/body/eval_jaxpr/ppermute | solution.py:15
  32.8 9.8 %collective-permute-start = (bf16[256,256]{0,1:T(8,128)(2,1)S(1)}, bf16[256,256]{0,1:T(8,128)(2,1)S(1)}, u32[]{:S(2)}, u32[]{:S(2)}) collective-permute-start(bf16[256,256]{0,1:T(8,128)(2,1)S(1)} %get-tuple-element.1273), channel_id=1, source_target_pairs={{0,1},{1,2},{2,3},{3,4},{4,5},{5,6},{6,7},{7,8},{8,9},{9,10},{10,1... | collective-permute-start | bytes 393224 | tf_op jit(solution)/shard_map/while/body/eval_jaxpr/ppermute | solution.py:15
  45.0 9.8 %collective-permute-start = (bf16[256,256]{0,1:T(8,128)(2,1)S(1)}, bf16[256,256]{0,1:T(8,128)(2,1)S(1)}, u32[]{:S(2)}, u32[]{:S(2)}) collective-permute-start(bf16[256,256]{0,1:T(8,128)(2,1)S(1)} %get-tuple-element.1273), channel_id=1, source_target_pairs={{0,1},{1,2},{2,3},{3,4},{4,5},{5,6},{6,7},{7,8},{8,9},{9,10},{10,1... | collective-permute-start | bytes 393224 | tf_op jit(solution)/shard_map/while/body/eval_jaxpr/ppermute | solution.py:15
  57.2 9.8 %collective-permute-start = (bf16[256,256]{0,1:T(8,128)(2,1)S(1)}, bf16[256,256]{0,1:T(8,128)(2,1)S(1)}, u32[]{:S(2)}, u32[]{:S(2)}) collective-permute-start(bf16[256,256]{0,1:T(8,128)(2,1)S(1)} %get-tuple-element.1273), channel_id=1, source_target_pairs={{0,1},{1,2},{2,3},{3,4},{4,5},{5,6},{6,7},{7,8},{8,9},{9,10},{10,1... | collective-permute-start | bytes 393224 | tf_op jit(solution)/shard_map/while/body/eval_jaxpr/ppermute | solution.py:15
  69.4 9.8 %collective-permute-start = (bf16[256,256]{0,1:T(8,128)(2,1)S(1)}, bf16[256,256]{0,1:T(8,128)(2,1)S(1)}, u32[]{:S(2)}, u32[]{:S(2)}) collective-permute-start(bf16[256,256]{0,1:T(8,128)(2,1)S(1)} %get-tuple-element.1273), channel_id=1, source_target_pairs={{0,1},{1,2},{2,3},{3,4},{4,5},{5,6},{6,7},{7,8},{8,9},{9,10},{10,1... | collective-permute-start | bytes 393224 | tf_op jit(solution)/shard_map/while/body/eval_jaxpr/ppermute | solution.py:15
  81.6 9.8 %collective-permute-start = (bf16[256,256]{0,1:T(8,128)(2,1)S(1)}, bf16[256,256]{0,1:T(8,128)(2,1)S(1)}, u32[]{:S(2)}, u32[]{:S(2)}) collective-permute-start(bf16[256,256]{0,1:T(8,128)(2,1)S(1)} %get-tuple-element.1273), channel_id=1, source_target_pairs={{0,1},{1,2},{2,3},{3,4},{4,5},{5,6},{6,7},{7,8},{8,9},{9,10},{10,1... | collective-permute-start | bytes 393224 | tf_op jit(solution)/shard_map/while/body/eval_jaxpr/ppermute | solution.py:15
  93.8 9.8 %collective-permute-start = (bf16[256,256]{0,1:T(8,128)(2,1)S(1)}, bf16[256,256]{0,1:T(8,128)(2,1)S(1)}, u32[]{:S(2)}, u32[]{:S(2)}) collective-permute-start(bf16[256,256]{0,1:T(8,128)(2,1)S(1)} %get-tuple-element.1273), channel_id=1, source_target_pairs={{0,1},{1,2},{2,3},{3,4},{4,5},{5,6},{6,7},{7,8},{8,9},{9,10},{10,1... | collective-permute-start | bytes 393224 | tf_op jit(solution)/shard_map/while/body/eval_jaxpr/ppermute | solution.py:15
  106.0 9.8 %collective-permute-start = (bf16[256,256]{0,1:T(8,128)(2,1)S(1)}, bf16[256,256]{0,1:T(8,128)(2,1)S(1)}, u32[]{:S(2)}, u32[]{:S(2)}) collective-permute-start(bf16[256,256]{0,1:T(8,128)(2,1)S(1)} %get-tuple-element.1273), channel_id=1, source_target_pairs={{0,1},{1,2},{2,3},{3,4},{4,5},{5,6},{6,7},{7,8},{8,9},{9,10},{10,1... | collective-permute-start | bytes 393224 | tf_op jit(solution)/shard_map/while/body/eval_jaxpr/ppermute | solution.py:15
  118.2 9.8 %collective-permute-start = (bf16[256,256]{0,1:T(8,128)(2,1)S(1)}, bf16[256,256]{0,1:T(8,128)(2,1)S(1)}, u32[]{:S(2)}, u32[]{:S(2)}) collective-permute-start(bf16[256,256]{0,1:T(8,128)(2,1)S(1)} %get-tuple-element.1273), channel_id=1, source_target_pairs={{0,1},{1,2},{2,3},{3,4},{4,5},{5,6},{6,7},{7,8},{8,9},{9,10},{10,1... | collective-permute-start | bytes 393224 | tf_op jit(solution)/shard_map/while/body/eval_jaxpr/ppermute | solution.py:15
  132.6 177.8 %while.65 = (s32[]{:T(128)}, bf16[256,256]{0,1:T(8,128)(2,1)S(1)}, bf16[256,256]{0,1:T(8,128)(2,1)S(1)}, f32[256,2,128]{2,0,1:T(8,128)S(1)}, s32[]{:T(128)}, /*i...) while((s32[]{:T(128)}, bf16[256,256]{0,1:T(8,128)(2,1)S(1)}, ...), condition=%wide.region_14.15_spmd.clone, body=%wide.region_11.14_spmd.clone.sunk | while | flops 68421376 | bytes 2637029 | solution.py:131
  132.6 9.8 %collective-permute-start.2 = (bf16[256,256]{0,1:T(8,128)(2,1)S(1)}, bf16[256,256]{0,1:T(8,128)(2,1)S(1)}, u32[]{:S(2)}, u32[]{:S(2)}) collective-permute-start(bf16[256,256]{0,1:T(8,128)(2,1)S(1)} %get-tuple-element.1305), channel_id=1, source_target_pairs={{0,1},{1,2},{2,3},{3,4},{4,5},{5,6},{6,7},{7,8},{8,9},{9,10},{10,1... | collective-permute-start | bytes 393224 | tf_op jit(solution)/shard_map/while/body/eval_jaxpr/ppermute | solution.py:15
  142.4 10.7 %collective-permute-start.1 = (bf16[256,256]{0,1:T(8,128)(2,1)S(1)}, bf16[256,256]{0,1:T(8,128)(2,1)S(1)}, u32[]{:S(2)}, u32[]{:S(2)}) collective-permute-start(bf16[256,256]{0,1:T(8,128)(2,1)S(1)} %get-tuple-element.1304), channel_id=1, source_target_pairs={{0,1},{1,2},{2,3},{3,4},{4,5},{5,6},{6,7},{7,8},{8,9},{9,10},{10,1... | collective-permute-start | bytes 393224 | tf_op jit(solution)/shard_map/while/body/eval_jaxpr/ppermute | solution.py:15
  155.5 8.8 %collective-permute-start.2 = (bf16[256,256]{0,1:T(8,128)(2,1)S(1)}, bf16[256,256]{0,1:T(8,128)(2,1)S(1)}, u32[]{:S(2)}, u32[]{:S(2)}) collective-permute-start(bf16[256,256]{0,1:T(8,128)(2,1)S(1)} %get-tuple-element.1305), channel_id=1, source_target_pairs={{0,1},{1,2},{2,3},{3,4},{4,5},{5,6},{6,7},{7,8},{8,9},{9,10},{10,1... | collective-permute-start | bytes 393224 | tf_op jit(solution)/shard_map/while/body/eval_jaxpr/ppermute | solution.py:15
  169.6 8.8 %collective-permute-start.2 = (bf16[256,256]{0,1:T(8,128)(2,1)S(1)}, bf16[256,256]{0,1:T(8,128)(2,1)S(1)}, u32[]{:S(2)}, u32[]{:S(2)}) collective-permute-start(bf16[256,256]{0,1:T(8,128)(2,1)S(1)} %get-tuple-element.1305), channel_id=1, source_target_pairs={{0,1},{1,2},{2,3},{3,4},{4,5},{5,6},{6,7},{7,8},{8,9},{9,10},{10,1... | collective-permute-start | bytes 393224 | tf_op jit(solution)/shard_map/while/body/eval_jaxpr/ppermute | solution.py:15
  183.7 8.8 %collective-permute-start.2 = (bf16[256,256]{0,1:T(8,128)(2,1)S(1)}, bf16[256,256]{0,1:T(8,128)(2,1)S(1)}, u32[]{:S(2)}, u32[]{:S(2)}) collective-permute-start(bf16[256,256]{0,1:T(8,128)(2,1)S(1)} %get-tuple-element.1305), channel_id=1, source_target_pairs={{0,1},{1,2},{2,3},{3,4},{4,5},{5,6},{6,7},{7,8},{8,9},{9,10},{10,1... | collective-permute-start | bytes 393224 | tf_op jit(solution)/shard_map/while/body/eval_jaxpr/ppermute | solution.py:15
  197.7 8.8 %collective-permute-start.2 = (bf16[256,256]{0,1:T(8,128)(2,1)S(1)}, bf16[256,256]{0,1:T(8,128)(2,1)S(1)}, u32[]{:S(2)}, u32[]{:S(2)}) collective-permute-start(bf16[256,256]{0,1:T(8,128)(2,1)S(1)} %get-tuple-element.1305), channel_id=1, source_target_pairs={{0,1},{1,2},{2,3},{3,4},{4,5},{5,6},{6,7},{7,8},{8,9},{9,10},{10,1... | collective-permute-start | bytes 393224 | tf_op jit(solution)/shard_map/while/body/eval_jaxpr/ppermute | solution.py:15
  211.8 8.8 %collective-permute-start.2 = (bf16[256,256]{0,1:T(8,128)(2,1)S(1)}, bf16[256,256]{0,1:T(8,128)(2,1)S(1)}, u32[]{:S(2)}, u32[]{:S(2)}) collective-permute-start(bf16[256,256]{0,1:T(8,128)(2,1)S(1)} %get-tuple-element.1305), channel_id=1, source_target_pairs={{0,1},{1,2},{2,3},{3,4},{4,5},{5,6},{6,7},{7,8},{8,9},{9,10},{10,1... | collective-permute-start | bytes 393224 | tf_op jit(solution)/shard_map/while/body/eval_jaxpr/ppermute | solution.py:15
  225.9 8.8 %collective-permute-start.2 = (bf16[256,256]{0,1:T(8,128)(2,1)S(1)}, bf16[256,256]{0,1:T(8,128)(2,1)S(1)}, u32[]{:S(2)}, u32[]{:S(2)}) collective-permute-start(bf16[256,256]{0,1:T(8,128)(2,1)S(1)} %get-tuple-element.1305), channel_id=1, source_target_pairs={{0,1},{1,2},{2,3},{3,4},{4,5},{5,6},{6,7},{7,8},{8,9},{9,10},{10,1... | collective-permute-start | bytes 393224 | tf_op jit(solution)/shard_map/while/body/eval_jaxpr/ppermute | solution.py:15
  240.0 8.8 %collective-permute-start.2 = (bf16[256,256]{0,1:T(8,128)(2,1)S(1)}, bf16[256,256]{0,1:T(8,128)(2,1)S(1)}, u32[]{:S(2)}, u32[]{:S(2)}) collective-permute-start(bf16[256,256]{0,1:T(8,128)(2,1)S(1)} %get-tuple-element.1305), channel_id=1, source_target_pairs={{0,1},{1,2},{2,3},{3,4},{4,5},{5,6},{6,7},{7,8},{8,9},{9,10},{10,1... | collective-permute-start | bytes 393224 | tf_op jit(solution)/shard_map/while/body/eval_jaxpr/ppermute | solution.py:15
  254.1 8.8 %collective-permute-start.2 = (bf16[256,256]{0,1:T(8,128)(2,1)S(1)}, bf16[256,256]{0,1:T(8,128)(2,1)S(1)}, u32[]{:S(2)}, u32[]{:S(2)}) collective-permute-start(bf16[256,256]{0,1:T(8,128)(2,1)S(1)} %get-tuple-element.1305), channel_id=1, source_target_pairs={{0,1},{1,2},{2,3},{3,4},{4,5},{5,6},{6,7},{7,8},{8,9},{9,10},{10,1... | collective-permute-start | bytes 393224 | tf_op jit(solution)/shard_map/while/body/eval_jaxpr/ppermute | solution.py:15
  268.1 8.8 %collective-permute-start.2 = (bf16[256,256]{0,1:T(8,128)(2,1)S(1)}, bf16[256,256]{0,1:T(8,128)(2,1)S(1)}, u32[]{:S(2)}, u32[]{:S(2)}) collective-permute-start(bf16[256,256]{0,1:T(8,128)(2,1)S(1)} %get-tuple-element.1305), channel_id=1, source_target_pairs={{0,1},{1,2},{2,3},{3,4},{4,5},{5,6},{6,7},{7,8},{8,9},{9,10},{10,1... | collective-permute-start | bytes 393224 | tf_op jit(solution)/shard_map/while/body/eval_jaxpr/ppermute | solution.py:15
  282.2 8.8 %collective-permute-start.2 = (bf16[256,256]{0,1:T(8,128)(2,1)S(1)}, bf16[256,256]{0,1:T(8,128)(2,1)S(1)}, u32[]{:S(2)}, u32[]{:S(2)}) collective-permute-start(bf16[256,256]{0,1:T(8,128)(2,1)S(1)} %get-tuple-element.1305), channel_id=1, source_target_pairs={{0,1},{1,2},{2,3},{3,4},{4,5},{5,6},{6,7},{7,8},{8,9},{9,10},{10,1... | collective-permute-start | bytes 393224 | tf_op jit(solution)/shard_map/while/body/eval_jaxpr/ppermute | solution.py:15
  296.3 8.8 %collective-permute-start.2 = (bf16[256,256]{0,1:T(8,128)(2,1)S(1)}, bf16[256,256]{0,1:T(8,128)(2,1)S(1)}, u32[]{:S(2)}, u32[]{:S(2)}) collective-permute-start(bf16[256,256]{0,1:T(8,128)(2,1)S(1)} %get-tuple-element.1305), channel_id=1, source_target_pairs={{0,1},{1,2},{2,3},{3,4},{4,5},{5,6},{6,7},{7,8},{8,9},{9,10},{10,1... | collective-permute-start | bytes 393224 | tf_op jit(solution)/shard_map/while/body/eval_jaxpr/ppermute | solution.py:15
  312.7 246.1 %while.66 = (s32[]{:T(128)}, bf16[256,256]{0,1:T(8,128)(2,1)S(1)}, bf16[256,256]{0,1:T(8,128)(2,1)S(1)}, f32[256,256]{0,1:T(8,128)S(1)}, f32[256,256]{0,1:T(8,12...) while((s32[]{:T(128)}, bf16[256,256]{0,1:T(8,128)(2,1)S(1)}, ...), condition=%wide.region_18.19_spmd.clone, body=%wide.region_15.18_spmd.clone.sunk | while | flops 169740032 | bytes 10241365 | solution.py:147
  312.7 8.8 %collective-permute-start.3 = (bf16[256,256]{0,1:T(8,128)(2,1)S(1)}, bf16[256,256]{0,1:T(8,128)(2,1)S(1)}, u32[]{:S(2)}, u32[]{:S(2)}) collective-permute-start(bf16[256,256]{0,1:T(8,128)(2,1)S(1)} %get-tuple-element.1341), channel_id=1, source_target_pairs={{0,1},{1,2},{2,3},{3,4},{4,5},{5,6},{6,7},{7,8},{8,9},{9,10},{10,1... | collective-permute-start | bytes 393224 | tf_op jit(solution)/shard_map/while/body/eval_jaxpr/ppermute | solution.py:15
  324.4 9.8 %collective-permute-start.5 = (f32[256,256]{0,1:T(8,128)S(1)}, f32[256,256]{0,1:T(8,128)S(1)}, u32[]{:S(2)}, u32[]{:S(2)}) collective-permute-start(f32[256,256]{0,1:T(8,128)S(1)} %get-tuple-element.1343), channel_id=1, source_target_pairs={{511,0},{0,1},{1,2},{2,3},{3,4},{4,5},{5,6},{6,7},{7,8},{8,9},{9,1... | collective-permute-start | bytes 786440 | tf_op jit(solution)/shard_map/while/body/eval_jaxpr/ppermute | solution.py:21
  340.3 4.4 collective-permute-start.3
  346.7 7.3 %collective-permute-start.5 = (f32[256,256]{0,1:T(8,128)S(1)}, f32[256,256]{0,1:T(8,128)S(1)}, u32[]{:S(2)}, u32[]{:S(2)}) collective-permute-start(f32[256,256]{0,1:T(8,128)S(1)} %get-tuple-element.1343), channel_id=1, source_target_pairs={{511,0},{0,1},{1,2},{2,3},{3,4},{4,5},{5,6},{6,7},{7,8},{8,9},{9,1... | collective-permute-start | bytes 786440 | tf_op jit(solution)/shard_map/while/body/eval_jaxpr/ppermute | solution.py:21
  360.2 4.4 collective-permute-start.3
  366.5 7.3 %collective-permute-start.5 = (f32[256,256]{0,1:T(8,128)S(1)}, f32[256,256]{0,1:T(8,128)S(1)}, u32[]{:S(2)}, u32[]{:S(2)}) collective-permute-start(f32[256,256]{0,1:T(8,128)S(1)} %get-tuple-element.1343), channel_id=1, source_target_pairs={{511,0},{0,1},{1,2},{2,3},{3,4},{4,5},{5,6},{6,7},{7,8},{8,9},{9,1... | collective-permute-start | bytes 786440 | tf_op jit(solution)/shard_map/while/body/eval_jaxpr/ppermute | solution.py:21
  380.1 4.4 collective-permute-start.3
  386.4 7.3 %collective-permute-start.5 = (f32[256,256]{0,1:T(8,128)S(1)}, f32[256,256]{0,1:T(8,128)S(1)}, u32[]{:S(2)}, u32[]{:S(2)}) collective-permute-start(f32[256,256]{0,1:T(8,128)S(1)} %get-tuple-element.1343), channel_id=1, source_target_pairs={{511,0},{0,1},{1,2},{2,3},{3,4},{4,5},{5,6},{6,7},{7,8},{8,9},{9,1... | collective-permute-start | bytes 786440 | tf_op jit(solution)/shard_map/while/body/eval_jaxpr/ppermute | solution.py:21
  399.9 4.4 collective-permute-start.3
  406.3 7.3 %collective-permute-start.5 = (f32[256,256]{0,1:T(8,128)S(1)}, f32[256,256]{0,1:T(8,128)S(1)}, u32[]{:S(2)}, u32[]{:S(2)}) collective-permute-start(f32[256,256]{0,1:T(8,128)S(1)} %get-tuple-element.1343), channel_id=1, source_target_pairs={{511,0},{0,1},{1,2},{2,3},{3,4},{4,5},{5,6},{6,7},{7,8},{8,9},{9,1... | collective-permute-start | bytes 786440 | tf_op jit(solution)/shard_map/while/body/eval_jaxpr/ppermute | solution.py:21
  419.8 4.4 collective-permute-start.3
  426.1 7.3 %collective-permute-start.5 = (f32[256,256]{0,1:T(8,128)S(1)}, f32[256,256]{0,1:T(8,128)S(1)}, u32[]{:S(2)}, u32[]{:S(2)}) collective-permute-start(f32[256,256]{0,1:T(8,128)S(1)} %get-tuple-element.1343), channel_id=1, source_target_pairs={{511,0},{0,1},{1,2},{2,3},{3,4},{4,5},{5,6},{6,7},{7,8},{8,9},{9,1... | collective-permute-start | bytes 786440 | tf_op jit(solution)/shard_map/while/body/eval_jaxpr/ppermute | solution.py:21
  439.6 4.4 collective-permute-start.3
  446.0 7.3 %collective-permute-start.5 = (f32[256,256]{0,1:T(8,128)S(1)}, f32[256,256]{0,1:T(8,128)S(1)}, u32[]{:S(2)}, u32[]{:S(2)}) collective-permute-start(f32[256,256]{0,1:T(8,128)S(1)} %get-tuple-element.1343), channel_id=1, source_target_pairs={{511,0},{0,1},{1,2},{2,3},{3,4},{4,5},{5,6},{6,7},{7,8},{8,9},{9,1... | collective-permute-start | bytes 786440 | tf_op jit(solution)/shard_map/while/body/eval_jaxpr/ppermute | solution.py:21
  459.5 4.4 collective-permute-start.3
  465.8 7.3 %collective-permute-start.5 = (f32[256,256]{0,1:T(8,128)S(1)}, f32[256,256]{0,1:T(8,128)S(1)}, u32[]{:S(2)}, u32[]{:S(2)}) collective-permute-start(f32[256,256]{0,1:T(8,128)S(1)} %get-tuple-element.1343), channel_id=1, source_target_pairs={{511,0},{0,1},{1,2},{2,3},{3,4},{4,5},{5,6},{6,7},{7,8},{8,9},{9,1... | collective-permute-start | bytes 786440 | tf_op jit(solution)/shard_map/while/body/eval_jaxpr/ppermute | solution.py:21
  479.4 4.4 collective-permute-start.3
  485.7 7.3 %collective-permute-start.5 = (f32[256,256]{0,1:T(8,128)S(1)}, f32[256,256]{0,1:T(8,128)S(1)}, u32[]{:S(2)}, u32[]{:S(2)}) collective-permute-start(f32[256,256]{0,1:T(8,128)S(1)} %get-tuple-element.1343), channel_id=1, source_target_pairs={{511,0},{0,1},{1,2},{2,3},{3,4},{4,5},{5,6},{6,7},{7,8},{8,9},{9,1... | collective-permute-start | bytes 786440 | tf_op jit(solution)/shard_map/while/body/eval_jaxpr/ppermute | solution.py:21
  499.2 4.4 collective-permute-start.3
  505.5 7.3 %collective-permute-start.5 = (f32[256,256]{0,1:T(8,128)S(1)}, f32[256,256]{0,1:T(8,128)S(1)}, u32[]{:S(2)}, u32[]{:S(2)}) collective-permute-start(f32[256,256]{0,1:T(8,128)S(1)} %get-tuple-element.1343), channel_id=1, source_target_pairs={{511,0},{0,1},{1,2},{2,3},{3,4},{4,5},{5,6},{6,7},{7,8},{8,9},{9,1... | collective-permute-start | bytes 786440 | tf_op jit(solution)/shard_map/while/body/eval_jaxpr/ppermute | solution.py:21
  525.4 7.3 %collective-permute-start.5 = (f32[256,256]{0,1:T(8,128)S(1)}, f32[256,256]{0,1:T(8,128)S(1)}, u32[]{:S(2)}, u32[]{:S(2)}) collective-permute-start(f32[256,256]{0,1:T(8,128)S(1)} %get-tuple-element.1343), channel_id=1, source_target_pairs={{511,0},{0,1},{1,2},{2,3},{3,4},{4,5},{5,6},{6,7},{7,8},{8,9},{9,1... | collective-permute-start | bytes 786440 | tf_op jit(solution)/shard_map/while/body/eval_jaxpr/ppermute | solution.py:21
  545.3 7.3 %collective-permute-start.5 = (f32[256,256]{0,1:T(8,128)S(1)}, f32[256,256]{0,1:T(8,128)S(1)}, u32[]{:S(2)}, u32[]{:S(2)}) collective-permute-start(f32[256,256]{0,1:T(8,128)S(1)} %get-tuple-element.1343), channel_id=1, source_target_pairs={{511,0},{0,1},{1,2},{2,3},{3,4},{4,5},{5,6},{6,7},{7,8},{8,9},{9,1... | collective-permute-start | bytes 786440 | tf_op jit(solution)/shard_map/while/body/eval_jaxpr/ppermute | solution.py:21
  563.6 12.9 %collective-permute-done.7 = bf16[256,256]{1,0:T(8,128)(2,1)S(1)} collective-permute-done((bf16[256,256]{1,0:T(8,128)(2,1)S(1)}, bf16[256,256]{1,0:T(8,128)(2,1)S(1)}, u32[]{:S(2)}, u32[]{:S(2)}) %collective-permute-start.7) | collective-permute-done | bytes 131104 | tf_op jit(solution)/shard_map/ppermute | solution.py:21
  (631 shorter events, 220.5 us)
Async XLA Ops:
  32.8 11.7 %collective-permute-start = (bf16[256,256]{0,1:T(8,128)(2,1)S(1)}, bf16[256,256]{0,1:T(8,128)(2,1)S(1)}, u32[]{:S(2)}, u32[]{:S(2)}) collective-permute-start(bf16[256,256]{0,1:T(8,128)(2,1)S(1)} %get-tuple-element.1273), channel_id=1, source_target_pairs={{0,1},{1,2},{2,3},{3,4},{4,5},{5,6},{6,7},{7,8},{8,9},{9,10},{10,1... | collective-permute-start | bytes 393224 | tf_op jit(solution)/shard_map/while/body/eval_jaxpr/ppermute | solution.py:15
  45.0 11.7 %collective-permute-start = (bf16[256,256]{0,1:T(8,128)(2,1)S(1)}, bf16[256,256]{0,1:T(8,128)(2,1)S(1)}, u32[]{:S(2)}, u32[]{:S(2)}) collective-permute-start(bf16[256,256]{0,1:T(8,128)(2,1)S(1)} %get-tuple-element.1273), channel_id=1, source_target_pairs={{0,1},{1,2},{2,3},{3,4},{4,5},{5,6},{6,7},{7,8},{8,9},{9,10},{10,1... | collective-permute-start | bytes 393224 | tf_op jit(solution)/shard_map/while/body/eval_jaxpr/ppermute | solution.py:15
  57.2 11.7 %collective-permute-start = (bf16[256,256]{0,1:T(8,128)(2,1)S(1)}, bf16[256,256]{0,1:T(8,128)(2,1)S(1)}, u32[]{:S(2)}, u32[]{:S(2)}) collective-permute-start(bf16[256,256]{0,1:T(8,128)(2,1)S(1)} %get-tuple-element.1273), channel_id=1, source_target_pairs={{0,1},{1,2},{2,3},{3,4},{4,5},{5,6},{6,7},{7,8},{8,9},{9,10},{10,1... | collective-permute-start | bytes 393224 | tf_op jit(solution)/shard_map/while/body/eval_jaxpr/ppermute | solution.py:15
  69.4 11.7 %collective-permute-start = (bf16[256,256]{0,1:T(8,128)(2,1)S(1)}, bf16[256,256]{0,1:T(8,128)(2,1)S(1)}, u32[]{:S(2)}, u32[]{:S(2)}) collective-permute-start(bf16[256,256]{0,1:T(8,128)(2,1)S(1)} %get-tuple-element.1273), channel_id=1, source_target_pairs={{0,1},{1,2},{2,3},{3,4},{4,5},{5,6},{6,7},{7,8},{8,9},{9,10},{10,1... | collective-permute-start | bytes 393224 | tf_op jit(solution)/shard_map/while/body/eval_jaxpr/ppermute | solution.py:15
  81.6 11.7 %collective-permute-start = (bf16[256,256]{0,1:T(8,128)(2,1)S(1)}, bf16[256,256]{0,1:T(8,128)(2,1)S(1)}, u32[]{:S(2)}, u32[]{:S(2)}) collective-permute-start(bf16[256,256]{0,1:T(8,128)(2,1)S(1)} %get-tuple-element.1273), channel_id=1, source_target_pairs={{0,1},{1,2},{2,3},{3,4},{4,5},{5,6},{6,7},{7,8},{8,9},{9,10},{10,1... | collective-permute-start | bytes 393224 | tf_op jit(solution)/shard_map/while/body/eval_jaxpr/ppermute | solution.py:15
  93.8 11.7 %collective-permute-start = (bf16[256,256]{0,1:T(8,128)(2,1)S(1)}, bf16[256,256]{0,1:T(8,128)(2,1)S(1)}, u32[]{:S(2)}, u32[]{:S(2)}) collective-permute-start(bf16[256,256]{0,1:T(8,128)(2,1)S(1)} %get-tuple-element.1273), channel_id=1, source_target_pairs={{0,1},{1,2},{2,3},{3,4},{4,5},{5,6},{6,7},{7,8},{8,9},{9,10},{10,1... | collective-permute-start | bytes 393224 | tf_op jit(solution)/shard_map/while/body/eval_jaxpr/ppermute | solution.py:15
  106.0 11.7 %collective-permute-start = (bf16[256,256]{0,1:T(8,128)(2,1)S(1)}, bf16[256,256]{0,1:T(8,128)(2,1)S(1)}, u32[]{:S(2)}, u32[]{:S(2)}) collective-permute-start(bf16[256,256]{0,1:T(8,128)(2,1)S(1)} %get-tuple-element.1273), channel_id=1, source_target_pairs={{0,1},{1,2},{2,3},{3,4},{4,5},{5,6},{6,7},{7,8},{8,9},{9,10},{10,1... | collective-permute-start | bytes 393224 | tf_op jit(solution)/shard_map/while/body/eval_jaxpr/ppermute | solution.py:15
  118.2 11.7 %collective-permute-start = (bf16[256,256]{0,1:T(8,128)(2,1)S(1)}, bf16[256,256]{0,1:T(8,128)(2,1)S(1)}, u32[]{:S(2)}, u32[]{:S(2)}) collective-permute-start(bf16[256,256]{0,1:T(8,128)(2,1)S(1)} %get-tuple-element.1273), channel_id=1, source_target_pairs={{0,1},{1,2},{2,3},{3,4},{4,5},{5,6},{6,7},{7,8},{8,9},{9,10},{10,1... | collective-permute-start | bytes 393224 | tf_op jit(solution)/shard_map/while/body/eval_jaxpr/ppermute | solution.py:15
  132.6 21.0 %collective-permute-start.2 = (bf16[256,256]{0,1:T(8,128)(2,1)S(1)}, bf16[256,256]{0,1:T(8,128)(2,1)S(1)}, u32[]{:S(2)}, u32[]{:S(2)}) collective-permute-start(bf16[256,256]{0,1:T(8,128)(2,1)S(1)} %get-tuple-element.1305), channel_id=1, source_target_pairs={{0,1},{1,2},{2,3},{3,4},{4,5},{5,6},{6,7},{7,8},{8,9},{9,10},{10,1... | collective-permute-start | bytes 393224 | tf_op jit(solution)/shard_map/while/body/eval_jaxpr/ppermute | solution.py:15
  142.4 12.7 %collective-permute-start.1 = (bf16[256,256]{0,1:T(8,128)(2,1)S(1)}, bf16[256,256]{0,1:T(8,128)(2,1)S(1)}, u32[]{:S(2)}, u32[]{:S(2)}) collective-permute-start(bf16[256,256]{0,1:T(8,128)(2,1)S(1)} %get-tuple-element.1304), channel_id=1, source_target_pairs={{0,1},{1,2},{2,3},{3,4},{4,5},{5,6},{6,7},{7,8},{8,9},{9,10},{10,1... | collective-permute-start | bytes 393224 | tf_op jit(solution)/shard_map/while/body/eval_jaxpr/ppermute | solution.py:15
  155.5 12.2 %collective-permute-start.2 = (bf16[256,256]{0,1:T(8,128)(2,1)S(1)}, bf16[256,256]{0,1:T(8,128)(2,1)S(1)}, u32[]{:S(2)}, u32[]{:S(2)}) collective-permute-start(bf16[256,256]{0,1:T(8,128)(2,1)S(1)} %get-tuple-element.1305), channel_id=1, source_target_pairs={{0,1},{1,2},{2,3},{3,4},{4,5},{5,6},{6,7},{7,8},{8,9},{9,10},{10,1... | collective-permute-start | bytes 393224 | tf_op jit(solution)/shard_map/while/body/eval_jaxpr/ppermute | solution.py:15
  169.6 12.2 %collective-permute-start.2 = (bf16[256,256]{0,1:T(8,128)(2,1)S(1)}, bf16[256,256]{0,1:T(8,128)(2,1)S(1)}, u32[]{:S(2)}, u32[]{:S(2)}) collective-permute-start(bf16[256,256]{0,1:T(8,128)(2,1)S(1)} %get-tuple-element.1305), channel_id=1, source_target_pairs={{0,1},{1,2},{2,3},{3,4},{4,5},{5,6},{6,7},{7,8},{8,9},{9,10},{10,1... | collective-permute-start | bytes 393224 | tf_op jit(solution)/shard_map/while/body/eval_jaxpr/ppermute | solution.py:15
  183.7 12.2 %collective-permute-start.2 = (bf16[256,256]{0,1:T(8,128)(2,1)S(1)}, bf16[256,256]{0,1:T(8,128)(2,1)S(1)}, u32[]{:S(2)}, u32[]{:S(2)}) collective-permute-start(bf16[256,256]{0,1:T(8,128)(2,1)S(1)} %get-tuple-element.1305), channel_id=1, source_target_pairs={{0,1},{1,2},{2,3},{3,4},{4,5},{5,6},{6,7},{7,8},{8,9},{9,10},{10,1... | collective-permute-start | bytes 393224 | tf_op jit(solution)/shard_map/while/body/eval_jaxpr/ppermute | solution.py:15
  197.7 12.2 %collective-permute-start.2 = (bf16[256,256]{0,1:T(8,128)(2,1)S(1)}, bf16[256,256]{0,1:T(8,128)(2,1)S(1)}, u32[]{:S(2)}, u32[]{:S(2)}) collective-permute-start(bf16[256,256]{0,1:T(8,128)(2,1)S(1)} %get-tuple-element.1305), channel_id=1, source_target_pairs={{0,1},{1,2},{2,3},{3,4},{4,5},{5,6},{6,7},{7,8},{8,9},{9,10},{10,1... | collective-permute-start | bytes 393224 | tf_op jit(solution)/shard_map/while/body/eval_jaxpr/ppermute | solution.py:15
  211.8 12.2 %collective-permute-start.2 = (bf16[256,256]{0,1:T(8,128)(2,1)S(1)}, bf16[256,256]{0,1:T(8,128)(2,1)S(1)}, u32[]{:S(2)}, u32[]{:S(2)}) collective-permute-start(bf16[256,256]{0,1:T(8,128)(2,1)S(1)} %get-tuple-element.1305), channel_id=1, source_target_pairs={{0,1},{1,2},{2,3},{3,4},{4,5},{5,6},{6,7},{7,8},{8,9},{9,10},{10,1... | collective-permute-start | bytes 393224 | tf_op jit(solution)/shard_map/while/body/eval_jaxpr/ppermute | solution.py:15
  225.9 12.2 %collective-permute-start.2 = (bf16[256,256]{0,1:T(8,128)(2,1)S(1)}, bf16[256,256]{0,1:T(8,128)(2,1)S(1)}, u32[]{:S(2)}, u32[]{:S(2)}) collective-permute-start(bf16[256,256]{0,1:T(8,128)(2,1)S(1)} %get-tuple-element.1305), channel_id=1, source_target_pairs={{0,1},{1,2},{2,3},{3,4},{4,5},{5,6},{6,7},{7,8},{8,9},{9,10},{10,1... | collective-permute-start | bytes 393224 | tf_op jit(solution)/shard_map/while/body/eval_jaxpr/ppermute | solution.py:15
  240.0 12.2 %collective-permute-start.2 = (bf16[256,256]{0,1:T(8,128)(2,1)S(1)}, bf16[256,256]{0,1:T(8,128)(2,1)S(1)}, u32[]{:S(2)}, u32[]{:S(2)}) collective-permute-start(bf16[256,256]{0,1:T(8,128)(2,1)S(1)} %get-tuple-element.1305), channel_id=1, source_target_pairs={{0,1},{1,2},{2,3},{3,4},{4,5},{5,6},{6,7},{7,8},{8,9},{9,10},{10,1... | collective-permute-start | bytes 393224 | tf_op jit(solution)/shard_map/while/body/eval_jaxpr/ppermute | solution.py:15
  254.1 12.2 %collective-permute-start.2 = (bf16[256,256]{0,1:T(8,128)(2,1)S(1)}, bf16[256,256]{0,1:T(8,128)(2,1)S(1)}, u32[]{:S(2)}, u32[]{:S(2)}) collective-permute-start(bf16[256,256]{0,1:T(8,128)(2,1)S(1)} %get-tuple-element.1305), channel_id=1, source_target_pairs={{0,1},{1,2},{2,3},{3,4},{4,5},{5,6},{6,7},{7,8},{8,9},{9,10},{10,1... | collective-permute-start | bytes 393224 | tf_op jit(solution)/shard_map/while/body/eval_jaxpr/ppermute | solution.py:15
  268.1 12.2 %collective-permute-start.2 = (bf16[256,256]{0,1:T(8,128)(2,1)S(1)}, bf16[256,256]{0,1:T(8,128)(2,1)S(1)}, u32[]{:S(2)}, u32[]{:S(2)}) collective-permute-start(bf16[256,256]{0,1:T(8,128)(2,1)S(1)} %get-tuple-element.1305), channel_id=1, source_target_pairs={{0,1},{1,2},{2,3},{3,4},{4,5},{5,6},{6,7},{7,8},{8,9},{9,10},{10,1... | collective-permute-start | bytes 393224 | tf_op jit(solution)/shard_map/while/body/eval_jaxpr/ppermute | solution.py:15
  282.2 12.2 %collective-permute-start.2 = (bf16[256,256]{0,1:T(8,128)(2,1)S(1)}, bf16[256,256]{0,1:T(8,128)(2,1)S(1)}, u32[]{:S(2)}, u32[]{:S(2)}) collective-permute-start(bf16[256,256]{0,1:T(8,128)(2,1)S(1)} %get-tuple-element.1305), channel_id=1, source_target_pairs={{0,1},{1,2},{2,3},{3,4},{4,5},{5,6},{6,7},{7,8},{8,9},{9,10},{10,1... | collective-permute-start | bytes 393224 | tf_op jit(solution)/shard_map/while/body/eval_jaxpr/ppermute | solution.py:15
  296.3 12.2 %collective-permute-start.2 = (bf16[256,256]{0,1:T(8,128)(2,1)S(1)}, bf16[256,256]{0,1:T(8,128)(2,1)S(1)}, u32[]{:S(2)}, u32[]{:S(2)}) collective-permute-start(bf16[256,256]{0,1:T(8,128)(2,1)S(1)} %get-tuple-element.1305), channel_id=1, source_target_pairs={{0,1},{1,2},{2,3},{3,4},{4,5},{5,6},{6,7},{7,8},{8,9},{9,10},{10,1... | collective-permute-start | bytes 393224 | tf_op jit(solution)/shard_map/while/body/eval_jaxpr/ppermute | solution.py:15
  312.7 23.9 %collective-permute-start.3 = (bf16[256,256]{0,1:T(8,128)(2,1)S(1)}, bf16[256,256]{0,1:T(8,128)(2,1)S(1)}, u32[]{:S(2)}, u32[]{:S(2)}) collective-permute-start(bf16[256,256]{0,1:T(8,128)(2,1)S(1)} %get-tuple-element.1341), channel_id=1, source_target_pairs={{0,1},{1,2},{2,3},{3,4},{4,5},{5,6},{6,7},{7,8},{8,9},{9,10},{10,1... | collective-permute-start | bytes 393224 | tf_op jit(solution)/shard_map/while/body/eval_jaxpr/ppermute | solution.py:15
  321.5 15.6 %collective-permute-start.4 = (bf16[256,256]{0,1:T(8,128)(2,1)S(1)}, bf16[256,256]{0,1:T(8,128)(2,1)S(1)}, u32[]{:S(2)}, u32[]{:S(2)}) collective-permute-start(bf16[256,256]{0,1:T(8,128)(2,1)S(1)} %get-tuple-element.1342), channel_id=1, source_target_pairs={{0,1},{1,2},{2,3},{3,4},{4,5},{5,6},{6,7},{7,8},{8,9},{9,10},{10,1... | collective-permute-start | bytes 393224 | tf_op jit(solution)/shard_map/while/body/eval_jaxpr/ppermute | solution.py:15
  324.4 13.6 %collective-permute-start.5 = (f32[256,256]{0,1:T(8,128)S(1)}, f32[256,256]{0,1:T(8,128)S(1)}, u32[]{:S(2)}, u32[]{:S(2)}) collective-permute-start(f32[256,256]{0,1:T(8,128)S(1)} %get-tuple-element.1343), channel_id=1, source_target_pairs={{511,0},{0,1},{1,2},{2,3},{3,4},{4,5},{5,6},{6,7},{7,8},{8,9},{9,1... | collective-permute-start | bytes 786440 | tf_op jit(solution)/shard_map/while/body/eval_jaxpr/ppermute | solution.py:21
  340.3 16.1 %collective-permute-start.3 = (bf16[256,256]{0,1:T(8,128)(2,1)S(1)}, bf16[256,256]{0,1:T(8,128)(2,1)S(1)}, u32[]{:S(2)}, u32[]{:S(2)}) collective-permute-start(bf16[256,256]{0,1:T(8,128)(2,1)S(1)} %get-tuple-element.1341), channel_id=1, source_target_pairs={{0,1},{1,2},{2,3},{3,4},{4,5},{5,6},{6,7},{7,8},{8,9},{9,10},{10,1... | collective-permute-start | bytes 393224 | tf_op jit(solution)/shard_map/while/body/eval_jaxpr/ppermute | solution.py:15
  344.7 12.2 %collective-permute-start.4 = (bf16[256,256]{0,1:T(8,128)(2,1)S(1)}, bf16[256,256]{0,1:T(8,128)(2,1)S(1)}, u32[]{:S(2)}, u32[]{:S(2)}) collective-permute-start(bf16[256,256]{0,1:T(8,128)(2,1)S(1)} %get-tuple-element.1342), channel_id=1, source_target_pairs={{0,1},{1,2},{2,3},{3,4},{4,5},{5,6},{6,7},{7,8},{8,9},{9,10},{10,1... | collective-permute-start | bytes 393224 | tf_op jit(solution)/shard_map/while/body/eval_jaxpr/ppermute | solution.py:15
  360.2 16.1 %collective-permute-start.3 = (bf16[256,256]{0,1:T(8,128)(2,1)S(1)}, bf16[256,256]{0,1:T(8,128)(2,1)S(1)}, u32[]{:S(2)}, u32[]{:S(2)}) collective-permute-start(bf16[256,256]{0,1:T(8,128)(2,1)S(1)} %get-tuple-element.1341), channel_id=1, source_target_pairs={{0,1},{1,2},{2,3},{3,4},{4,5},{5,6},{6,7},{7,8},{8,9},{9,10},{10,1... | collective-permute-start | bytes 393224 | tf_op jit(solution)/shard_map/while/body/eval_jaxpr/ppermute | solution.py:15
  364.6 12.2 %collective-permute-start.4 = (bf16[256,256]{0,1:T(8,128)(2,1)S(1)}, bf16[256,256]{0,1:T(8,128)(2,1)S(1)}, u32[]{:S(2)}, u32[]{:S(2)}) collective-permute-start(bf16[256,256]{0,1:T(8,128)(2,1)S(1)} %get-tuple-element.1342), channel_id=1, source_target_pairs={{0,1},{1,2},{2,3},{3,4},{4,5},{5,6},{6,7},{7,8},{8,9},{9,10},{10,1... | collective-permute-start | bytes 393224 | tf_op jit(solution)/shard_map/while/body/eval_jaxpr/ppermute | solution.py:15
  380.1 16.1 %collective-permute-start.3 = (bf16[256,256]{0,1:T(8,128)(2,1)S(1)}, bf16[256,256]{0,1:T(8,128)(2,1)S(1)}, u32[]{:S(2)}, u32[]{:S(2)}) collective-permute-start(bf16[256,256]{0,1:T(8,128)(2,1)S(1)} %get-tuple-element.1341), channel_id=1, source_target_pairs={{0,1},{1,2},{2,3},{3,4},{4,5},{5,6},{6,7},{7,8},{8,9},{9,10},{10,1... | collective-permute-start | bytes 393224 | tf_op jit(solution)/shard_map/while/body/eval_jaxpr/ppermute | solution.py:15
  384.5 12.2 %collective-permute-start.4 = (bf16[256,256]{0,1:T(8,128)(2,1)S(1)}, bf16[256,256]{0,1:T(8,128)(2,1)S(1)}, u32[]{:S(2)}, u32[]{:S(2)}) collective-permute-start(bf16[256,256]{0,1:T(8,128)(2,1)S(1)} %get-tuple-element.1342), channel_id=1, source_target_pairs={{0,1},{1,2},{2,3},{3,4},{4,5},{5,6},{6,7},{7,8},{8,9},{9,10},{10,1... | collective-permute-start | bytes 393224 | tf_op jit(solution)/shard_map/while/body/eval_jaxpr/ppermute | solution.py:15
  399.9 16.1 %collective-permute-start.3 = (bf16[256,256]{0,1:T(8,128)(2,1)S(1)}, bf16[256,256]{0,1:T(8,128)(2,1)S(1)}, u32[]{:S(2)}, u32[]{:S(2)}) collective-permute-start(bf16[256,256]{0,1:T(8,128)(2,1)S(1)} %get-tuple-element.1341), channel_id=1, source_target_pairs={{0,1},{1,2},{2,3},{3,4},{4,5},{5,6},{6,7},{7,8},{8,9},{9,10},{10,1... | collective-permute-start | bytes 393224 | tf_op jit(solution)/shard_map/while/body/eval_jaxpr/ppermute | solution.py:15
  404.3 12.2 %collective-permute-start.4 = (bf16[256,256]{0,1:T(8,128)(2,1)S(1)}, bf16[256,256]{0,1:T(8,128)(2,1)S(1)}, u32[]{:S(2)}, u32[]{:S(2)}) collective-permute-start(bf16[256,256]{0,1:T(8,128)(2,1)S(1)} %get-tuple-element.1342), channel_id=1, source_target_pairs={{0,1},{1,2},{2,3},{3,4},{4,5},{5,6},{6,7},{7,8},{8,9},{9,10},{10,1... | collective-permute-start | bytes 393224 | tf_op jit(solution)/shard_map/while/body/eval_jaxpr/ppermute | solution.py:15
  419.8 16.1 %collective-permute-start.3 = (bf16[256,256]{0,1:T(8,128)(2,1)S(1)}, bf16[256,256]{0,1:T(8,128)(2,1)S(1)}, u32[]{:S(2)}, u32[]{:S(2)}) collective-permute-start(bf16[256,256]{0,1:T(8,128)(2,1)S(1)} %get-tuple-element.1341), channel_id=1, source_target_pairs={{0,1},{1,2},{2,3},{3,4},{4,5},{5,6},{6,7},{7,8},{8,9},{9,10},{10,1... | collective-permute-start | bytes 393224 | tf_op jit(solution)/shard_map/while/body/eval_jaxpr/ppermute | solution.py:15
  424.2 12.2 %collective-permute-start.4 = (bf16[256,256]{0,1:T(8,128)(2,1)S(1)}, bf16[256,256]{0,1:T(8,128)(2,1)S(1)}, u32[]{:S(2)}, u32[]{:S(2)}) collective-permute-start(bf16[256,256]{0,1:T(8,128)(2,1)S(1)} %get-tuple-element.1342), channel_id=1, source_target_pairs={{0,1},{1,2},{2,3},{3,4},{4,5},{5,6},{6,7},{7,8},{8,9},{9,10},{10,1... | collective-permute-start | bytes 393224 | tf_op jit(solution)/shard_map/while/body/eval_jaxpr/ppermute | solution.py:15
  439.6 16.1 %collective-permute-start.3 = (bf16[256,256]{0,1:T(8,128)(2,1)S(1)}, bf16[256,256]{0,1:T(8,128)(2,1)S(1)}, u32[]{:S(2)}, u32[]{:S(2)}) collective-permute-start(bf16[256,256]{0,1:T(8,128)(2,1)S(1)} %get-tuple-element.1341), channel_id=1, source_target_pairs={{0,1},{1,2},{2,3},{3,4},{4,5},{5,6},{6,7},{7,8},{8,9},{9,10},{10,1... | collective-permute-start | bytes 393224 | tf_op jit(solution)/shard_map/while/body/eval_jaxpr/ppermute | solution.py:15
  444.0 12.2 %collective-permute-start.4 = (bf16[256,256]{0,1:T(8,128)(2,1)S(1)}, bf16[256,256]{0,1:T(8,128)(2,1)S(1)}, u32[]{:S(2)}, u32[]{:S(2)}) collective-permute-start(bf16[256,256]{0,1:T(8,128)(2,1)S(1)} %get-tuple-element.1342), channel_id=1, source_target_pairs={{0,1},{1,2},{2,3},{3,4},{4,5},{5,6},{6,7},{7,8},{8,9},{9,10},{10,1... | collective-permute-start | bytes 393224 | tf_op jit(solution)/shard_map/while/body/eval_jaxpr/ppermute | solution.py:15
  459.5 16.1 %collective-permute-start.3 = (bf16[256,256]{0,1:T(8,128)(2,1)S(1)}, bf16[256,256]{0,1:T(8,128)(2,1)S(1)}, u32[]{:S(2)}, u32[]{:S(2)}) collective-permute-start(bf16[256,256]{0,1:T(8,128)(2,1)S(1)} %get-tuple-element.1341), channel_id=1, source_target_pairs={{0,1},{1,2},{2,3},{3,4},{4,5},{5,6},{6,7},{7,8},{8,9},{9,10},{10,1... | collective-permute-start | bytes 393224 | tf_op jit(solution)/shard_map/while/body/eval_jaxpr/ppermute | solution.py:15
  463.9 12.2 %collective-permute-start.4 = (bf16[256,256]{0,1:T(8,128)(2,1)S(1)}, bf16[256,256]{0,1:T(8,128)(2,1)S(1)}, u32[]{:S(2)}, u32[]{:S(2)}) collective-permute-start(bf16[256,256]{0,1:T(8,128)(2,1)S(1)} %get-tuple-element.1342), channel_id=1, source_target_pairs={{0,1},{1,2},{2,3},{3,4},{4,5},{5,6},{6,7},{7,8},{8,9},{9,10},{10,1... | collective-permute-start | bytes 393224 | tf_op jit(solution)/shard_map/while/body/eval_jaxpr/ppermute | solution.py:15
  479.4 16.1 %collective-permute-start.3 = (bf16[256,256]{0,1:T(8,128)(2,1)S(1)}, bf16[256,256]{0,1:T(8,128)(2,1)S(1)}, u32[]{:S(2)}, u32[]{:S(2)}) collective-permute-start(bf16[256,256]{0,1:T(8,128)(2,1)S(1)} %get-tuple-element.1341), channel_id=1, source_target_pairs={{0,1},{1,2},{2,3},{3,4},{4,5},{5,6},{6,7},{7,8},{8,9},{9,10},{10,1... | collective-permute-start | bytes 393224 | tf_op jit(solution)/shard_map/while/body/eval_jaxpr/ppermute | solution.py:15
  483.8 12.2 %collective-permute-start.4 = (bf16[256,256]{0,1:T(8,128)(2,1)S(1)}, bf16[256,256]{0,1:T(8,128)(2,1)S(1)}, u32[]{:S(2)}, u32[]{:S(2)}) collective-permute-start(bf16[256,256]{0,1:T(8,128)(2,1)S(1)} %get-tuple-element.1342), channel_id=1, source_target_pairs={{0,1},{1,2},{2,3},{3,4},{4,5},{5,6},{6,7},{7,8},{8,9},{9,10},{10,1... | collective-permute-start | bytes 393224 | tf_op jit(solution)/shard_map/while/body/eval_jaxpr/ppermute | solution.py:15
  499.2 16.1 %collective-permute-start.3 = (bf16[256,256]{0,1:T(8,128)(2,1)S(1)}, bf16[256,256]{0,1:T(8,128)(2,1)S(1)}, u32[]{:S(2)}, u32[]{:S(2)}) collective-permute-start(bf16[256,256]{0,1:T(8,128)(2,1)S(1)} %get-tuple-element.1341), channel_id=1, source_target_pairs={{0,1},{1,2},{2,3},{3,4},{4,5},{5,6},{6,7},{7,8},{8,9},{9,10},{10,1... | collective-permute-start | bytes 393224 | tf_op jit(solution)/shard_map/while/body/eval_jaxpr/ppermute | solution.py:15
  503.6 12.2 %collective-permute-start.4 = (bf16[256,256]{0,1:T(8,128)(2,1)S(1)}, bf16[256,256]{0,1:T(8,128)(2,1)S(1)}, u32[]{:S(2)}, u32[]{:S(2)}) collective-permute-start(bf16[256,256]{0,1:T(8,128)(2,1)S(1)} %get-tuple-element.1342), channel_id=1, source_target_pairs={{0,1},{1,2},{2,3},{3,4},{4,5},{5,6},{6,7},{7,8},{8,9},{9,10},{10,1... | collective-permute-start | bytes 393224 | tf_op jit(solution)/shard_map/while/body/eval_jaxpr/ppermute | solution.py:15
  519.1 16.1 %collective-permute-start.3 = (bf16[256,256]{0,1:T(8,128)(2,1)S(1)}, bf16[256,256]{0,1:T(8,128)(2,1)S(1)}, u32[]{:S(2)}, u32[]{:S(2)}) collective-permute-start(bf16[256,256]{0,1:T(8,128)(2,1)S(1)} %get-tuple-element.1341), channel_id=1, source_target_pairs={{0,1},{1,2},{2,3},{3,4},{4,5},{5,6},{6,7},{7,8},{8,9},{9,10},{10,1... | collective-permute-start | bytes 393224 | tf_op jit(solution)/shard_map/while/body/eval_jaxpr/ppermute | solution.py:15
  523.5 12.2 %collective-permute-start.4 = (bf16[256,256]{0,1:T(8,128)(2,1)S(1)}, bf16[256,256]{0,1:T(8,128)(2,1)S(1)}, u32[]{:S(2)}, u32[]{:S(2)}) collective-permute-start(bf16[256,256]{0,1:T(8,128)(2,1)S(1)} %get-tuple-element.1342), channel_id=1, source_target_pairs={{0,1},{1,2},{2,3},{3,4},{4,5},{5,6},{6,7},{7,8},{8,9},{9,10},{10,1... | collective-permute-start | bytes 393224 | tf_op jit(solution)/shard_map/while/body/eval_jaxpr/ppermute | solution.py:15
  538.9 16.1 %collective-permute-start.3 = (bf16[256,256]{0,1:T(8,128)(2,1)S(1)}, bf16[256,256]{0,1:T(8,128)(2,1)S(1)}, u32[]{:S(2)}, u32[]{:S(2)}) collective-permute-start(bf16[256,256]{0,1:T(8,128)(2,1)S(1)} %get-tuple-element.1341), channel_id=1, source_target_pairs={{0,1},{1,2},{2,3},{3,4},{4,5},{5,6},{6,7},{7,8},{8,9},{9,10},{10,1... | collective-permute-start | bytes 393224 | tf_op jit(solution)/shard_map/while/body/eval_jaxpr/ppermute | solution.py:15
  543.3 12.2 %collective-permute-start.4 = (bf16[256,256]{0,1:T(8,128)(2,1)S(1)}, bf16[256,256]{0,1:T(8,128)(2,1)S(1)}, u32[]{:S(2)}, u32[]{:S(2)}) collective-permute-start(bf16[256,256]{0,1:T(8,128)(2,1)S(1)} %get-tuple-element.1342), channel_id=1, source_target_pairs={{0,1},{1,2},{2,3},{3,4},{4,5},{5,6},{6,7},{7,8},{8,9},{9,10},{10,1... | collective-permute-start | bytes 393224 | tf_op jit(solution)/shard_map/while/body/eval_jaxpr/ppermute | solution.py:15
  558.9 17.6 %collective-permute-start.7 = (bf16[256,256]{1,0:T(8,128)(2,1)S(1)}, bf16[256,256]{1,0:T(8,128)(2,1)S(1)}, u32[]{:S(2)}, u32[]{:S(2)}) collective-permute-start(bf16[256,256]{1,0:T(8,128)(2,1)S(1)} %copy.115), channel_id=1, source_target_pairs={{12,0},{13,1},{14,2},{15,3},{16,4},{17,5},{18,6},{19,7},{20,8},{21... | collective-permute-start | bytes 393224 | tf_op jit(solution)/shard_map/ppermute | solution.py:21
  560.9 17.5 %collective-permute-start.8 = (bf16[256,256]{1,0:T(8,128)(2,1)S(1)}, bf16[256,256]{1,0:T(8,128)(2,1)S(1)}, u32[]{:S(2)}, u32[]{:S(2)}) collective-permute-start(bf16[256,256]{1,0:T(8,128)(2,1)S(1)} %copy.116), channel_id=1, source_target_pairs={{12,0},{13,1},{14,2},{15,3},{16,4},{17,5},{18,6},{19,7},{20,8},{21... | collective-permute-start | bytes 393224 | tf_op jit(solution)/shard_map/ppermute | solution.py:21
  (45 other events, 406.5 us)
where the time goes:
time: 584 us; the launch traced here: 580 us
  starting transfers between devices  444 us (76%)
  waiting for transfers between devices  77.3 us (13%)
  matrix products  23.6 us (4%)
  other arithmetic  21 us (4%)
  local copies, waits for them, and re-layouts  8.62 us (1%)
    ppermute x60, starting transfers between devices, passed_along(): lax.ppermute(value, axis, [(source, source + steps) for source in range(f...  327 us
    ppermute x26, starting transfers between devices, shifted(): return lax.ppermute(block, axis, route)  118 us
    ppermute x26, waiting for transfers between devices, shifted(): return lax.ppermute(block, axis, route)  42 us
    ppermute x60, waiting for transfers between devices, passed_along(): lax.ppermute(value, axis, [(source, source + steps) for source in range(f...  35.3 us
  transfers between devices with their start and end apart: 86, of which 38 were waited for; matrix products, arithmetic and copies ran while one was open for 6% of the time, Pallas kernels for 0%

commit v1 on v0

v1 whole, which is shorter than its diff:
```python
import functools
import math

import jax
import jax.numpy as jnp
from jax import lax
from jax.experimental import pallas as pl
from jax.experimental.pallas import tpu as pltpu
from jax.sharding import PartitionSpec as P

HEADS = 2
HD = 128
CTX = 2
BLK = 256
NX, NY, NC = 4, 2, 2
ROW = NX * NY * NC
COL = NY * NC
NQ = NX * NC
NEG = -1e30
LOG2E = math.log2(math.e)

XC_GROUPS = [[x * 4 + y * 2 + c for x in range(NX) for c in range(NC)] for y in range(NY)]
COL_GROUPS = [[x * 4 + y * 2 + c for y in range(NY) for c in range(NC)] for x in range(NX)]
X_GROUPS = [[x * 4 + k for x in range(NX)] for k in range(COL)]


def exchange(value, groups):
    return lax.all_to_all(value, "inner", 0, 0, axis_index_groups=groups, tiled=True)


def row_step(value, steps):
    count = lax.axis_size("outer")
    first, last = max(0, -steps), min(count, count - steps)
    return lax.ppermute(value, "outer", [(i, i + steps) for i in range(first, last)])


def by_head(left, right):
    return jnp.stack(
        [
            jnp.concatenate([left[:, h * HD : (h + 1) * HD], right[:, h * HD : (h + 1) * HD]], axis=1)
            for h in range(HEADS)
        ]
    )


def key_ranges(group_lengths, row, y_lo):
    ends = jnp.cumsum(group_lengths).astype(jnp.int32)
    x = jnp.arange(NX, dtype=jnp.int32)[:, None, None]
    c = jnp.arange(NC, dtype=jnp.int32)[None, :, None]
    i = jnp.arange(BLK, dtype=jnp.int32)[None, None, :]
    first = (row * ROW + x * COL + y_lo * NC + c) * BLK
    pos = (first + i).reshape(NQ, BLK)
    last = (first + BLK + 0 * i).reshape(NQ, BLK)
    e = ends[:, None, None]
    low = jnp.max(jnp.where(e[CTX:] <= pos[None], e[:-CTX], 0), axis=0)
    high = jnp.min(jnp.where(e > pos[None], e, jnp.int32(1 << 30)), axis=0)
    return low, jnp.minimum(high, last)


def tile_terms(kv_ref, qg_ref, lohi_ref, n, t, base):
    rows = pl.ds(pl.multiple_of(t * BLK, BLK), BLK)
    k = kv_ref[rows, :HD]
    v = kv_ref[rows, HD:]
    q = qg_ref[n, :, :HD]
    g = qg_ref[n, :, HD:]
    dims = (((1,), (1,)), ((), ()))
    s = lax.dot_general(k, q, dims, preferred_element_type=jnp.float32) * (LOG2E / math.sqrt(HD))
    dp = lax.dot_general(v, g, dims, preferred_element_type=jnp.float32)
    pos = base + t * BLK + lax.broadcasted_iota(jnp.int32, (BLK, BLK), 0)
    lohi = lohi_ref[n]
    allowed = (pos >= lohi[0:1]) & (pos < lohi[1:2])
    return jnp.where(allowed, s, NEG), dp, q, g, rows


def stats_kernel(info_ref, qg_ref, kva_ref, kvb_ref, lohi_ref, out_ref):
    x = info_ref[0]

    def run(kv_ref, base, first, last):
        def block(n, _):
            def tile(t, carry):
                m, l, u = carry
                s, dp, _, _, _ = tile_terms(kv_ref, qg_ref, lohi_ref, n, t, base)
                m_new = jnp.maximum(m, jnp.max(s, axis=0, keepdims=True))
                keep = jnp.exp2(m - m_new)
                e = jnp.exp2(s - m_new)
                l = l * keep + jnp.sum(e, axis=0, keepdims=True)
                u = u * keep + jnp.sum(e * dp, axis=0, keepdims=True)
                return m_new, l, u

            zero = jnp.zeros((1, BLK), jnp.float32)
            m, l, u = lax.fori_loop(
                info_ref[8 + n], info_ref[16 + n], tile, (jnp.full((1, BLK), NEG, jnp.float32), zero, zero)
            )
            l = jnp.where(m > 0.5 * NEG, l, 1.0)
            out_ref[n, 0:1] = m + jnp.log2(l)
            out_ref[n, 1:2] = u / l
            return 0

        lax.fori_loop(first, last, block, 0)

    run(kvb_ref, info_ref[2], 0, x * NC)
    run(kva_ref, info_ref[1], x * NC, NQ)


def grads_kernel(
    info_ref, qg_ref, kva_ref, kvb_ref, lohi_ref, stats_ref, dq_ref, da_ref, db_ref, ka_ref, kb_ref, acca_ref, accb_ref
):
    x = info_ref[0]
    scale = 1.0 / math.sqrt(HD)
    ka_ref[...] = kva_ref[:, :HD].T
    kb_ref[...] = kvb_ref[:, :HD].T
    acca_ref[...] = jnp.zeros_like(acca_ref)
    accb_ref[...] = jnp.zeros_like(accb_ref)

    def run(kv_ref, kt_ref, acc_ref, base, first, last):
        def block(n, _):
            part = [stats_ref[i, n] for i in range(NX)]
            top = functools.reduce(jnp.maximum, [p[0:1] for p in part])
            weights = [jnp.exp2(p[0:1] - top) for p in part]
            total = sum(weights)
            lse = top + jnp.log2(total)
            delta = sum(w * p[1:2] for w, p in zip(weights, part)) / total

            def tile(t, dq):
                s, dp, q, g, rows = tile_terms(kv_ref, qg_ref, lohi_ref, n, t, base)
                p = jnp.exp2(s - lse)
                pb = p.astype(jnp.bfloat16)
                ds = (p * (dp - delta)).astype(jnp.bfloat16)
                dims = (((1,), (0,)), ((), ()))
                acc_ref[rows, HD:] += lax.dot_general(pb, g, dims, preferred_element_type=jnp.float32)
                acc_ref[rows, :HD] += lax.dot_general(ds, q, dims, preferred_element_type=jnp.float32)
                return dq + lax.dot_general(kt_ref[:, rows], ds, dims, preferred_element_type=jnp.float32)

            dq = lax.fori_loop(info_ref[8 + n], info_ref[16 + n], tile, jnp.zeros((HD, BLK), jnp.float32))
            dq_ref[n] = (dq * scale).astype(jnp.bfloat16)
            return 0

        lax.fori_loop(first, last, block, 0)

    run(kvb_ref, kb_ref, accb_ref, info_ref[2], 0, x * NC)
    run(kva_ref, ka_ref, acca_ref, info_ref[1], x * NC, NQ)
    for i in range(COL):
        rows = slice(i * BLK, (i + 1) * BLK)
        for out_ref, acc_ref in ((da_ref, acca_ref), (db_ref, accb_ref)):
            out_ref[i, :, :HD] = (acc_ref[rows, :HD] * scale).astype(jnp.bfloat16)
            out_ref[i, :, HD:] = acc_ref[rows, HD:].astype(jnp.bfloat16)


SMEM = pl.BlockSpec(memory_space=pltpu.SMEM)
VMEM = pl.BlockSpec(memory_space=pltpu.VMEM)


def per_device(queries, keys, values, grad_out, group_lengths):
    row = lax.axis_index("outer").astype(jnp.int32)
    inner = lax.axis_index("inner").astype(jnp.int32)
    x, y_lo = inner // COL, inner // NC % NY

    kv = by_head(keys, values)
    kv_before = row_step(kv, 1)
    qg = jnp.broadcast_to(by_head(queries, grad_out)[None], (NX, HEADS, BLK, 2 * HD))
    qg = exchange(qg.reshape(NQ, BLK, 2 * HD), XC_GROUPS)

    def column(value):
        return exchange(jnp.broadcast_to(value[None], (NY,) + value.shape).reshape(COL, BLK, 2 * HD), COL_GROUPS)

    kva = column(kv).reshape(COL * BLK, 2 * HD)
    kvb = column(kv_before).reshape(COL * BLK, 2 * HD)

    low, high = key_ranges(group_lengths, row, y_lo)
    lohi = jnp.stack([low, high], axis=1)
    base_a = (row * ROW + x * COL) * BLK
    base_b = base_a - ROW * BLK
    base = jnp.where(jnp.arange(NQ, dtype=jnp.int32) < x * NC, base_b, base_a)
    tile_first = jnp.clip((low[:, 0] - base) // BLK, 0, COL)
    tile_last = jnp.clip((high[:, -1] - base + BLK - 1) // BLK, 0, COL)
    info = jnp.concatenate([jnp.stack([x, base_a, base_b, row, x, x, x, x]), tile_first, tile_last]).astype(jnp.int32)

    params = pltpu.CompilerParams(vmem_limit_bytes=48 * 1024 * 1024)
    stats = pl.pallas_call(
        stats_kernel,
        out_shape=jax.ShapeDtypeStruct((NQ, 2, BLK), jnp.float32),
        in_specs=[SMEM, VMEM, VMEM, VMEM, VMEM],
        out_specs=VMEM,
        compiler_params=params,
        cost_estimate=pl.CostEstimate(flops=16 * 2 * 2 * BLK * BLK * HD, bytes_accessed=2 << 20, transcendentals=16 * BLK * BLK),
        name="stats",
    )(info, qg, kva, kvb, lohi)

    stats = exchange(jnp.broadcast_to(stats[None], (NX,) + stats.shape), X_GROUPS)

    dq, da, db = pl.pallas_call(
        grads_kernel,
        out_shape=(
            jax.ShapeDtypeStruct((NQ, HD, BLK), jnp.bfloat16),
            jax.ShapeDtypeStruct((COL, BLK, 2 * HD), jnp.bfloat16),
            jax.ShapeDtypeStruct((COL, BLK, 2 * HD), jnp.bfloat16),
        ),
        in_specs=[SMEM, VMEM, VMEM, VMEM, VMEM, VMEM],
        out_specs=(VMEM, VMEM, VMEM),
        scratch_shapes=[
            pltpu.VMEM((HD, COL * BLK), jnp.bfloat16),
            pltpu.VMEM((HD, COL * BLK), jnp.bfloat16),
            pltpu.VMEM((COL * BLK, 2 * HD), jnp.float32),
            pltpu.VMEM((COL * BLK, 2 * HD), jnp.float32),
        ],
        compiler_params=params,
        cost_estimate=pl.CostEstimate(flops=16 * 5 * 2 * BLK * BLK * HD, bytes_accessed=4 << 20, transcendentals=16 * BLK * BLK),
        name="grads",
    )(info, qg, kva, kvb, lohi, stats)

    def owners(value):
        value = exchange(value, COL_GROUPS).reshape(NY, HEADS, BLK, 2 * HD)
        return jnp.sum(value.astype(jnp.float32), axis=0)

    from_next = row_step(owners(db).astype(jnp.bfloat16), -1)
    dq = exchange(dq, XC_GROUPS).reshape(NX, HEADS, HD, BLK)
    dq = jnp.sum(dq.astype(jnp.float32), axis=0).astype(jnp.bfloat16)
    grad_q = jnp.transpose(dq, (2, 0, 1)).reshape(BLK, HEADS * HD)
    dkv = (owners(da) + from_next.astype(jnp.float32)).astype(jnp.bfloat16)
    grad_k = jnp.concatenate([dkv[h, :, :HD] for h in range(HEADS)], axis=1)
    grad_v = jnp.concatenate([dkv[h, :, HD:] for h in range(HEADS)], axis=1)
    return grad_q, grad_k, grad_v


def solution(mesh):
    placed = P(("outer", "inner"), None)
    return jax.shard_map(
        per_device,
        mesh=mesh,
        in_specs=(placed, placed, placed, placed, P()),
        out_specs=(placed, placed, placed),
        check_vma=False,
    )
```

time: 584 us -> 137 us (0.23)
  the two profiles are of different devices: /device:TPU:247 before, /device:TPU:136 now
where the time goes in v1:
time: 137 us; the launch traced here: 136 us
  waiting for transfers between devices  51.9 us (38%)
  blocking collectives  32 us (23%)
  starting transfers between devices  25.7 us (19%)
  Pallas kernels  15.2 us (11%)
  local copies, waits for them, and re-layouts  5.9 us (4%)
  other arithmetic  4.69 us (3%)
    all_to_all x4, waiting for transfers between devices, exchange(): lax.all_to_all(value, 'inner', 0, 0, axis_index_groups=groups, tiled=True)  34.3 us
    all_to_all x3, blocking collectives, exchange(): lax.all_to_all(value, 'inner', 0, 0, axis_index_groups=groups, tiled=True)  32 us
    ppermute x2, waiting for transfers between devices, row_step(): lax.ppermute(value, 'outer', [(i, i + steps) for i in range(first, last)])  17.6 us
    all_to_all x4, starting transfers between devices, exchange(): lax.all_to_all(value, 'inner', 0, 0, axis_index_groups=groups, tiled=True)  16.8 us
    pallas_call x1, Pallas kernels, per_device(): pl.pallas_call(grads_kernel, out_shape=(jax.ShapeDtypeStruct((NQ, HD, BLK...  9.51 us
    ppermute x2, starting transfers between devices, row_step(): lax.ppermute(value, 'outer', [(i, i + steps) for i in range(first, last)])  8.93 us
    pallas_call x1, Pallas kernels, per_device(): pl.pallas_call(stats_kernel, out_shape=jax.ShapeDtypeStruct((NQ, 2, BLK),...  5.71 us
  transfers between devices with their start and end apart: 6, of which 5 were waited for; matrix products, arithmetic and copies ran while one was open for 5% of the time, Pallas kernels for 0%

profile of v1, /device:TPU:136, one launch (start us, length us, event | category | flops | bytes accessed | tf_op | source)
XLA Modules:
  0.0 136.3 jit_solution(2149421883651665025)
XLA Ops:
  0.6 0.9 fusion.3
  1.5 0.9 fusion.4
  2.5 0.0 copy-start.2
  2.5 0.0 copy-start
  2.5 0.0 copy-start.1
  2.5 4.6 %collective-permute-start = (bf16[2,256,256]{2,1,0:T(8,128)(2,1)S(1)}, bf16[2,256,256]{2,1,0:T(8,128)(2,1)S(1)}, u32[]{:S(2)}, u32[]{:S(2)}) collective-permute-start(bf16[2,256,256]{2,1,0:T(8,128)(2,1)S(1)} %pad_maximum_fusion.1), channel_id=1, source_target_pairs={{0,16},{16,32},{32,48},{48,64},{64,80},{80,96},{96,112},{112,128},... | collective-permute-start | bytes 786440 | tf_op jit(solution)/shard_map/ppermute | solution.py:34
  7.2 0.8 broadcast_in_dim.67
  8.0 3.9 %all-to-all-start.1 = ((bf16[4,256,256]{2,1,0:T(8,128)(2,1)}), bf16[4,256,256]{2,1,0:T(8,128)(2,1)S(1)}, u32[]{:S(2)}, u32[]{:S(2)}) async-start(bf16[4,256,256]{2,1,0:T(8,128)(2,1)} %bitcast.14), calls=%async_computation.1 | async-start | bytes 1048576 | tf_op jit(solution)/shard_map/all_to_all | solution.py:28
  11.9 0.0 copy-done.2
  11.9 0.3 reduce-window.9
  12.2 0.1 slice.55
  12.3 0.1 add_multiply_fusion
  12.4 0.1 mul.44
  12.5 0.1 slice_reduce_fusion.1
  12.7 0.1 fusion.8
  12.8 0.1 iota_add_fusion
  12.8 12.1 %all-to-all-done.1 = bf16[4,256,256]{2,1,0:T(8,128)(2,1)S(1)} async-done(((bf16[4,256,256]{2,1,0:T(8,128)(2,1)}), bf16[4,256,256]{2,1,0:T(8,128)(2,1)S(1)}, u32[]{:S(2)}, u32[]{:S(2)}) %all-to-all-start.1) | async-done | bytes 524320 | tf_op jit(solution)/shard_map/all_to_all | solution.py:28
  24.9 1.1 broadcast_in_dim.66
  26.0 4.3 %all-to-all-start = ((bf16[8,256,256]{2,1,0:T(8,128)(2,1)}), bf16[8,256,256]{2,1,0:T(8,128)(2,1)S(1)}, u32[]{:S(2)}, u32[]{:S(2)}) async-start(bf16[8,256,256]{2,1,0:T(8,128)(2,1)} %bitcast.11), calls=%async_computation | async-start | bytes 2097152 | tf_op jit(solution)/shard_map/all_to_all | solution.py:28
  30.3 0.8 select_reduce_fusion
  31.1 0.1 broadcast_add_fusion
  31.2 0.1 fusion.7
  31.3 1.1 select_reduce_fusion.1
  32.4 0.0 collective-permute-done
  32.4 13.9 %all-to-all-done.qg_ref = bf16[8,256,256]{2,1,0:T(8,128)(2,1)S(1)} async-done(((bf16[8,256,256]{2,1,0:T(8,128)(2,1)}), bf16[8,256,256]{2,1,0:T(8,128)(2,1)S(1)}, u32[]{:S(2)}, u32[]{:S(2)}) %all-to-all-start) | async-done | bytes 1048608 | tf_op jit(solution)/shard_map/all_to_all | solution.py:28
  46.2 0.8 broadcast_in_dim.68
  47.1 3.5 %all-to-all-start.2 = ((bf16[4,256,256]{2,1,0:T(8,128)(2,1)}), bf16[4,256,256]{2,1,0:T(8,128)(2,1)S(1)}, u32[]{:S(2)}, u32[]{:S(2)}) async-start(bf16[4,256,256]{2,1,0:T(8,128)(2,1)} %bitcast.16), calls=%async_computation.2 | async-start | bytes 1048576 | tf_op jit(solution)/shard_map/all_to_all | solution.py:28
  50.5 0.1 slice_reduce_fusion
  50.7 0.2 fusion
  50.9 0.1 concatenate.21.info_ref
  51.0 0.1 reshape_minimum_fusion
  51.1 6.5 %all-to-all-done.2 = bf16[4,256,256]{2,1,0:T(8,128)(2,1)S(1)} async-done(((bf16[4,256,256]{2,1,0:T(8,128)(2,1)}), bf16[4,256,256]{2,1,0:T(8,128)(2,1)S(1)}, u32[]{:S(2)}, u32[]{:S(2)}) %all-to-all-start.2) | async-done | bytes 524320 | tf_op jit(solution)/shard_map/all_to_all | solution.py:28
  57.5 5.7 %stats.1 = f32[8,2,256]{2,1,0:T(2,128)S(1)} custom-call(s32[24]{0:T(128)S(1)} %concatenate.21.info_ref, bf16[8,256,256]{2,1,0:T(8,128)(2,1)S(1)} %all-to-all-done.qg_ref, bf16[1024,256]{1,0:T(8,128)(2,1)S(1)} %bitcast.38, bf16[1024,256]{1,0:T(8,128)(2,1)S(1)} %bitcast.40, s32[8,2,256]{2,1,0:T(2,128)S(1)} %pad_add_fusion.lohi_ref), custom_call_target="tpu_custom_call" | custom-call | flops 536870912 | bytes 2097152 | tf_op jit(solution)/shard_map/stats/pallas_call | solution.py:179
  63.3 8.0 %all_to_all.35.stats_ref = f32[4,8,2,256]{3,2,1,0:T(2,128)S(1)} all-to-all(f32[4,8,2,256]{3,2,1,0:T(2,128)S(1)} %broadcast_in_dim.69), channel_id=1, replica_groups={{0,4,8,12},{1,5,9,13},{2,6,10,14},{3,7,11,15},{16,20,24,28},{17,21,25,2..., dimensions={0} | all-to-all | bytes 131072 | tf_op jit(solution)/shard_map/all_to_all | solution.py:28
  71.3 9.5 %grads.1 = (bf16[8,128,256]{2,1,0:T(8,128)(2,1)S(1)}, bf16[4,256,256]{2,1,0:T(8,128)(2,1)}, bf16[4,256,256]{2,1,0:T(8,128)(2,1)S(1)}) custom-call(s32[24]{0:T(128)S(1)} %concatenate.21.info_ref, bf16[8,256,256]{2,1,0:T(8,128)(2,1)S(1)} %all-to-all-done.qg_ref, bf16[1024,256]{1,0:T(8,128)(2,1)S(1)} %bitcast.39, bf16[1024,256]{1,0:T(8,128)(2,1)S(1)} %bitcast.41, ...), custom_call_target="tpu_custom_call" | custom-call | flops 1342177280 | bytes 4194304 | tf_op jit(solution)/shard_map/grads/pallas_call | solution.py:191
  80.8 12.9 %all_to_all.36 = bf16[8,128,256]{2,1,0:T(8,128)(2,1)S(1)} all-to-all(bf16[8,128,256]{2,1,0:T(8,128)(2,1)S(1)} %get-tuple-element.6), channel_id=1, replica_groups={{0,1,4,5,8,9,12,13},{2,3,6,7,10,11,14,15},{16,17,20,21,24,25,28,29},{18..., dimensions={0} | all-to-all | bytes 1048576 | tf_op jit(solution)/shard_map/all_to_all | solution.py:28
  93.7 11.1 %all_to_all.37 = bf16[4,256,256]{2,1,0:T(8,128)(2,1)S(1)} all-to-all(bf16[4,256,256]{2,1,0:T(8,128)(2,1)S(1)} %get-tuple-element.8), channel_id=1, replica_groups={{0,1,2,3},{4,5,6,7},{8,9,10,11},{12,13,14,15},{16,17,18,19},{20,21,22,2..., dimensions={0} | all-to-all | bytes 1048576 | tf_op jit(solution)/shard_map/all_to_all | solution.py:28
  104.8 5.1 %all-to-all-start.5 = ((bf16[4,256,256]{2,1,0:T(8,128)(2,1)}), bf16[4,256,256]{2,1,0:T(8,128)(2,1)S(1)}, u32[]{:S(2)}, u32[]{:S(2)}) async-start(bf16[4,256,256]{2,1,0:T(8,128)(2,1)} %get-tuple-element.7), calls=%async_computation.5 | async-start | bytes 1048576 | tf_op jit(solution)/shard_map/all_to_all | solution.py:28
  109.9 0.2 reduce_sum.35
  110.1 4.3 %collective-permute-start.1 = (bf16[2,256,256]{2,1,0:T(8,128)(2,1)S(1)}, bf16[2,256,256]{2,1,0:T(8,128)(2,1)S(1)}, u32[]{:S(2)}, u32[]{:S(2)}) collective-permute-start(bf16[2,256,256]{2,1,0:T(8,128)(2,1)S(1)} %reduce_sum.35), channel_id=1, source_target_pairs={{16,0},{32,16},{48,32},{64,48},{80,64},{96,80},{112,96},{128,112},... | collective-permute-start | bytes 786440 | tf_op jit(solution)/shard_map/ppermute | solution.py:34
  114.4 0.1 reduce_sum.33
  114.5 0.8 copy.9
  115.3 1.8 %all-to-all-done.5 = bf16[4,256,256]{2,1,0:T(8,128)(2,1)S(1)} async-done(((bf16[4,256,256]{2,1,0:T(8,128)(2,1)}), bf16[4,256,256]{2,1,0:T(8,128)(2,1)S(1)}, u32[]{:S(2)}, u32[]{:S(2)}) %all-to-all-start.5) | async-done | bytes 524320 | tf_op jit(solution)/shard_map/all_to_all | solution.py:28
  117.1 0.1 convert_reduce_fusion
  117.2 17.6 %collective-permute-done.1 = bf16[2,256,256]{2,1,0:T(8,128)(2,1)S(1)} collective-permute-done((bf16[2,256,256]{2,1,0:T(8,128)(2,1)S(1)}, bf16[2,256,256]{2,1,0:T(8,128)(2,1)S(1)}, u32[]{:S(2)}, u32[]{:S(2)}) %collective-permute-start.1) | collective-permute-done | bytes 262176 | tf_op jit(solution)/shard_map/ppermute | solution.py:34
  134.8 0.1 add_convert_fusion
  134.9 0.7 pad_maximum_fusion.3
  135.6 0.7 pad_maximum_fusion.2
  (16 shorter events, 0.3 us)
Async XLA Ops:
  2.5 9.4 %copy-start.2 = (s32[256]{0:T(256)S(1)}, s32[256]{0:T(256)}, u32[]{:S(2)}) copy-start(s32[256]{0:T(256)} %param.9) | copy-start | bytes 3076
  2.5 10.0 %copy-start = (bf16[256,256]{1,0:T(8,128)(2,1)S(1)}, bf16[256,256]{1,0:T(8,128)(2,1)}, u32[]{:S(2)}) copy-start(bf16[256,256]{1,0:T(8,128)(2,1)} %param.5) | copy-start | bytes 393220
  2.5 10.0 %copy-start.1 = (bf16[256,256]{1,0:T(8,128)(2,1)S(1)}, bf16[256,256]{1,0:T(8,128)(2,1)}, u32[]{:S(2)}) copy-start(bf16[256,256]{1,0:T(8,128)(2,1)} %param.8) | copy-start | bytes 393220
  2.5 29.9 %collective-permute-start = (bf16[2,256,256]{2,1,0:T(8,128)(2,1)S(1)}, bf16[2,256,256]{2,1,0:T(8,128)(2,1)S(1)}, u32[]{:S(2)}, u32[]{:S(2)}) collective-permute-start(bf16[2,256,256]{2,1,0:T(8,128)(2,1)S(1)} %pad_maximum_fusion.1), channel_id=1, source_target_pairs={{0,16},{16,32},{32,48},{48,64},{64,80},{80,96},{96,112},{112,128},... | collective-permute-start | bytes 786440 | tf_op jit(solution)/shard_map/ppermute | solution.py:34
  8.0 16.9 %all-to-all-start.1 = ((bf16[4,256,256]{2,1,0:T(8,128)(2,1)}), bf16[4,256,256]{2,1,0:T(8,128)(2,1)S(1)}, u32[]{:S(2)}, u32[]{:S(2)}) async-start(bf16[4,256,256]{2,1,0:T(8,128)(2,1)} %bitcast.14), calls=%async_computation.1 | async-start | bytes 1048576 | tf_op jit(solution)/shard_map/all_to_all | solution.py:28
  26.0 20.3 %all-to-all-start = ((bf16[8,256,256]{2,1,0:T(8,128)(2,1)}), bf16[8,256,256]{2,1,0:T(8,128)(2,1)S(1)}, u32[]{:S(2)}, u32[]{:S(2)}) async-start(bf16[8,256,256]{2,1,0:T(8,128)(2,1)} %bitcast.11), calls=%async_computation | async-start | bytes 2097152 | tf_op jit(solution)/shard_map/all_to_all | solution.py:28
  47.1 10.5 %all-to-all-start.2 = ((bf16[4,256,256]{2,1,0:T(8,128)(2,1)}), bf16[4,256,256]{2,1,0:T(8,128)(2,1)S(1)}, u32[]{:S(2)}, u32[]{:S(2)}) async-start(bf16[4,256,256]{2,1,0:T(8,128)(2,1)} %bitcast.16), calls=%async_computation.2 | async-start | bytes 1048576 | tf_op jit(solution)/shard_map/all_to_all | solution.py:28
  104.8 12.3 %all-to-all-start.5 = ((bf16[4,256,256]{2,1,0:T(8,128)(2,1)}), bf16[4,256,256]{2,1,0:T(8,128)(2,1)S(1)}, u32[]{:S(2)}, u32[]{:S(2)}) async-start(bf16[4,256,256]{2,1,0:T(8,128)(2,1)} %get-tuple-element.7), calls=%async_computation.5 | async-start | bytes 1048576 | tf_op jit(solution)/shard_map/all_to_all | solution.py:28
  110.1 24.7 %collective-permute-start.1 = (bf16[2,256,256]{2,1,0:T(8,128)(2,1)S(1)}, bf16[2,256,256]{2,1,0:T(8,128)(2,1)S(1)}, u32[]{:S(2)}, u32[]{:S(2)}) collective-permute-start(bf16[2,256,256]{2,1,0:T(8,128)(2,1)S(1)} %reduce_sum.35), channel_id=1, source_target_pairs={{16,0},{32,16},{48,32},{64,48},{80,64},{96,80},{112,96},{128,112},... | collective-permute-start | bytes 786440 | tf_op jit(solution)/shard_map/ppermute | solution.py:34

commit v2 on v1

v2 whole, which is shorter than its diff:
```python
import functools
import math

import jax
import jax.numpy as jnp
from jax import lax
from jax.experimental import pallas as pl
from jax.experimental.pallas import tpu as pltpu
from jax.sharding import PartitionSpec as P

HEADS = 2
HD = 128
CTX = 2
BLK = 256
NX, NY, NC = 4, 2, 2
ROW = NX * NY * NC
COL = NY * NC
NQ = NX * NC
NEG = -1e30
UNROLL = 4
LOG2E = math.log2(math.e)

XC_GROUPS = [[x * 4 + y * 2 + c for x in range(NX) for c in range(NC)] for y in range(NY)]
X_GROUPS = [[x * 4 + k for x in range(NX)] for k in range(COL)]


def exchange(value, groups):
    return lax.all_to_all(value, "inner", 0, 0, axis_index_groups=groups, tiled=True)


def row_step(value, steps):
    count = lax.axis_size("outer")
    first, last = max(0, -steps), min(count, count - steps)
    return lax.ppermute(value, "outer", [(i, i + steps) for i in range(first, last)])


def partner(value, flip):
    return lax.ppermute(value, "inner", [(i ^ flip, i) for i in range(ROW)])


def key_ranges(group_lengths, row, y_lo, core):
    ends = jnp.cumsum(group_lengths).astype(jnp.int32)
    x = jnp.arange(NX, dtype=jnp.int32)[:, None, None]
    c = jnp.arange(NC, dtype=jnp.int32)[None, :, None] ^ core
    i = jnp.arange(BLK, dtype=jnp.int32)[None, None, :]
    first = (row * ROW + x * COL + y_lo * NC + c) * BLK
    pos = (first + i).reshape(NQ, BLK)
    last = (first + BLK + 0 * i).reshape(NQ, BLK)
    e = ends[:, None, None]
    low = jnp.max(jnp.where(e[CTX:] <= pos[None], e[:-CTX], 0), axis=0)
    high = jnp.min(jnp.where(e > pos[None], e, jnp.int32(1 << 30)), axis=0)
    return low, jnp.minimum(high, last)


def list_tiles(info_ref, tiles_ref):
    x = info_ref[0]
    count = jnp.int32(0)
    for n in range(NQ):
        before = n // NC < x
        row = jnp.where(before, COL * BLK, 0)
        pos = jnp.where(before, info_ref[2], info_ref[1])

        def put(t, i, n=n, row=row, pos=pos):
            tiles_ref[0, i] = n
            tiles_ref[1, i] = row + t * BLK
            tiles_ref[2, i] = pos + t * BLK
            return i + 1

        count = lax.fori_loop(info_ref[8 + n], info_ref[16 + n], put, count)
    for i in range(UNROLL - 1):
        tiles_ref[0, count + i] = 0
        tiles_ref[1, count + i] = 0
        tiles_ref[2, count + i] = -(1 << 30)
    return (count + UNROLL - 1) // UNROLL


def tile_terms(tiles_ref, i, kv_ref, qg_ref, lohi_ref):
    n, row, pos = tiles_ref[0, i], tiles_ref[1, i], tiles_ref[2, i]
    rows = pl.ds(pl.multiple_of(row, BLK), BLK)
    k = kv_ref[rows, :HD]
    v = kv_ref[rows, HD:]
    q = qg_ref[n, :, :HD]
    g = qg_ref[n, :, HD:]
    dims = (((1,), (1,)), ((), ()))
    s = lax.dot_general(k, q, dims, preferred_element_type=jnp.float32) * (LOG2E / math.sqrt(HD))
    dp = lax.dot_general(v, g, dims, preferred_element_type=jnp.float32)
    key = lax.broadcasted_iota(jnp.int32, (BLK, BLK), 0)
    low, high = lohi_ref[n, 0:1] - pos, lohi_ref[n, 1:2] - pos
    return n, rows, q, g, jnp.where((key >= low) & (key < high), s, NEG), dp


def pack_kernel(info_ref, q_ref, k_ref, v_ref, g_ref, give_ref, kv_ref, qg_ref):
    core = info_ref[0]
    refs = (k_ref, v_ref, q_ref, g_ref)
    for c in range(NC):

        @pl.when(core == c)
        def _():
            for i, ref in enumerate(refs):
                give_ref[:, i * HD : (i + 1) * HD] = ref[:, (1 - c) * HD : (2 - c) * HD]
                mine_ref = (kv_ref, qg_ref)[i // 2]
                mine_ref[:, i % 2 * HD : (i % 2 + 1) * HD] = ref[:, c * HD : (c + 1) * HD]


def assemble(y_lo, core, own_ref, other_ref, out_ref, start):
    for y, ref in ((y_lo, own_ref), (1 - y_lo, other_ref)):
        for i in range(NC):
            row = start + (y * NC + (core ^ i)) * BLK
            out_ref[pl.ds(pl.multiple_of(row, BLK), BLK)] = ref[i]


def stats_kernel(
    info_ref, qg_ref, kva_own_ref, kva_other_ref, kvb_own_ref, kvb_other_ref, lohi_ref,
    out_ref, tiles_ref, kv_ref, m_ref, l_ref, u_ref,
):
    y_lo, core = info_ref[3], info_ref[4]
    pairs = list_tiles(info_ref, tiles_ref)
    assemble(y_lo, core, kva_own_ref, kva_other_ref, kv_ref, 0)
    assemble(y_lo, core, kvb_own_ref, kvb_other_ref, kv_ref, COL * BLK)
    m_ref[...] = jnp.full_like(m_ref, NEG)
    l_ref[...] = jnp.zeros_like(l_ref)
    u_ref[...] = jnp.zeros_like(u_ref)

    def step(i, _):
        terms = [tile_terms(tiles_ref, UNROLL * i + j, kv_ref, qg_ref, lohi_ref) for j in range(UNROLL)]
        parts = []
        for n, _, _, _, s, dp in terms:
            m = jnp.max(s, axis=0, keepdims=True)
            e = jnp.exp2(s - m)
            parts.append((n, m, jnp.sum(e, axis=0, keepdims=True), jnp.sum(e * dp, axis=0, keepdims=True)))
        for n, m, l, u in parts:
            old = m_ref[n]
            new = jnp.maximum(old, m)
            keep, add = jnp.exp2(old - new), jnp.exp2(m - new)
            m_ref[n] = new
            l_ref[n] = l_ref[n] * keep + l * add
            u_ref[n] = u_ref[n] * keep + u * add
        return 0

    lax.fori_loop(0, pairs, step, 0)
    for n in range(NQ):
        m = m_ref[n]
        l = jnp.where(m > 0.5 * NEG, l_ref[n], 1.0)
        lse, delta = m + jnp.log2(l), u_ref[n] / l
        for i in range(NX):
            out_ref[i, n, 0:1] = lse
            out_ref[i, n, 1:2] = delta


def grads_kernel(
    info_ref, qg_ref, kva_own_ref, kva_other_ref, kvb_own_ref, kvb_other_ref, lohi_ref, stats_ref,
    dq_ref, own_a_ref, own_b_ref, away_a_ref, away_b_ref,
    tiles_ref, kv_ref, kt_ref, acc_ref, dqt_ref, sums_ref,
):
    y_lo, core = info_ref[3], info_ref[4]
    scale = 1.0 / math.sqrt(HD)
    pairs = list_tiles(info_ref, tiles_ref)
    assemble(y_lo, core, kva_own_ref, kva_other_ref, kv_ref, 0)
    assemble(y_lo, core, kvb_own_ref, kvb_other_ref, kv_ref, COL * BLK)
    kt_ref[...] = kv_ref[:, :HD].T
    acc_ref[...] = jnp.zeros_like(acc_ref)
    dqt_ref[...] = jnp.zeros_like(dqt_ref)
    for n in range(NQ):
        part = [stats_ref[i, n] for i in range(NX)]
        top = functools.reduce(jnp.maximum, [p[0:1] for p in part])
        weights = [jnp.exp2(p[0:1] - top) for p in part]
        total = sum(weights)
        sums_ref[n, 0:1] = top + jnp.log2(total)
        sums_ref[n, 1:2] = sum(w * p[1:2] for w, p in zip(weights, part)) / total

    def step(i, _):
        terms = [tile_terms(tiles_ref, UNROLL * i + j, kv_ref, qg_ref, lohi_ref) for j in range(UNROLL)]
        parts = []
        for n, rows, q, g, s, dp in terms:
            p = jnp.exp2(s - sums_ref[n, 0:1])
            pb = p.astype(jnp.bfloat16)
            ds = (p * (dp - sums_ref[n, 1:2])).astype(jnp.bfloat16)
            dims = (((1,), (0,)), ((), ()))
            dv = lax.dot_general(pb, g, dims, preferred_element_type=jnp.float32)
            dk = lax.dot_general(ds, q, dims, preferred_element_type=jnp.float32)
            dq = lax.dot_general(kt_ref[:, rows], ds, dims, preferred_element_type=jnp.float32)
            parts.append((n, rows, dk, dv, dq))
        for n, rows, dk, dv, dq in parts:
            acc_ref[rows, :HD] += dk
            acc_ref[rows, HD:] += dv
            dqt_ref[n] += dq
        return 0

    lax.fori_loop(0, pairs, step, 0)
    for n in range(NQ):
        dq_ref[n ^ core] = (dqt_ref[n] * scale).astype(jnp.bfloat16)
    for i in range(NC):
        for start, own_ref, away_ref in ((0, own_a_ref, away_a_ref), (COL * BLK, own_b_ref, away_b_ref)):
            for y, out_ref in ((y_lo, own_ref), (1 - y_lo, away_ref)):
                rows = pl.ds(pl.multiple_of(start + (y * NC + (core ^ i)) * BLK, BLK), BLK)
                out_ref[i, :, :HD] = (acc_ref[rows, :HD] * scale).astype(out_ref.dtype)
                out_ref[i, :, HD:] = acc_ref[rows, HD:].astype(out_ref.dtype)


def finish_kernel(
    info_ref, own_a_ref, got_a_ref, mate_a_ref, next_ref, dq_ref, grad_q_ref, grad_k_ref, grad_v_ref
):
    core = info_ref[0]
    f32 = jnp.float32
    mine = own_a_ref[0] + got_a_ref[0].astype(f32) + next_ref[0].astype(f32)
    other = mate_a_ref[...].astype(f32) + next_ref[1].astype(f32)
    for c in range(NC):

        @pl.when(core == c)
        def _():
            for h, part in ((c, mine), (1 - c, other)):
                cols = slice(h * HD, (h + 1) * HD)
                grad_k_ref[:, cols] = part[:, :HD].astype(jnp.bfloat16)
                grad_v_ref[:, cols] = part[:, HD:].astype(jnp.bfloat16)

    for h in range(HEADS):
        dq = sum(dq_ref[i * HEADS + h].astype(f32) for i in range(NX))
        grad_q_ref[:, h * HD : (h + 1) * HD] = dq.T.astype(jnp.bfloat16)


SMEM = pl.BlockSpec(memory_space=pltpu.SMEM)
VMEM = pl.BlockSpec(memory_space=pltpu.VMEM)
PARAMS = pltpu.CompilerParams(vmem_limit_bytes=24 * 1024 * 1024)


def stats_call(info, qg, kv, lohi):
    return pl.pallas_call(
        stats_kernel,
        out_shape=jax.ShapeDtypeStruct((NX, NQ, 2, BLK), jnp.float32),
        in_specs=[SMEM] + [VMEM] * 6,
        out_specs=VMEM,
        scratch_shapes=[
            pltpu.SMEM((3, NQ * COL + UNROLL), jnp.int32),
            pltpu.VMEM((2 * COL * BLK, 2 * HD), jnp.bfloat16),
        ]
        + [pltpu.VMEM((NQ, 1, BLK), jnp.float32)] * 3,
        compiler_params=PARAMS,
        cost_estimate=pl.CostEstimate(flops=16 * 2 * 2 * BLK * BLK * HD, bytes_accessed=2 << 20, transcendentals=16 * BLK * BLK),
        name="stats",
    )(info, qg, *kv, lohi)


def grads_call(info, qg, kv, lohi, stats):
    part = (NC, BLK, 2 * HD)
    return pl.pallas_call(
        grads_kernel,
        out_shape=(
            jax.ShapeDtypeStruct((NQ, HD, BLK), jnp.bfloat16),
            jax.ShapeDtypeStruct(part, jnp.float32),
            jax.ShapeDtypeStruct(part, jnp.float32),
            jax.ShapeDtypeStruct(part, jnp.bfloat16),
            jax.ShapeDtypeStruct(part, jnp.bfloat16),
        ),
        in_specs=[SMEM] + [VMEM] * 7,
        out_specs=(VMEM,) * 5,
        scratch_shapes=[
            pltpu.SMEM((3, NQ * COL + UNROLL), jnp.int32),
            pltpu.VMEM((2 * COL * BLK, 2 * HD), jnp.bfloat16),
            pltpu.VMEM((HD, 2 * COL * BLK), jnp.bfloat16),
            pltpu.VMEM((2 * COL * BLK, 2 * HD), jnp.float32),
            pltpu.VMEM((NQ, HD, BLK), jnp.float32),
            pltpu.VMEM((NQ, 2, BLK), jnp.float32),
        ],
        compiler_params=PARAMS,
        cost_estimate=pl.CostEstimate(flops=16 * 5 * 2 * BLK * BLK * HD, bytes_accessed=4 << 20, transcendentals=16 * BLK * BLK),
        name="grads",
    )(info, qg, *kv, lohi, stats)


def per_device(queries, keys, values, grad_out, group_lengths):
    row = lax.axis_index("outer").astype(jnp.int32)
    inner = lax.axis_index("inner").astype(jnp.int32)
    x, y_lo, core = inner // COL, inner // NC % NY, inner % NC

    bf16 = jnp.bfloat16
    me = core[None]
    give, kv_mine, qg_mine = pl.pallas_call(
        pack_kernel,
        out_shape=(
            jax.ShapeDtypeStruct((BLK, 4 * HD), bf16),
            jax.ShapeDtypeStruct((BLK, 2 * HD), bf16),
            jax.ShapeDtypeStruct((BLK, 2 * HD), bf16),
        ),
        in_specs=[SMEM] + [VMEM] * 4,
        out_specs=(VMEM,) * 3,
        compiler_params=pltpu.CompilerParams(vmem_limit_bytes=60 * 1024 * 1024),
        cost_estimate=pl.CostEstimate(flops=0, bytes_accessed=1 << 20, transcendentals=0),
        name="pack",
    )(me, queries, keys, values, grad_out)
    got = partner(give, 1)

    kva = jnp.stack([kv_mine, got[:, : 2 * HD]])
    kvb = row_step(kva, 1)
    kva, got = lax.optimization_barrier((kva, got))
    qg = jnp.broadcast_to(jnp.stack([qg_mine, got[:, 2 * HD :]])[None], (NX, NC, BLK, 2 * HD))
    qg, group_lengths = lax.optimization_barrier((qg, group_lengths))
    qg = exchange(qg, X_GROUPS).reshape(NQ, BLK, 2 * HD)
    kv = [kva, partner(kva, 2), kvb, partner(kvb, 2)]

    low, high = key_ranges(group_lengths, row, y_lo, core)
    lohi = jnp.stack([low, high], axis=1)
    base_a = (row * ROW + x * COL) * BLK
    base_b = base_a - ROW * BLK
    base = jnp.where(jnp.arange(NQ, dtype=jnp.int32) < x * NC, base_b, base_a)
    tile_first = jnp.clip((low[:, 0] - base) // BLK, 0, COL)
    tile_last = jnp.clip((high[:, -1] - base + BLK - 1) // BLK, 0, COL)
    info = jnp.concatenate([jnp.stack([x, base_a, base_b, y_lo, core, x, x, x]), tile_first, tile_last]).astype(jnp.int32)

    stats = stats_call(info, qg, kv, lohi)
    stats = exchange(stats, X_GROUPS)

    dq, own_a, own_b, away_a, away_b = grads_call(info, qg, kv, lohi, stats)

    got_b = partner(away_b, 2)
    dq = exchange(dq, XC_GROUPS)
    sum_b = (own_b + got_b.astype(jnp.float32)).astype(bf16)
    sum_b, away_a = lax.optimization_barrier((sum_b, away_a))
    got_a = partner(away_a, 2)
    mate_b, dq = lax.optimization_barrier((partner(sum_b[1], 1), dq))
    from_next = row_step(jnp.stack([sum_b[0], mate_b]), -1)
    mate_a = partner((own_a[1] + got_a[1].astype(jnp.float32)).astype(bf16), 1)
    return pl.pallas_call(
        finish_kernel,
        out_shape=(jax.ShapeDtypeStruct((BLK, HEADS * HD), bf16),) * 3,
        in_specs=[SMEM] + [VMEM] * 5,
        out_specs=(VMEM,) * 3,
        compiler_params=PARAMS,
        cost_estimate=pl.CostEstimate(flops=0, bytes_accessed=2 << 20, transcendentals=0),
        name="finish",
    )(me, own_a, got_a, mate_a, from_next, dq)


def solution(mesh):
    placed = P(("outer", "inner"), None)
    return jax.shard_map(
        per_device,
        mesh=mesh,
        in_specs=(placed, placed, placed, placed, P()),
        out_specs=(placed, placed, placed),
        check_vma=False,
    )
```

time: 137 us -> 96 us (0.70)
  the two profiles are of different devices: /device:TPU:136 before, /device:TPU:248 now
where the time goes in v2:
time: 96 us; the launch traced here: 95.5 us
  starting transfers between devices  34.5 us (36%)
  waiting for transfers between devices  32.1 us (33%)
  Pallas kernels  14.3 us (15%)
  blocking collectives  7.99 us (8%)
  other arithmetic  3.85 us (4%)
  local copies, waits for them, and re-layouts  1.83 us (2%)
    ppermute x7, starting transfers between devices, partner(): return lax.ppermute(value, 'inner', [(i ^ flip, i) for i in range(ROW)])  19.1 us
    ppermute x2, waiting for transfers between devices, row_step(): lax.ppermute(value, 'outer', [(i, i + steps) for i in range(first, last)])  14.7 us
    ppermute x7, waiting for transfers between devices, partner(): return lax.ppermute(value, 'inner', [(i ^ flip, i) for i in range(ROW)])  12.9 us
    all_to_all x1, blocking collectives, exchange(): lax.all_to_all(value, 'inner', 0, 0, axis_index_groups=groups, tiled=True)  7.99 us
    all_to_all x2, starting transfers between devices, exchange(): lax.all_to_all(value, 'inner', 0, 0, axis_index_groups=groups, tiled=True)  7.81 us
    ppermute x2, starting transfers between devices, row_step(): lax.ppermute(value, 'outer', [(i, i + steps) for i in range(first, last)])  7.63 us
    pallas_call x1, Pallas kernels, grads_call(): pl.pallas_call(grads_kernel, out_shape=(jax.ShapeDtypeStruct((NQ, HD, BLK...  7.03 us
    all_to_all x2, waiting for transfers between devices, exchange(): lax.all_to_all(value, 'inner', 0, 0, axis_index_groups=groups, tiled=True)  4.55 us
  transfers between devices with their start and end apart: 11, of which 10 were waited for; matrix products, arithmetic and copies ran while one was open for 5% of the time, Pallas kernels for 0%

profile of v2, /device:TPU:248, one launch (start us, length us, event | category | flops | bytes accessed | tf_op | source)
XLA Modules:
  0.0 95.5 jit_solution(2701377068315838843)
XLA Ops:
  0.6 2.0 %pack.1 = (bf16[256,512]{1,0:T(8,128)(2,1)}, bf16[256,256]{1,0:T(8,128)(2,1)}, bf16[256,256]{1,0:T(8,128)(2,1)}) custom-call(s32[1]{0:T(128)} %bitcast.info_ref, bf16[256,256]{1,0:T(8,128)(2,1)} %q_ref.1, bf16[256,256]{1,0:T(8,128)(2,1)} %k_ref.1, bf16[256,256]{1,0:T(8,128)(2,1)} %v_ref.1, bf16[256,256]{1,0:T(8,128)(2,1)} %g_ref.1), custom_call_target="tpu_custom_call" | custom-call | bytes 1048576 | tf_op jit(solution)/shard_map/pack/pallas_call | solution.py:277
  2.6 2.0 %collective-permute-start = (bf16[256,512]{1,0:T(8,128)(2,1)}, bf16[256,512]{1,0:T(8,128)(2,1)S(1)}, u32[]{:S(2)}, u32[]{:S(2)}) collective-permute-start(bf16[256,512]{1,0:T(8,128)(2,1)} %get-tuple-element.21), channel_id=1, source_target_pairs={{1,0},{0,1},{3,2},{2,3},{5,4},{4,5},{7,6},{6,7},{9,8},{8,9},{11,10... | collective-permute-start | bytes 786440 | tf_op jit(solution)/shard_map/ppermute | solution.py:38
  4.7 0.1 add.115
  4.8 0.1 add.112
  4.9 0.1 add.113
  5.0 0.1 iota_add_fusion
  5.1 1.3 %collective-permute-done = bf16[256,512]{1,0:T(8,128)(2,1)S(1)} collective-permute-done((bf16[256,512]{1,0:T(8,128)(2,1)}, bf16[256,512]{1,0:T(8,128)(2,1)S(1)}, u32[]{:S(2)}, u32[]{:S(2)}) %collective-permute-start) | collective-permute-done | bytes 262176 | tf_op jit(solution)/shard_map/ppermute | solution.py:38
  6.4 0.9 pad_maximum_fusion.kva_own_ref
  7.3 0.0 copy-start.1
  7.3 5.7 %collective-permute-start.2 = (bf16[2,256,256]{2,1,0:T(8,128)(2,1)S(1)}, bf16[2,256,256]{2,1,0:T(8,128)(2,1)S(1)}, u32[]{:S(2)}, u32[]{:S(2)}) collective-permute-start(bf16[2,256,256]{2,1,0:T(8,128)(2,1)S(1)} %pad_maximum_fusion.kva_own_ref), channel_id=1, source_target_pairs={{0,16},{16,32},{32,48},{48,64},{64,80},{80,96},{96,112},{112,128},... | collective-permute-start | bytes 786440 | tf_op jit(solution)/shard_map/ppermute | solution.py:34
  13.1 0.0 copy-done
  13.1 1.1 %broadcast_in_dim.46 = bf16[4,2,256,256]{3,2,1,0:T(8,128)(2,1)} broadcast(bf16[2,256,256]{2,1,0:T(8,128)(2,1)S(1)} %pad_maximum_fusion.1), dimensions={1,2,3} | broadcast | bytes 1310720 | tf_op jit(solution)/shard_map/broadcast_in_dim | solution.py:295
  14.2 0.3 reduce-window.9
  14.5 0.1 slice.39
  14.6 0.1 slice_reduce_fusion.1
  14.7 0.1 fusion.6
  14.8 0.1 broadcast_add_fusion
  14.9 2.3 %collective-permute-start.1 = (bf16[2,256,256]{2,1,0:T(8,128)(2,1)S(1)}, bf16[2,256,256]{2,1,0:T(8,128)(2,1)S(1)}, u32[]{:S(2)}, u32[]{:S(2)}) collective-permute-start(bf16[2,256,256]{2,1,0:T(8,128)(2,1)S(1)} %pad_maximum_fusion.kva_own_ref), channel_id=1, source_target_pairs={{2,0},{3,1},{0,2},{1,3},{6,4},{7,5},{4,6},{5,7},{10,8},{11,9},{8,1... | collective-permute-start | bytes 786440 | tf_op jit(solution)/shard_map/ppermute | solution.py:38
  17.2 0.1 fusion.5
  17.3 0.8 select_reduce_fusion
  18.1 1.1 %select_reduce_fusion.1 = s32[8,256]{1,0:T(8,128)S(1)} fusion(s32[254]{0:T(256)S(1)} %bitcast.32, s32[8,256]{1,0:T(8,128)S(1)} %iota_add_fusion, s32[254]{0:T(256)S(1)} %bitcast.31), kind=kLoop, calls=%fused_computation.1 | loop fusion | flops 1558528 | bytes 18416 | tf_op jit(solution)/shard_map/reduce_max | solution.py:50
  19.2 4.3 %all-to-all-start = ((bf16[4,2,256,256]{3,2,1,0:T(8,128)(2,1)}), bf16[4,2,256,256]{3,2,1,0:T(8,128)(2,1)S(1)}, u32[]{:S(2)}, u32[]{:S(2)}) async-start(bf16[4,2,256,256]{3,2,1,0:T(8,128)(2,1)} %broadcast_in_dim.46), calls=%async_computation | async-start | bytes 2097152 | tf_op jit(solution)/shard_map/all_to_all | solution.py:28
  23.5 0.2 fusion.1
  23.7 0.1 slice_reduce_fusion
  23.8 0.1 concatenate.3.info_ref
  23.9 0.4 collective-permute-done.2.kvb_own_ref
  24.3 3.9 %collective-permute-start.3 = (bf16[2,256,256]{2,1,0:T(8,128)(2,1)S(1)}, bf16[2,256,256]{2,1,0:T(8,128)(2,1)S(1)}, u32[]{:S(2)}, u32[]{:S(2)}) collective-permute-start(bf16[2,256,256]{2,1,0:T(8,128)(2,1)S(1)} %collective-permute-done.2.kvb_own_ref), channel_id=1, source_target_pairs={{2,0},{3,1},{0,2},{1,3},{6,4},{7,5},{4,6},{5,7},{10,8},{11,9},{8,1... | collective-permute-start | bytes 786440 | tf_op jit(solution)/shard_map/ppermute | solution.py:38
  28.2 0.1 reshape_minimum_fusion
  28.3 2.6 %collective-permute-done.1.kva_other_ref = bf16[2,256,256]{2,1,0:T(8,128)(2,1)S(1)} collective-permute-done((bf16[2,256,256]{2,1,0:T(8,128)(2,1)S(1)}, bf16[2,256,256]{2,1,0:T(8,128)(2,1)S(1)}, u32[]{:S(2)}, u32[]{:S(2)}) %collective-permute-start.1) | collective-permute-done | bytes 262176 | tf_op jit(solution)/shard_map/ppermute | solution.py:38
  31.0 4.8 %collective-permute-done.3.kvb_other_ref = bf16[2,256,256]{2,1,0:T(8,128)(2,1)S(1)} collective-permute-done((bf16[2,256,256]{2,1,0:T(8,128)(2,1)S(1)}, bf16[2,256,256]{2,1,0:T(8,128)(2,1)S(1)}, u32[]{:S(2)}, u32[]{:S(2)}) %collective-permute-start.3) | collective-permute-done | bytes 262176 | tf_op jit(solution)/shard_map/ppermute | solution.py:38
  35.8 2.6 %all-to-all-done = bf16[4,2,256,256]{3,2,1,0:T(8,128)(2,1)S(1)} async-done(((bf16[4,2,256,256]{3,2,1,0:T(8,128)(2,1)}), bf16[4,2,256,256]{3,2,1,0:T(8,128)(2,1)S(1)}, u32[]{:S(2)}, u32[]{:S(2)}) %all-to-all-start) | async-done | bytes 1048608 | tf_op jit(solution)/shard_map/all_to_all | solution.py:28
  38.4 4.3 %stats.1 = f32[4,8,2,256]{3,2,1,0:T(2,128)S(1)} custom-call(s32[24]{0:T(128)S(1)} %concatenate.3.info_ref, bf16[8,256,256]{2,1,0:T(8,128)(2,1)S(1)} %bitcast.25, bf16[2,256,256]{2,1,0:T(8,128)(2,1)S(1)} %pad_maximum_fusion.kva_own_ref, bf16[2,256,256]{2,1,0:T(8,128)(2,1)S(1)} %collective-permute-done.1.kva_other_ref, ...), custom_call_target="tpu_custom_call" | custom-call | flops 536870912 | bytes 2097152 | tf_op jit(solution)/shard_map/stats/pallas_call | solution.py:227
  42.7 8.0 %all_to_all.15.stats_ref = f32[4,8,2,256]{3,2,1,0:T(2,128)S(1)} all-to-all(f32[4,8,2,256]{3,2,1,0:T(2,128)S(1)} %stats.1), channel_id=1, replica_groups={{0,4,8,12},{1,5,9,13},{2,6,10,14},{3,7,11,15},{16,20,24,28},{17,21,25,2..., dimensions={0} | all-to-all | bytes 131072 | tf_op jit(solution)/shard_map/all_to_all | solution.py:28
  50.7 7.0 %grads.1 = (bf16[8,128,256]{2,1,0:T(8,128)(2,1)}, f32[2,256,256]{2,1,0:T(8,128)S(1)}, f32[2,256,256]{2,1,0:T(8,128)S(1)}, bf16[2,256,256]{2,1,0:T(8,128)(2,1)S(1)}, bf16[2,256,256]{2,1,0:T(8,128)(2,1)}) custom-call(s32[24]{0:T(128)S(1)} %concatenate.3.info_ref, bf16[8,256,256]{2,1,0:T(8,128)(2,1)S(1)} %bitcast.26, ...), custom_call_target="tpu_custom_call" | custom-call | flops 1342177280 | bytes 4194304 | tf_op jit(solution)/shard_map/grads/pallas_call | solution.py:245
  57.7 3.5 %collective-permute-start.4 = (bf16[2,256,256]{2,1,0:T(8,128)(2,1)}, bf16[2,256,256]{2,1,0:T(8,128)(2,1)S(1)}, u32[]{:S(2)}, u32[]{:S(2)}) collective-permute-start(bf16[2,256,256]{2,1,0:T(8,128)(2,1)} %get-tuple-element.28), channel_id=1, source_target_pairs={{2,0},{3,1},{0,2},{1,3},{6,4},{7,5},{4,6},{5,7},{10,8},{11,9},{8,1... | collective-permute-start | bytes 786440 | tf_op jit(solution)/shard_map/ppermute | solution.py:38
  61.2 3.5 %all-to-all-start.2 = ((bf16[8,128,256]{2,1,0:T(8,128)(2,1)}), bf16[8,128,256]{2,1,0:T(8,128)(2,1)S(1)}, u32[]{:S(2)}, u32[]{:S(2)}) async-start(bf16[8,128,256]{2,1,0:T(8,128)(2,1)} %get-tuple-element.32), calls=%async_computation.2 | async-start | bytes 1048576 | tf_op jit(solution)/shard_map/all_to_all | solution.py:28
  64.7 1.5 %collective-permute-done.4 = bf16[2,256,256]{2,1,0:T(8,128)(2,1)S(1)} collective-permute-done((bf16[2,256,256]{2,1,0:T(8,128)(2,1)}, bf16[2,256,256]{2,1,0:T(8,128)(2,1)S(1)}, u32[]{:S(2)}, u32[]{:S(2)}) %collective-permute-start.4) | collective-permute-done | bytes 262176 | tf_op jit(solution)/shard_map/ppermute | solution.py:38
  66.2 0.1 add_convert_fusion
  66.3 3.5 %collective-permute-start.5 = (bf16[2,256,256]{2,1,0:T(8,128)(2,1)S(1)}, bf16[2,256,256]{2,1,0:T(8,128)(2,1)S(1)}, u32[]{:S(2)}, u32[]{:S(2)}) collective-permute-start(bf16[2,256,256]{2,1,0:T(8,128)(2,1)S(1)} %get-tuple-element.30), channel_id=1, source_target_pairs={{2,0},{3,1},{0,2},{1,3},{6,4},{7,5},{4,6},{5,7},{10,8},{11,9},{8,1... | collective-permute-start | bytes 786440 | tf_op jit(solution)/shard_map/ppermute | solution.py:38
  69.8 1.9 %collective-permute-start.7 = (bf16[256,256]{1,0:T(8,128)(2,1)S(1)}, bf16[256,256]{1,0:T(8,128)(2,1)S(1)}, u32[]{:S(2)}, u32[]{:S(2)}) collective-permute-start(bf16[256,256]{1,0:T(8,128)(2,1)S(1)} %get-tuple-element.38), channel_id=1, source_target_pairs={{1,0},{0,1},{3,2},{2,3},{5,4},{4,5},{7,6},{6,7},{9,8},{8,9},{11,10... | collective-permute-start | bytes 393224 | tf_op jit(solution)/shard_map/ppermute | solution.py:38
  71.7 1.3 %collective-permute-done.7 = bf16[256,256]{1,0:T(8,128)(2,1)S(1)} collective-permute-done((bf16[256,256]{1,0:T(8,128)(2,1)S(1)}, bf16[256,256]{1,0:T(8,128)(2,1)S(1)}, u32[]{:S(2)}, u32[]{:S(2)}) %collective-permute-start.7) | collective-permute-done | bytes 131104 | tf_op jit(solution)/shard_map/ppermute | solution.py:38
  73.0 2.0 %all-to-all-done.2.dq_ref = bf16[8,128,256]{2,1,0:T(8,128)(2,1)S(1)} async-done(((bf16[8,128,256]{2,1,0:T(8,128)(2,1)}), bf16[8,128,256]{2,1,0:T(8,128)(2,1)S(1)}, u32[]{:S(2)}, u32[]{:S(2)}) %all-to-all-start.2) | async-done | bytes 524320 | tf_op jit(solution)/shard_map/all_to_all | solution.py:28
  75.0 1.9 %collective-permute-start.8 = (bf16[2,256,256]{2,1,0:T(8,128)(2,1)S(1)}, bf16[2,256,256]{2,1,0:T(8,128)(2,1)S(1)}, u32[]{:S(2)}, u32[]{:S(2)}) collective-permute-start(bf16[2,256,256]{2,1,0:T(8,128)(2,1)S(1)} %pad_maximum_fusion.2), channel_id=1, source_target_pairs={{16,0},{32,16},{48,32},{64,48},{80,64},{96,80},{112,96},{128,112},... | collective-permute-start | bytes 786440 | tf_op jit(solution)/shard_map/ppermute | solution.py:34
  76.9 0.0 collective-permute-done.5.got_a_ref
  77.0 1.9 %collective-permute-start.6 = (bf16[256,256]{1,0:T(8,128)(2,1)S(1)}, bf16[256,256]{1,0:T(8,128)(2,1)S(1)}, u32[]{:S(2)}, u32[]{:S(2)}) collective-permute-start(bf16[256,256]{1,0:T(8,128)(2,1)S(1)} %fusion), channel_id=1, source_target_pairs={{1,0},{0,1},{3,2},{2,3},{5,4},{4,5},{7,6},{6,7},{9,8},{8,9},{11,10... | collective-permute-start | bytes 393224 | tf_op jit(solution)/shard_map/ppermute | solution.py:38
  78.9 1.3 %collective-permute-done.6.mate_a_ref = bf16[256,256]{1,0:T(8,128)(2,1)S(1)} collective-permute-done((bf16[256,256]{1,0:T(8,128)(2,1)S(1)}, bf16[256,256]{1,0:T(8,128)(2,1)S(1)}, u32[]{:S(2)}, u32[]{:S(2)}) %collective-permute-start.6) | collective-permute-done | bytes 131104 | tf_op jit(solution)/shard_map/ppermute | solution.py:38
  80.2 14.3 %collective-permute-done.8.next_ref = bf16[2,256,256]{2,1,0:T(8,128)(2,1)S(1)} collective-permute-done((bf16[2,256,256]{2,1,0:T(8,128)(2,1)S(1)}, bf16[2,256,256]{2,1,0:T(8,128)(2,1)S(1)}, u32[]{:S(2)}, u32[]{:S(2)}) %collective-permute-start.8) | collective-permute-done | bytes 262176 | tf_op jit(solution)/shard_map/ppermute | solution.py:34
  94.5 0.9 finish.1
  (16 shorter events, 0.2 us)
Async XLA Ops:
  2.6 10.5 %copy-start = (bf16[256,256]{1,0:T(8,128)(2,1)S(1)}, bf16[256,256]{1,0:T(8,128)(2,1)}, u32[]{:S(2)}) copy-start(bf16[256,256]{1,0:T(8,128)(2,1)} %get-tuple-element.19) | copy-start | bytes 393220
  2.6 3.8 %collective-permute-start = (bf16[256,512]{1,0:T(8,128)(2,1)}, bf16[256,512]{1,0:T(8,128)(2,1)S(1)}, u32[]{:S(2)}, u32[]{:S(2)}) collective-permute-start(bf16[256,512]{1,0:T(8,128)(2,1)} %get-tuple-element.21), channel_id=1, source_target_pairs={{1,0},{0,1},{3,2},{2,3},{5,4},{4,5},{7,6},{6,7},{9,8},{8,9},{11,10... | collective-permute-start | bytes 786440 | tf_op jit(solution)/shard_map/ppermute | solution.py:38
  7.3 6.8 %copy-start.1 = (s32[256]{0:T(256)S(1)}, s32[256]{0:T(256)}, u32[]{:S(2)}) copy-start(s32[256]{0:T(256)} %param.9) | copy-start | bytes 3076
  7.3 17.0 %collective-permute-start.2 = (bf16[2,256,256]{2,1,0:T(8,128)(2,1)S(1)}, bf16[2,256,256]{2,1,0:T(8,128)(2,1)S(1)}, u32[]{:S(2)}, u32[]{:S(2)}) collective-permute-start(bf16[2,256,256]{2,1,0:T(8,128)(2,1)S(1)} %pad_maximum_fusion.kva_own_ref), channel_id=1, source_target_pairs={{0,16},{16,32},{32,48},{48,64},{64,80},{80,96},{96,112},{112,128},... | collective-permute-start | bytes 786440 | tf_op jit(solution)/shard_map/ppermute | solution.py:34
  14.9 16.1 %collective-permute-start.1 = (bf16[2,256,256]{2,1,0:T(8,128)(2,1)S(1)}, bf16[2,256,256]{2,1,0:T(8,128)(2,1)S(1)}, u32[]{:S(2)}, u32[]{:S(2)}) collective-permute-start(bf16[2,256,256]{2,1,0:T(8,128)(2,1)S(1)} %pad_maximum_fusion.kva_own_ref), channel_id=1, source_target_pairs={{2,0},{3,1},{0,2},{1,3},{6,4},{7,5},{4,6},{5,7},{10,8},{11,9},{8,1... | collective-permute-start | bytes 786440 | tf_op jit(solution)/shard_map/ppermute | solution.py:38
  19.2 19.1 %all-to-all-start = ((bf16[4,2,256,256]{3,2,1,0:T(8,128)(2,1)}), bf16[4,2,256,256]{3,2,1,0:T(8,128)(2,1)S(1)}, u32[]{:S(2)}, u32[]{:S(2)}) async-start(bf16[4,2,256,256]{3,2,1,0:T(8,128)(2,1)} %broadcast_in_dim.46), calls=%async_computation | async-start | bytes 2097152 | tf_op jit(solution)/shard_map/all_to_all | solution.py:28
  24.3 11.4 %collective-permute-start.3 = (bf16[2,256,256]{2,1,0:T(8,128)(2,1)S(1)}, bf16[2,256,256]{2,1,0:T(8,128)(2,1)S(1)}, u32[]{:S(2)}, u32[]{:S(2)}) collective-permute-start(bf16[2,256,256]{2,1,0:T(8,128)(2,1)S(1)} %collective-permute-done.2.kvb_own_ref), channel_id=1, source_target_pairs={{2,0},{3,1},{0,2},{1,3},{6,4},{7,5},{4,6},{5,7},{10,8},{11,9},{8,1... | collective-permute-start | bytes 786440 | tf_op jit(solution)/shard_map/ppermute | solution.py:38
  57.7 8.5 %collective-permute-start.4 = (bf16[2,256,256]{2,1,0:T(8,128)(2,1)}, bf16[2,256,256]{2,1,0:T(8,128)(2,1)S(1)}, u32[]{:S(2)}, u32[]{:S(2)}) collective-permute-start(bf16[2,256,256]{2,1,0:T(8,128)(2,1)} %get-tuple-element.28), channel_id=1, source_target_pairs={{2,0},{3,1},{0,2},{1,3},{6,4},{7,5},{4,6},{5,7},{10,8},{11,9},{8,1... | collective-permute-start | bytes 786440 | tf_op jit(solution)/shard_map/ppermute | solution.py:38
  61.2 13.8 %all-to-all-start.2 = ((bf16[8,128,256]{2,1,0:T(8,128)(2,1)}), bf16[8,128,256]{2,1,0:T(8,128)(2,1)S(1)}, u32[]{:S(2)}, u32[]{:S(2)}) async-start(bf16[8,128,256]{2,1,0:T(8,128)(2,1)} %get-tuple-element.32), calls=%async_computation.2 | async-start | bytes 1048576 | tf_op jit(solution)/shard_map/all_to_all | solution.py:28
  66.3 10.7 %collective-permute-start.5 = (bf16[2,256,256]{2,1,0:T(8,128)(2,1)S(1)}, bf16[2,256,256]{2,1,0:T(8,128)(2,1)S(1)}, u32[]{:S(2)}, u32[]{:S(2)}) collective-permute-start(bf16[2,256,256]{2,1,0:T(8,128)(2,1)S(1)} %get-tuple-element.30), channel_id=1, source_target_pairs={{2,0},{3,1},{0,2},{1,3},{6,4},{7,5},{4,6},{5,7},{10,8},{11,9},{8,1... | collective-permute-start | bytes 786440 | tf_op jit(solution)/shard_map/ppermute | solution.py:38
  69.8 3.2 %collective-permute-start.7 = (bf16[256,256]{1,0:T(8,128)(2,1)S(1)}, bf16[256,256]{1,0:T(8,128)(2,1)S(1)}, u32[]{:S(2)}, u32[]{:S(2)}) collective-permute-start(bf16[256,256]{1,0:T(8,128)(2,1)S(1)} %get-tuple-element.38), channel_id=1, source_target_pairs={{1,0},{0,1},{3,2},{2,3},{5,4},{4,5},{7,6},{6,7},{9,8},{8,9},{11,10... | collective-permute-start | bytes 393224 | tf_op jit(solution)/shard_map/ppermute | solution.py:38
  75.0 19.5 %collective-permute-start.8 = (bf16[2,256,256]{2,1,0:T(8,128)(2,1)S(1)}, bf16[2,256,256]{2,1,0:T(8,128)(2,1)S(1)}, u32[]{:S(2)}, u32[]{:S(2)}) collective-permute-start(bf16[2,256,256]{2,1,0:T(8,128)(2,1)S(1)} %pad_maximum_fusion.2), channel_id=1, source_target_pairs={{16,0},{32,16},{48,32},{64,48},{80,64},{96,80},{112,96},{128,112},... | collective-permute-start | bytes 786440 | tf_op jit(solution)/shard_map/ppermute | solution.py:34
  77.0 3.2 %collective-permute-start.6 = (bf16[256,256]{1,0:T(8,128)(2,1)S(1)}, bf16[256,256]{1,0:T(8,128)(2,1)S(1)}, u32[]{:S(2)}, u32[]{:S(2)}) collective-permute-start(bf16[256,256]{1,0:T(8,128)(2,1)S(1)} %fusion), channel_id=1, source_target_pairs={{1,0},{0,1},{3,2},{2,3},{5,4},{4,5},{7,6},{6,7},{9,8},{8,9},{11,10... | collective-permute-start | bytes 393224 | tf_op jit(solution)/shard_map/ppermute | solution.py:38

commit v3 on v2

--- a/solution.py
+++ b/solution.py
@@ -28,20 +28,21 @@
     return lax.all_to_all(value, "inner", 0, 0, axis_index_groups=groups, tiled=True)
 
 
-def row_step(value, steps):
+def row_step(value, steps, flip=0):
     count = lax.axis_size("outer")
     first, last = max(0, -steps), min(count, count - steps)
-    return lax.ppermute(value, "outer", [(i, i + steps) for i in range(first, last)])
+    route = [(r * ROW + i, (r + steps) * ROW + (i ^ flip)) for r in range(first, last) for i in range(ROW)]
+    return lax.ppermute(value, ("outer", "inner"), route)
 
 
 def partner(value, flip):
     return lax.ppermute(value, "inner", [(i ^ flip, i) for i in range(ROW)])
 
 
-def key_ranges(group_lengths, row, y_lo, core):
+def key_ranges(group_lengths, row, y_lo):
     ends = jnp.cumsum(group_lengths).astype(jnp.int32)
     x = jnp.arange(NX, dtype=jnp.int32)[:, None, None]
-    c = jnp.arange(NC, dtype=jnp.int32)[None, :, None] ^ core
+    c = jnp.arange(NC, dtype=jnp.int32)[None, :, None]
     i = jnp.arange(BLK, dtype=jnp.int32)[None, None, :]
     first = (row * ROW + x * COL + y_lo * NC + c) * BLK
     pos = (first + i).reshape(NQ, BLK)
@@ -85,38 +86,46 @@
     s = lax.dot_general(k, q, dims, preferred_element_type=jnp.float32) * (LOG2E / math.sqrt(HD))
     dp = lax.dot_general(v, g, dims, preferred_element_type=jnp.float32)
     key = lax.broadcasted_iota(jnp.int32, (BLK, BLK), 0)
-    low, high = lohi_ref[n, 0:1] - pos, lohi_ref[n, 1:2] - pos
-    return n, rows, q, g, jnp.where((key >= low) & (key < high), s, NEG), dp
-
-
-def pack_kernel(info_ref, q_ref, k_ref, v_ref, g_ref, give_ref, kv_ref, qg_ref):
+    low = lohi_ref[n, 0:1]
+    width = (lohi_ref[n, 1:2] - low).astype(jnp.uint32)
+    allowed = (key - (low - pos)).astype(jnp.uint32) < width
+    return n, rows, q, g, jnp.where(allowed, s, NEG), dp
+
+
+def split_kernel(info_ref, k_ref, v_ref, mine_ref, give_ref):
     core = info_ref[0]
-    refs = (k_ref, v_ref, q_ref, g_ref)
     for c in range(NC):
 
         @pl.when(core == c)
         def _():
-            for i, ref in enumerate(refs):
-                give_ref[:, i * HD : (i + 1) * HD] = ref[:, (1 - c) * HD : (2 - c) * HD]
-                mine_ref = (kv_ref, qg_ref)[i // 2]
-                mine_ref[:, i % 2 * HD : (i % 2 + 1) * HD] = ref[:, c * HD : (c + 1) * HD]
-
-
-def assemble(y_lo, core, own_ref, other_ref, out_ref, start):
-    for y, ref in ((y_lo, own_ref), (1 - y_lo, other_ref)):
-        for i in range(NC):
-            row = start + (y * NC + (core ^ i)) * BLK
-            out_ref[pl.ds(pl.multiple_of(row, BLK), BLK)] = ref[i]
+            for i, ref in enumerate((k_ref, v_ref)):
+                cols = slice(i * HD, (i + 1) * HD)
+                mine_ref[:, cols] = ref[:, c * HD : (c + 1) * HD]
+                give_ref[:, cols] = ref[:, (1 - c) * HD : (2 - c) * HD]
+
+
+def pack_kernel(q_ref, g_ref, qg_ref):
+    for n in range(NQ):
+        head = slice(n % HEADS * HD, (n % HEADS + 1) * HD)
+        qg_ref[n, :, :HD] = q_ref[:, head]
+        qg_ref[n, :, HD:] = g_ref[:, head]
+
+
+def assemble(y_lo, core, refs, out_ref):
+    for j, ref in enumerate(refs):
+        y = y_lo ^ (j // NC % NY)
+        row = j // COL * COL * BLK + (y * NC + (core ^ (j % NC))) * BLK
+        out_ref[pl.ds(pl.multiple_of(row, BLK), BLK)] = ref[...]
 
 
 def stats_kernel(
-    info_ref, qg_ref, kva_own_ref, kva_other_ref, kvb_own_ref, kvb_other_ref, lohi_ref,
+    info_ref, qg_ref, a0_ref, a1_ref, a23_ref, b0_ref, b1_ref, b2_ref, b3_ref, lohi_ref,
     out_ref, tiles_ref, kv_ref, m_ref, l_ref, u_ref,
 ):
     y_lo, core = info_ref[3], info_ref[4]
     pairs = list_tiles(info_ref, tiles_ref)
-    assemble(y_lo, core, kva_own_ref, kva_other_ref, kv_ref, 0)
-    assemble(y_lo, core, kvb_own_ref, kvb_other_ref, kv_ref, COL * BLK)
+    blocks = (a0_ref, a1_ref, a23_ref.at[0], a23_ref.at[1], b0_ref, b1_ref, b2_ref, b3_ref)
+    assemble(y_lo, core, blocks, kv_ref)
     m_ref[...] = jnp.full_like(m_ref, NEG)
     l_ref[...] = jnp.zeros_like(l_ref)
     u_ref[...] = jnp.zeros_like(u_ref)
@@ -148,15 +157,15 @@
 
 
 def grads_kernel(
-    info_ref, qg_ref, kva_own_ref, kva_other_ref, kvb_own_ref, kvb_other_ref, lohi_ref, stats_ref,
+    info_ref, qg_ref, a0_ref, a1_ref, a23_ref, b0_ref, b1_ref, b2_ref, b3_ref, lohi_ref, stats_ref,
     dq_ref, own_a_ref, own_b_ref, away_a_ref, away_b_ref,
     tiles_ref, kv_ref, kt_ref, acc_ref, dqt_ref, sums_ref,
 ):
     y_lo, core = info_ref[3], info_ref[4]
     scale = 1.0 / math.sqrt(HD)
     pairs = list_tiles(info_ref, tiles_ref)
-    assemble(y_lo, core, kva_own_ref, kva_other_ref, kv_ref, 0)
-    assemble(y_lo, core, kvb_own_ref, kvb_other_ref, kv_ref, COL * BLK)
+    blocks = (a0_ref, a1_ref, a23_ref.at[0], a23_ref.at[1], b0_ref, b1_ref, b2_ref, b3_ref)
+    assemble(y_lo, core, blocks, kv_ref)
     kt_ref[...] = kv_ref[:, :HD].T
     acc_ref[...] = jnp.zeros_like(acc_ref)
     dqt_ref[...] = jnp.zeros_like(dqt_ref)
@@ -188,7 +197,7 @@
 
     lax.fori_loop(0, pairs, step, 0)
     for n in range(NQ):
-        dq_ref[n ^ core] = (dqt_ref[n] * scale).astype(jnp.bfloat16)
+        dq_ref[n] = (dqt_ref[n] * scale).astype(jnp.bfloat16)
     for i in range(NC):
         for start, own_ref, away_ref in ((0, own_a_ref, away_a_ref), (COL * BLK, own_b_ref, away_b_ref)):
             for y, out_ref in ((y_lo, own_ref), (1 - y_lo, away_ref)):
@@ -198,12 +207,12 @@
 
 
 def finish_kernel(
-    info_ref, own_a_ref, got_a_ref, mate_a_ref, next_ref, dq_ref, grad_q_ref, grad_k_ref, grad_v_ref
+    info_ref, own_a_ref, got_a_ref, mate_a_ref, next_mine_ref, next_other_ref, dq_ref, grad_q_ref, grad_k_ref, grad_v_ref
 ):
     core = info_ref[0]
     f32 = jnp.float32
-    mine = own_a_ref[0] + got_a_ref[0].astype(f32) + next_ref[0].astype(f32)
-    other = mate_a_ref[...].astype(f32) + next_ref[1].astype(f32)
+    mine = own_a_ref[0] + got_a_ref[0].astype(f32) + next_mine_ref[...].astype(f32)
+    other = mate_a_ref[...].astype(f32) + next_other_ref[...].astype(f32)
     for c in range(NC):
 
         @pl.when(core == c)
@@ -227,7 +236,7 @@
     return pl.pallas_call(
         stats_kernel,
         out_shape=jax.ShapeDtypeStruct((NX, NQ, 2, BLK), jnp.float32),
-        in_specs=[SMEM] + [VMEM] * 6,
+        in_specs=[SMEM] + [VMEM] * 9,
         out_specs=VMEM,
         scratch_shapes=[
             pltpu.SMEM((3, NQ * COL + UNROLL), jnp.int32),
@@ -251,7 +260,7 @@
             jax.ShapeDtypeStruct(part, jnp.bfloat16),
             jax.ShapeDtypeStruct(part, jnp.bfloat16),
         ),
-        in_specs=[SMEM] + [VMEM] * 7,
+        in_specs=[SMEM] + [VMEM] * 10,
         out_specs=(VMEM,) * 5,
         scratch_shapes=[
             pltpu.SMEM((3, NQ * COL + UNROLL), jnp.int32),
@@ -274,30 +283,34 @@
 
     bf16 = jnp.bfloat16
     me = core[None]
-    give, kv_mine, qg_mine = pl.pallas_call(
+    big = pltpu.CompilerParams(vmem_limit_bytes=60 * 1024 * 1024)
+    mine, give = pl.pallas_call(
+        split_kernel,
+        out_shape=(jax.ShapeDtypeStruct((BLK, 2 * HD), bf16),) * 2,
+        in_specs=[SMEM] + [VMEM] * 2,
+        out_specs=(VMEM,) * 2,
+        compiler_params=big,
+        cost_estimate=pl.CostEstimate(flops=0, bytes_accessed=1 << 19, transcendentals=0),
+        name="split",
+    )(me, keys, values)
+    qg = pl.pallas_call(
         pack_kernel,
-        out_shape=(
-            jax.ShapeDtypeStruct((BLK, 4 * HD), bf16),
-            jax.ShapeDtypeStruct((BLK, 2 * HD), bf16),
-            jax.ShapeDtypeStruct((BLK, 2 * HD), bf16),
-        ),
-        in_specs=[SMEM] + [VMEM] * 4,
-        out_specs=(VMEM,) * 3,
-        compiler_params=pltpu.CompilerParams(vmem_limit_bytes=60 * 1024 * 1024),
+        out_shape=jax.ShapeDtypeStruct((NQ, BLK, 2 * HD), bf16),
+        in_specs=[VMEM] * 2,
+        out_specs=VMEM,
+        compiler_params=big,
         cost_estimate=pl.CostEstimate(flops=0, bytes_accessed=1 << 20, transcendentals=0),
         name="pack",
-    )(me, queries, keys, values, grad_out)
-    got = partner(give, 1)
-
-    kva = jnp.stack([kv_mine, got[:, : 2 * HD]])
-    kvb = row_step(kva, 1)
-    kva, got = lax.optimization_barrier((kva, got))
-    qg = jnp.broadcast_to(jnp.stack([qg_mine, got[:, 2 * HD :]])[None], (NX, NC, BLK, 2 * HD))
-    qg, group_lengths = lax.optimization_barrier((qg, group_lengths))
-    qg = exchange(qg, X_GROUPS).reshape(NQ, BLK, 2 * HD)
-    kv = [kva, partner(kva, 2), kvb, partner(kvb, 2)]
-
-    low, high = key_ranges(group_lengths, row, y_lo, core)
+    )(queries, grad_out)
+
+    b0, b1 = row_step(mine, 1), row_step(give, 1, 1)
+    a1 = partner(give, 1)
+    qg = exchange(qg, XC_GROUPS)
+    a23 = partner(jnp.stack([mine, a1]), 2)
+    b3, group_lengths = lax.optimization_barrier((partner(b1, 2), group_lengths))
+    kv = [mine, a1, a23, b0, b1, partner(b0, 2), b3]
+
+    low, high = key_ranges(group_lengths, row, y_lo)
     lohi = jnp.stack([low, high], axis=1)
     base_a = (row * ROW + x * COL) * BLK
     base_b = base_a - ROW * BLK
@@ -313,21 +326,22 @@
 
     got_b = partner(away_b, 2)
     dq = exchange(dq, XC_GROUPS)
-    sum_b = (own_b + got_b.astype(jnp.float32)).astype(bf16)
-    sum_b, away_a = lax.optimization_barrier((sum_b, away_a))
+    mine_b, other_b = [(own_b[i] + got_b[i].astype(jnp.float32)).astype(bf16) for i in range(NC)]
+    mine_b, other_b, away_a = lax.optimization_barrier((mine_b, other_b, away_a))
+    next_mine = row_step(mine_b, -1)
+    other_b, dq = lax.optimization_barrier((other_b, dq))
+    next_other = row_step(other_b, -1, 1)
     got_a = partner(away_a, 2)
-    mate_b, dq = lax.optimization_barrier((partner(sum_b[1], 1), dq))
-    from_next = row_step(jnp.stack([sum_b[0], mate_b]), -1)
     mate_a = partner((own_a[1] + got_a[1].astype(jnp.float32)).astype(bf16), 1)
     return pl.pallas_call(
         finish_kernel,
         out_shape=(jax.ShapeDtypeStruct((BLK, HEADS * HD), bf16),) * 3,
-        in_specs=[SMEM] + [VMEM] * 5,
+        in_specs=[SMEM] + [VMEM] * 6,
         out_specs=(VMEM,) * 3,
         compiler_params=PARAMS,
         cost_estimate=pl.CostEstimate(flops=0, bytes_accessed=2 << 20, transcendentals=0),
         name="finish",
-    )(me, own_a, got_a, mate_a, from_next, dq)
+    )(me, own_a, got_a, mate_a, next_mine, next_other, dq)
 
 
 def solution(mesh):

time: 96 us -> 90.8 us (0.946)
  the two profiles are of different devices: /device:TPU:248 before, /device:TPU:249 now
where the time goes in v3:
time: 90.8 us; the launch traced here: 90.1 us
  starting transfers between devices  45.2 us (50%)
  waiting for transfers between devices  18.5 us (20%)
  Pallas kernels  13.8 us (15%)
  blocking collectives  8.26 us (9%)
  other arithmetic  2.94 us (3%)
    ppermute x7, starting transfers between devices, partner(): return lax.ppermute(value, 'inner', [(i ^ flip, i) for i in range(ROW)])  19.9 us
    ppermute x4, starting transfers between devices, row_step(): return lax.ppermute(value, ('outer', 'inner'), route)  14.3 us
    all_to_all x2, starting transfers between devices, exchange(): lax.all_to_all(value, 'inner', 0, 0, axis_index_groups=groups, tiled=True)  11 us
    ppermute x4, waiting for transfers between devices, row_step(): return lax.ppermute(value, ('outer', 'inner'), route)  9.89 us
    all_to_all x1, blocking collectives, exchange(): lax.all_to_all(value, 'inner', 0, 0, axis_index_groups=groups, tiled=True)  8.26 us
    pallas_call x1, Pallas kernels, grads_call(): pl.pallas_call(grads_kernel, out_shape=(jax.ShapeDtypeStruct((NQ, HD, BLK...  5.71 us
    ppermute x7, waiting for transfers between devices, partner(): return lax.ppermute(value, 'inner', [(i ^ flip, i) for i in range(ROW)])  4.76 us
    all_to_all x2, waiting for transfers between devices, exchange(): lax.all_to_all(value, 'inner', 0, 0, axis_index_groups=groups, tiled=True)  3.86 us
  transfers between devices with their start and end apart: 13, of which 4 were waited for; matrix products, arithmetic and copies ran while one was open for 4% of the time, Pallas kernels for 2%

profile of v3, /device:TPU:249, one launch (start us, length us, event | category | flops | bytes accessed | tf_op | source)
XLA Modules:
  0.0 90.1 jit_solution(154335451148836931)
XLA Ops:
  0.6 1.7 %split.1 = (bf16[256,256]{1,0:T(8,128)(2,1)}, bf16[256,256]{1,0:T(8,128)(2,1)}) custom-call(s32[1]{0:T(128)} %bitcast.info_ref, bf16[256,256]{1,0:T(8,128)(2,1)} %k_ref.1, bf16[256,256]{1,0:T(8,128)(2,1)} %v_ref.1), custom_call_target="tpu_custom_call" | custom-call | bytes 524288 | tf_op jit(solution)/shard_map/split/pallas_call | solution.py:287
  2.4 2.6 %collective-permute-start.2 = (bf16[256,256]{1,0:T(8,128)(2,1)}, bf16[256,256]{1,0:T(8,128)(2,1)S(1)}, u32[]{:S(2)}, u32[]{:S(2)}) collective-permute-start(bf16[256,256]{1,0:T(8,128)(2,1)} %get-tuple-element.17), channel_id=1, source_target_pairs={{1,0},{0,1},{3,2},{2,3},{5,4},{4,5},{7,6},{6,7},{9,8},{8,9},{11,10... | collective-permute-start | bytes 393224 | tf_op jit(solution)/shard_map/ppermute | solution.py:39
  4.9 5.3 %collective-permute-start = (bf16[256,256]{1,0:T(8,128)(2,1)}, bf16[256,256]{1,0:T(8,128)(2,1)S(1)}, u32[]{:S(2)}, u32[]{:S(2)}) collective-permute-start(bf16[256,256]{1,0:T(8,128)(2,1)} %get-tuple-element.17), channel_id=1, source_target_pairs={{0,17},{1,16},{2,19},{3,18},{4,21},{5,20},{6,23},{7,22},{8,25},{9,... | collective-permute-start | bytes 393224 | tf_op jit(solution)/shard_map/ppermute | solution.py:35
  10.3 4.2 %collective-permute-start.4 = (bf16[256,256]{1,0:T(8,128)(2,1)}, bf16[256,256]{1,0:T(8,128)(2,1)S(1)}, u32[]{:S(2)}, u32[]{:S(2)}) collective-permute-start(bf16[256,256]{1,0:T(8,128)(2,1)} %get-tuple-element.19.a0_ref), channel_id=1, source_target_pairs={{0,16},{1,17},{2,18},{3,19},{4,20},{5,21},{6,22},{7,23},{8,24},{9,... | collective-permute-start | bytes 393224 | tf_op jit(solution)/shard_map/ppermute | solution.py:35
  14.5 2.1 %pack.1 = bf16[8,256,256]{2,1,0:T(8,128)(2,1)} custom-call(bf16[256,256]{1,0:T(8,128)(2,1)} %q_ref.1, bf16[256,256]{1,0:T(8,128)(2,1)} %g_ref.1), custom_call_target="tpu_custom_call" | custom-call | bytes 1048576 | tf_op jit(solution)/shard_map/pack/pallas_call | solution.py:296
  16.6 5.2 %all-to-all-start = ((bf16[8,256,256]{2,1,0:T(8,128)(2,1)}), bf16[8,256,256]{2,1,0:T(8,128)(2,1)S(1)}, u32[]{:S(2)}, u32[]{:S(2)}) async-start(bf16[8,256,256]{2,1,0:T(8,128)(2,1)} %pack.1), calls=%async_computation | async-start | bytes 2097152 | tf_op jit(solution)/shard_map/all_to_all | solution.py:28
  21.8 0.1 add_multiply_fusion
  21.9 0.1 mul.44
  22.0 0.1 iota_add_fusion
  22.0 0.0 collective-permute-done.b1_ref
  22.0 2.1 %collective-permute-start.1 = (bf16[256,256]{1,0:T(8,128)(2,1)S(1)}, bf16[256,256]{1,0:T(8,128)(2,1)S(1)}, u32[]{:S(2)}, u32[]{:S(2)}) collective-permute-start(bf16[256,256]{1,0:T(8,128)(2,1)S(1)} %collective-permute-done.b1_ref), channel_id=1, source_target_pairs={{2,0},{3,1},{0,2},{1,3},{6,4},{7,5},{4,6},{5,7},{10,8},{11,9},{8,1... | collective-permute-start | bytes 393224 | tf_op jit(solution)/shard_map/ppermute | solution.py:39
  24.1 0.0 collective-permute-done.2.a1_ref
  24.2 3.2 %collective-permute-start.3 = (bf16[2,256,256]{2,1,0:T(8,128)(2,1)S(1)}, bf16[2,256,256]{2,1,0:T(8,128)(2,1)S(1)}, u32[]{:S(2)}, u32[]{:S(2)}) collective-permute-start(bf16[2,256,256]{2,1,0:T(8,128)(2,1)S(1)} %pad_maximum_fusion), channel_id=1, source_target_pairs={{2,0},{3,1},{0,2},{1,3},{6,4},{7,5},{4,6},{5,7},{10,8},{11,9},{8,1... | collective-permute-start | bytes 786440 | tf_op jit(solution)/shard_map/ppermute | solution.py:39
  27.4 0.0 collective-permute-done.4.b0_ref
  27.4 2.1 %collective-permute-start.5 = (bf16[256,256]{1,0:T(8,128)(2,1)S(1)}, bf16[256,256]{1,0:T(8,128)(2,1)S(1)}, u32[]{:S(2)}, u32[]{:S(2)}) collective-permute-start(bf16[256,256]{1,0:T(8,128)(2,1)S(1)} %collective-permute-done.4.b0_ref), channel_id=1, source_target_pairs={{2,0},{3,1},{0,2},{1,3},{6,4},{7,5},{4,6},{5,7},{10,8},{11,9},{8,1... | collective-permute-start | bytes 393224 | tf_op jit(solution)/shard_map/ppermute | solution.py:39
  29.5 0.0 collective-permute-done.1.b3_ref
  29.5 0.3 reduce-window.9
  29.8 0.1 slice.37
  29.9 0.1 slice_reduce_fusion.1
  30.1 0.1 fusion.7
  30.1 0.1 broadcast_add_fusion
  30.2 0.1 fusion.6
  30.3 1.1 %select_reduce_fusion.1 = s32[8,256]{1,0:T(8,128)S(1)} fusion(s32[254]{0:T(256)S(1)} %bitcast.23, s32[8,256]{1,0:T(8,128)S(1)} %iota_add_fusion, s32[254]{0:T(256)S(1)} %bitcast.22), kind=kLoop, calls=%fused_computation.1 | loop fusion | flops 1558528 | bytes 18416 | tf_op jit(solution)/shard_map/reduce_max | solution.py:51
  31.3 0.1 slice_reduce_fusion
  31.5 0.8 select_reduce_fusion
  32.3 0.2 fusion.3
  32.5 0.1 reshape_minimum_fusion
  32.6 0.1 concatenate.3.info_ref
  32.7 4.7 %collective-permute-done.5.b2_ref = bf16[256,256]{1,0:T(8,128)(2,1)S(1)} collective-permute-done((bf16[256,256]{1,0:T(8,128)(2,1)S(1)}, bf16[256,256]{1,0:T(8,128)(2,1)S(1)}, u32[]{:S(2)}, u32[]{:S(2)}) %collective-permute-start.5) | collective-permute-done | bytes 131104 | tf_op jit(solution)/shard_map/ppermute | solution.py:39
  37.5 0.0 collective-permute-done.3.a23_ref
  37.5 0.0 all-to-all-done.qg_ref
  37.5 3.4 %stats.1 = f32[4,8,2,256]{3,2,1,0:T(2,128)S(1)} custom-call(s32[24]{0:T(128)S(1)} %concatenate.3.info_ref, bf16[8,256,256]{2,1,0:T(8,128)(2,1)S(1)} %all-to-all-done.qg_ref, bf16[256,256]{1,0:T(8,128)(2,1)S(1)} %copy-done, bf16[256,256]{1,0:T(8,128)(2,1)S(1)} %collective-permute-done.2.a1_ref, bf16[2,256,256]{2,1,0:T(8,128)(2,1)S(1)} %collective-permute-done.3.a23_ref, ...), custom_call_target="tpu_custom_call" | custom-call | flops 536870912 | bytes 2097152 | tf_op jit(solution)/shard_map/stats/pallas_call | solution.py:236
  40.8 8.3 %all_to_all.15.stats_ref = f32[4,8,2,256]{3,2,1,0:T(2,128)S(1)} all-to-all(f32[4,8,2,256]{3,2,1,0:T(2,128)S(1)} %stats.1), channel_id=1, replica_groups={{0,4,8,12},{1,5,9,13},{2,6,10,14},{3,7,11,15},{16,20,24,28},{17,21,25,2..., dimensions={0} | all-to-all | bytes 131072 | tf_op jit(solution)/shard_map/all_to_all | solution.py:28
  49.1 5.7 %grads.1 = (bf16[8,128,256]{2,1,0:T(8,128)(2,1)}, f32[2,256,256]{2,1,0:T(8,128)S(1)}, f32[2,256,256]{2,1,0:T(8,128)S(1)}, bf16[2,256,256]{2,1,0:T(8,128)(2,1)S(1)}, bf16[2,256,256]{2,1,0:T(8,128)(2,1)}) custom-call(s32[24]{0:T(128)S(1)} %concatenate.3.info_ref, bf16[8,256,256]{2,1,0:T(8,128)(2,1)S(1)} %all-to-all-done.qg_ref, bf16[256,256]{1,0:T(8,128)(2,1)S(1)} %copy-done, ...), custom_call_target="tpu_custom_call" | custom-call | flops 1342177280 | bytes 4194304 | tf_op jit(solution)/shard_map/grads/pallas_call | solution.py:254
  54.8 1.9 %collective-permute-start.6 = (bf16[2,256,256]{2,1,0:T(8,128)(2,1)}, bf16[2,256,256]{2,1,0:T(8,128)(2,1)S(1)}, u32[]{:S(2)}, u32[]{:S(2)}) collective-permute-start(bf16[2,256,256]{2,1,0:T(8,128)(2,1)} %get-tuple-element.23), channel_id=1, source_target_pairs={{2,0},{3,1},{0,2},{1,3},{6,4},{7,5},{4,6},{5,7},{10,8},{11,9},{8,1... | collective-permute-start | bytes 786440 | tf_op jit(solution)/shard_map/ppermute | solution.py:39
  56.7 5.8 %all-to-all-start.2 = ((bf16[8,128,256]{2,1,0:T(8,128)(2,1)}), bf16[8,128,256]{2,1,0:T(8,128)(2,1)S(1)}, u32[]{:S(2)}, u32[]{:S(2)}) async-start(bf16[8,128,256]{2,1,0:T(8,128)(2,1)} %get-tuple-element.28), calls=%async_computation.2 | async-start | bytes 1048576 | tf_op jit(solution)/shard_map/all_to_all | solution.py:28
  62.5 0.0 collective-permute-done.6
  62.5 0.1 fusion.1
  62.6 3.6 %collective-permute-start.7 = (bf16[2,256,256]{2,1,0:T(8,128)(2,1)S(1)}, bf16[2,256,256]{2,1,0:T(8,128)(2,1)S(1)}, u32[]{:S(2)}, u32[]{:S(2)}) collective-permute-start(bf16[2,256,256]{2,1,0:T(8,128)(2,1)S(1)} %get-tuple-element.25), channel_id=1, source_target_pairs={{2,0},{3,1},{0,2},{1,3},{6,4},{7,5},{4,6},{5,7},{10,8},{11,9},{8,1... | collective-permute-start | bytes 786440 | tf_op jit(solution)/shard_map/ppermute | solution.py:39
  66.3 1.9 %collective-permute-start.9 = (bf16[256,256]{1,0:T(8,128)(2,1)S(1)}, bf16[256,256]{1,0:T(8,128)(2,1)S(1)}, u32[]{:S(2)}, u32[]{:S(2)}) collective-permute-start(bf16[256,256]{1,0:T(8,128)(2,1)S(1)} %get-tuple-element.26), channel_id=1, source_target_pairs={{16,0},{17,1},{18,2},{19,3},{20,4},{21,5},{22,6},{23,7},{24,8},{25... | collective-permute-start | bytes 393224 | tf_op jit(solution)/shard_map/ppermute | solution.py:35
  68.2 3.9 %all-to-all-done.2.dq_ref = bf16[8,128,256]{2,1,0:T(8,128)(2,1)S(1)} async-done(((bf16[8,128,256]{2,1,0:T(8,128)(2,1)}), bf16[8,128,256]{2,1,0:T(8,128)(2,1)S(1)}, u32[]{:S(2)}, u32[]{:S(2)}) %all-to-all-start.2) | async-done | bytes 524320 | tf_op jit(solution)/shard_map/all_to_all | solution.py:28
  72.0 2.8 %collective-permute-start.10 = (bf16[256,256]{1,0:T(8,128)(2,1)S(1)}, bf16[256,256]{1,0:T(8,128)(2,1)S(1)}, u32[]{:S(2)}, u32[]{:S(2)}) collective-permute-start(bf16[256,256]{1,0:T(8,128)(2,1)S(1)} %get-tuple-element.29), channel_id=1, source_target_pairs={{16,1},{17,0},{18,3},{19,2},{20,5},{21,4},{22,7},{23,6},{24,9},{25... | collective-permute-start | bytes 393224 | tf_op jit(solution)/shard_map/ppermute | solution.py:35
  74.8 0.0 collective-permute-done.7.got_a_ref
  74.9 4.4 %collective-permute-start.8 = (bf16[256,256]{1,0:T(8,128)(2,1)S(1)}, bf16[256,256]{1,0:T(8,128)(2,1)S(1)}, u32[]{:S(2)}, u32[]{:S(2)}) collective-permute-start(bf16[256,256]{1,0:T(8,128)(2,1)S(1)} %fusion.2), channel_id=1, source_target_pairs={{1,0},{0,1},{3,2},{2,3},{5,4},{4,5},{7,6},{6,7},{9,8},{8,9},{11,10... | collective-permute-start | bytes 393224 | tf_op jit(solution)/shard_map/ppermute | solution.py:39
  79.3 0.4 collective-permute-done.9.next_mine_ref
  79.8 9.4 %collective-permute-done.10.next_other_ref = bf16[256,256]{1,0:T(8,128)(2,1)S(1)} collective-permute-done((bf16[256,256]{1,0:T(8,128)(2,1)S(1)}, bf16[256,256]{1,0:T(8,128)(2,1)S(1)}, u32[]{:S(2)}, u32[]{:S(2)}) %collective-permute-start.10) | collective-permute-done | bytes 131104 | tf_op jit(solution)/shard_map/ppermute | solution.py:35
  89.2 0.0 collective-permute-done.8.mate_a_ref
  89.2 0.9 %finish.1 = (bf16[256,256]{1,0:T(8,128)(2,1)}, bf16[256,256]{1,0:T(8,128)(2,1)}, bf16[256,256]{1,0:T(8,128)(2,1)}) custom-call(s32[1]{0:T(128)} %bitcast.info_ref, f32[2,256,256]{2,1,0:T(8,128)S(1)} %get-tuple-element.21.own_a_ref, bf16[2,256,256]{2,1,0:T(8,128)(2,1)S(1)} %collective-permute-done.7.got_a_ref, ...), custom_call_target="tpu_custom_call" | custom-call | bytes 2097152 | tf_op jit(solution)/shard_map/finish/pallas_call | solution.py:336
  (12 shorter events, 0.2 us)
Async XLA Ops:
  2.4 21.8 %collective-permute-start.2 = (bf16[256,256]{1,0:T(8,128)(2,1)}, bf16[256,256]{1,0:T(8,128)(2,1)S(1)}, u32[]{:S(2)}, u32[]{:S(2)}) collective-permute-start(bf16[256,256]{1,0:T(8,128)(2,1)} %get-tuple-element.17), channel_id=1, source_target_pairs={{1,0},{0,1},{3,2},{2,3},{5,4},{4,5},{7,6},{6,7},{9,8},{8,9},{11,10... | collective-permute-start | bytes 393224 | tf_op jit(solution)/shard_map/ppermute | solution.py:39
  4.9 17.1 %collective-permute-start = (bf16[256,256]{1,0:T(8,128)(2,1)}, bf16[256,256]{1,0:T(8,128)(2,1)S(1)}, u32[]{:S(2)}, u32[]{:S(2)}) collective-permute-start(bf16[256,256]{1,0:T(8,128)(2,1)} %get-tuple-element.17), channel_id=1, source_target_pairs={{0,17},{1,16},{2,19},{3,18},{4,21},{5,20},{6,23},{7,22},{8,25},{9,... | collective-permute-start | bytes 393224 | tf_op jit(solution)/shard_map/ppermute | solution.py:35
  10.3 17.1 %collective-permute-start.4 = (bf16[256,256]{1,0:T(8,128)(2,1)}, bf16[256,256]{1,0:T(8,128)(2,1)S(1)}, u32[]{:S(2)}, u32[]{:S(2)}) collective-permute-start(bf16[256,256]{1,0:T(8,128)(2,1)} %get-tuple-element.19.a0_ref), channel_id=1, source_target_pairs={{0,16},{1,17},{2,18},{3,19},{4,20},{5,21},{6,22},{7,23},{8,24},{9,... | collective-permute-start | bytes 393224 | tf_op jit(solution)/shard_map/ppermute | solution.py:35
  16.6 7.6 %copy-start = (bf16[256,256]{1,0:T(8,128)(2,1)S(1)}, bf16[256,256]{1,0:T(8,128)(2,1)}, u32[]{:S(2)}) copy-start(bf16[256,256]{1,0:T(8,128)(2,1)} %get-tuple-element.19.a0_ref) | copy-start | bytes 393220
  16.6 12.9 %copy-start.1 = (s32[256]{0:T(256)S(1)}, s32[256]{0:T(256)}, u32[]{:S(2)}) copy-start(s32[256]{0:T(256)} %param.9) | copy-start | bytes 3076
  16.6 20.9 %all-to-all-start = ((bf16[8,256,256]{2,1,0:T(8,128)(2,1)}), bf16[8,256,256]{2,1,0:T(8,128)(2,1)S(1)}, u32[]{:S(2)}, u32[]{:S(2)}) async-start(bf16[8,256,256]{2,1,0:T(8,128)(2,1)} %pack.1), calls=%async_computation | async-start | bytes 2097152 | tf_op jit(solution)/shard_map/all_to_all | solution.py:28
  22.0 7.5 %collective-permute-start.1 = (bf16[256,256]{1,0:T(8,128)(2,1)S(1)}, bf16[256,256]{1,0:T(8,128)(2,1)S(1)}, u32[]{:S(2)}, u32[]{:S(2)}) collective-permute-start(bf16[256,256]{1,0:T(8,128)(2,1)S(1)} %collective-permute-done.b1_ref), channel_id=1, source_target_pairs={{2,0},{3,1},{0,2},{1,3},{6,4},{7,5},{4,6},{5,7},{10,8},{11,9},{8,1... | collective-permute-start | bytes 393224 | tf_op jit(solution)/shard_map/ppermute | solution.py:39
  24.2 13.3 %collective-permute-start.3 = (bf16[2,256,256]{2,1,0:T(8,128)(2,1)S(1)}, bf16[2,256,256]{2,1,0:T(8,128)(2,1)S(1)}, u32[]{:S(2)}, u32[]{:S(2)}) collective-permute-start(bf16[2,256,256]{2,1,0:T(8,128)(2,1)S(1)} %pad_maximum_fusion), channel_id=1, source_target_pairs={{2,0},{3,1},{0,2},{1,3},{6,4},{7,5},{4,6},{5,7},{10,8},{11,9},{8,1... | collective-permute-start | bytes 786440 | tf_op jit(solution)/shard_map/ppermute | solution.py:39
  27.4 10.1 %collective-permute-start.5 = (bf16[256,256]{1,0:T(8,128)(2,1)S(1)}, bf16[256,256]{1,0:T(8,128)(2,1)S(1)}, u32[]{:S(2)}, u32[]{:S(2)}) collective-permute-start(bf16[256,256]{1,0:T(8,128)(2,1)S(1)} %collective-permute-done.4.b0_ref), channel_id=1, source_target_pairs={{2,0},{3,1},{0,2},{1,3},{6,4},{7,5},{4,6},{5,7},{10,8},{11,9},{8,1... | collective-permute-start | bytes 393224 | tf_op jit(solution)/shard_map/ppermute | solution.py:39
  54.8 7.7 %collective-permute-start.6 = (bf16[2,256,256]{2,1,0:T(8,128)(2,1)}, bf16[2,256,256]{2,1,0:T(8,128)(2,1)S(1)}, u32[]{:S(2)}, u32[]{:S(2)}) collective-permute-start(bf16[2,256,256]{2,1,0:T(8,128)(2,1)} %get-tuple-element.23), channel_id=1, source_target_pairs={{2,0},{3,1},{0,2},{1,3},{6,4},{7,5},{4,6},{5,7},{10,8},{11,9},{8,1... | collective-permute-start | bytes 786440 | tf_op jit(solution)/shard_map/ppermute | solution.py:39
  56.7 15.3 %all-to-all-start.2 = ((bf16[8,128,256]{2,1,0:T(8,128)(2,1)}), bf16[8,128,256]{2,1,0:T(8,128)(2,1)S(1)}, u32[]{:S(2)}, u32[]{:S(2)}) async-start(bf16[8,128,256]{2,1,0:T(8,128)(2,1)} %get-tuple-element.28), calls=%async_computation.2 | async-start | bytes 1048576 | tf_op jit(solution)/shard_map/all_to_all | solution.py:28
  62.6 12.2 %collective-permute-start.7 = (bf16[2,256,256]{2,1,0:T(8,128)(2,1)S(1)}, bf16[2,256,256]{2,1,0:T(8,128)(2,1)S(1)}, u32[]{:S(2)}, u32[]{:S(2)}) collective-permute-start(bf16[2,256,256]{2,1,0:T(8,128)(2,1)S(1)} %get-tuple-element.25), channel_id=1, source_target_pairs={{2,0},{3,1},{0,2},{1,3},{6,4},{7,5},{4,6},{5,7},{10,8},{11,9},{8,1... | collective-permute-start | bytes 786440 | tf_op jit(solution)/shard_map/ppermute | solution.py:39
  66.3 13.5 %collective-permute-start.9 = (bf16[256,256]{1,0:T(8,128)(2,1)S(1)}, bf16[256,256]{1,0:T(8,128)(2,1)S(1)}, u32[]{:S(2)}, u32[]{:S(2)}) collective-permute-start(bf16[256,256]{1,0:T(8,128)(2,1)S(1)} %get-tuple-element.26), channel_id=1, source_target_pairs={{16,0},{17,1},{18,2},{19,3},{20,4},{21,5},{22,6},{23,7},{24,8},{25... | collective-permute-start | bytes 393224 | tf_op jit(solution)/shard_map/ppermute | solution.py:35
  72.0 17.2 %collective-permute-start.10 = (bf16[256,256]{1,0:T(8,128)(2,1)S(1)}, bf16[256,256]{1,0:T(8,128)(2,1)S(1)}, u32[]{:S(2)}, u32[]{:S(2)}) collective-permute-start(bf16[256,256]{1,0:T(8,128)(2,1)S(1)} %get-tuple-element.29), channel_id=1, source_target_pairs={{16,1},{17,0},{18,3},{19,2},{20,5},{21,4},{22,7},{23,6},{24,9},{25... | collective-permute-start | bytes 393224 | tf_op jit(solution)/shard_map/ppermute | solution.py:35
  74.9 14.3 %collective-permute-start.8 = (bf16[256,256]{1,0:T(8,128)(2,1)S(1)}, bf16[256,256]{1,0:T(8,128)(2,1)S(1)}, u32[]{:S(2)}, u32[]{:S(2)}) collective-permute-start(bf16[256,256]{1,0:T(8,128)(2,1)S(1)} %fusion.2), channel_id=1, source_target_pairs={{1,0},{0,1},{3,2},{2,3},{5,4},{4,5},{7,6},{6,7},{9,8},{8,9},{11,10... | collective-permute-start | bytes 393224 | tf_op jit(solution)/shard_map/ppermute | solution.py:39

commit v4 on v3

--- a/solution.py
+++ b/solution.py
@@ -293,6 +293,9 @@
         cost_estimate=pl.CostEstimate(flops=0, bytes_accessed=1 << 19, transcendentals=0),
         name="split",
     )(me, keys, values)
+    b0, b1 = row_step(mine, 1), row_step(give, 1, 1)
+    a1 = partner(give, 1)
+    to_a, queries = lax.optimization_barrier((jnp.stack([mine, a1]), queries))
     qg = pl.pallas_call(
         pack_kernel,
         out_shape=jax.ShapeDtypeStruct((NQ, BLK, 2 * HD), bf16),
@@ -302,13 +305,9 @@
         cost_estimate=pl.CostEstimate(flops=0, bytes_accessed=1 << 20, transcendentals=0),
         name="pack",
     )(queries, grad_out)
-
-    b0, b1 = row_step(mine, 1), row_step(give, 1, 1)
-    a1 = partner(give, 1)
     qg = exchange(qg, XC_GROUPS)
-    a23 = partner(jnp.stack([mine, a1]), 2)
-    b3, group_lengths = lax.optimization_barrier((partner(b1, 2), group_lengths))
-    kv = [mine, a1, a23, b0, b1, partner(b0, 2), b3]
+    a23, group_lengths = lax.optimization_barrier((partner(to_a, 2), group_lengths))
+    kv = [mine, a1, a23, b0, b1, partner(b0, 2), partner(b1, 2)]
 
     low, high = key_ranges(group_lengths, row, y_lo)
     lohi = jnp.stack([low, high], axis=1)

time: 90.8 us -> 91.1 us (level)
  the two profiles are of different devices: /device:TPU:249 before, /device:TPU:251 now
where the time goes in v4:
time: 91.1 us; the launch traced here: 90.5 us
  starting transfers between devices  45.1 us (50%)
  waiting for transfers between devices  19 us (21%)
  Pallas kernels  15.3 us (17%)
  blocking collectives  5.83 us (6%)
  other arithmetic  3.84 us (4%)
    ppermute x7, starting transfers between devices, partner(): return lax.ppermute(value, 'inner', [(i ^ flip, i) for i in range(ROW)])  16.8 us
    ppermute x4, starting transfers between devices, row_step(): return lax.ppermute(value, ('outer', 'inner'), route)  16 us
    all_to_all x2, starting transfers between devices, exchange(): lax.all_to_all(value, 'inner', 0, 0, axis_index_groups=groups, tiled=True)  12.3 us
    ppermute x4, waiting for transfers between devices, row_step(): return lax.ppermute(value, ('outer', 'inner'), route)  9.69 us
    all_to_all x2, waiting for transfers between devices, exchange(): lax.all_to_all(value, 'inner', 0, 0, axis_index_groups=groups, tiled=True)  8.29 us
    pallas_call x1, Pallas kernels, grads_call(): pl.pallas_call(grads_kernel, out_shape=(jax.ShapeDtypeStruct((NQ, HD, BLK...  6.6 us
    all_to_all x1, blocking collectives, exchange(): lax.all_to_all(value, 'inner', 0, 0, axis_index_groups=groups, tiled=True)  5.83 us
    pallas_call x1, Pallas kernels, stats_call(): pl.pallas_call(stats_kernel, out_shape=jax.ShapeDtypeStruct((NX, NQ, 2, B...  4.01 us
  transfers between devices with their start and end apart: 13, of which 5 were waited for; matrix products, arithmetic and copies ran while one was open for 5% of the time, Pallas kernels for 2%

profile of v4, /device:TPU:251, one launch (start us, length us, event | category | flops | bytes accessed | tf_op | source)
XLA Modules:
  0.0 90.5 jit_solution(5804011560468185344)
XLA Ops:
  0.6 1.7 %split.1 = (bf16[256,256]{1,0:T(8,128)(2,1)}, bf16[256,256]{1,0:T(8,128)(2,1)}) custom-call(s32[1]{0:T(128)} %bitcast.info_ref, bf16[256,256]{1,0:T(8,128)(2,1)} %k_ref.1, bf16[256,256]{1,0:T(8,128)(2,1)} %v_ref.1), custom_call_target="tpu_custom_call" | custom-call | bytes 524288 | tf_op jit(solution)/shard_map/split/pallas_call | solution.py:287
  2.4 6.0 %collective-permute-start.3 = (bf16[256,256]{1,0:T(8,128)(2,1)}, bf16[256,256]{1,0:T(8,128)(2,1)S(1)}, u32[]{:S(2)}, u32[]{:S(2)}) collective-permute-start(bf16[256,256]{1,0:T(8,128)(2,1)} %get-tuple-element.20), channel_id=1, source_target_pairs={{0,17},{1,16},{2,19},{3,18},{4,21},{5,20},{6,23},{7,22},{8,25},{9,... | collective-permute-start | bytes 393224 | tf_op jit(solution)/shard_map/ppermute | solution.py:35
  8.3 1.9 %collective-permute-start = (bf16[256,256]{1,0:T(8,128)(2,1)}, bf16[256,256]{1,0:T(8,128)(2,1)S(1)}, u32[]{:S(2)}, u32[]{:S(2)}) collective-permute-start(bf16[256,256]{1,0:T(8,128)(2,1)} %get-tuple-element.20), channel_id=1, source_target_pairs={{1,0},{0,1},{3,2},{2,3},{5,4},{4,5},{7,6},{6,7},{9,8},{8,9},{11,10... | collective-permute-start | bytes 393224 | tf_op jit(solution)/shard_map/ppermute | solution.py:39
  10.3 4.2 %collective-permute-start.2 = (bf16[256,256]{1,0:T(8,128)(2,1)}, bf16[256,256]{1,0:T(8,128)(2,1)S(1)}, u32[]{:S(2)}, u32[]{:S(2)}) collective-permute-start(bf16[256,256]{1,0:T(8,128)(2,1)} %get-tuple-element.19.a0_ref), channel_id=1, source_target_pairs={{0,16},{1,17},{2,18},{3,19},{4,20},{5,21},{6,22},{7,23},{8,24},{9,... | collective-permute-start | bytes 393224 | tf_op jit(solution)/shard_map/ppermute | solution.py:35
  14.5 0.1 add_multiply_fusion
  14.6 0.1 mul.44
  14.7 0.0 collective-permute-done.a1_ref
  14.7 0.9 %pad_maximum_fusion = bf16[2,256,256]{2,1,0:T(8,128)(2,1)S(1)} fusion(bf16[1,256,256]{2,1,0:T(8,128)(2,1)S(1)} %bitcast.20, bf16[1,256,256]{2,1,0:T(8,128)(2,1)} %bitcast.19), kind=kLoop, calls=%fused_computation.2 | loop fusion | flops 131072 | bytes 524288 | tf_op jit(solution)/shard_map/stack | solution.py:298
  15.6 2.1 %collective-permute-start.1 = (bf16[2,256,256]{2,1,0:T(8,128)(2,1)S(1)}, bf16[2,256,256]{2,1,0:T(8,128)(2,1)S(1)}, u32[]{:S(2)}, u32[]{:S(2)}) collective-permute-start(bf16[2,256,256]{2,1,0:T(8,128)(2,1)S(1)} %pad_maximum_fusion), channel_id=1, source_target_pairs={{2,0},{3,1},{0,2},{1,3},{6,4},{7,5},{4,6},{5,7},{10,8},{11,9},{8,1... | collective-permute-start | bytes 786440 | tf_op jit(solution)/shard_map/ppermute | solution.py:39
  17.7 0.1 iota_add_fusion
  17.8 2.1 %pack.1 = bf16[8,256,256]{2,1,0:T(8,128)(2,1)} custom-call(bf16[256,256]{1,0:T(8,128)(2,1)} %q_ref, bf16[256,256]{1,0:T(8,128)(2,1)} %g_ref.1), custom_call_target="tpu_custom_call" | custom-call | bytes 1048576 | tf_op jit(solution)/shard_map/pack/pallas_call | solution.py:299
  19.9 5.7 %all-to-all-start = ((bf16[8,256,256]{2,1,0:T(8,128)(2,1)}), bf16[8,256,256]{2,1,0:T(8,128)(2,1)S(1)}, u32[]{:S(2)}, u32[]{:S(2)}) async-start(bf16[8,256,256]{2,1,0:T(8,128)(2,1)} %pack.1), calls=%async_computation | async-start | bytes 2097152 | tf_op jit(solution)/shard_map/all_to_all | solution.py:28
  25.5 0.0 collective-permute-done.3.b1_ref
  25.5 3.2 %collective-permute-start.5 = (bf16[256,256]{1,0:T(8,128)(2,1)S(1)}, bf16[256,256]{1,0:T(8,128)(2,1)S(1)}, u32[]{:S(2)}, u32[]{:S(2)}) collective-permute-start(bf16[256,256]{1,0:T(8,128)(2,1)S(1)} %collective-permute-done.3.b1_ref), channel_id=1, source_target_pairs={{2,0},{3,1},{0,2},{1,3},{6,4},{7,5},{4,6},{5,7},{10,8},{11,9},{8,1... | collective-permute-start | bytes 393224 | tf_op jit(solution)/shard_map/ppermute | solution.py:39
  28.8 0.0 collective-permute-done.2.b0_ref
  28.8 2.1 %collective-permute-start.4 = (bf16[256,256]{1,0:T(8,128)(2,1)S(1)}, bf16[256,256]{1,0:T(8,128)(2,1)S(1)}, u32[]{:S(2)}, u32[]{:S(2)}) collective-permute-start(bf16[256,256]{1,0:T(8,128)(2,1)S(1)} %collective-permute-done.2.b0_ref), channel_id=1, source_target_pairs={{2,0},{3,1},{0,2},{1,3},{6,4},{7,5},{4,6},{5,7},{10,8},{11,9},{8,1... | collective-permute-start | bytes 393224 | tf_op jit(solution)/shard_map/ppermute | solution.py:39
  30.8 0.0 collective-permute-done.1.a23_ref
  30.9 0.3 reduce-window.9
  31.2 0.1 slice.37
  31.3 0.1 slice_reduce_fusion.1
  31.4 0.1 fusion.7
  31.5 0.1 broadcast_add_fusion
  31.6 0.1 fusion.6
  31.6 1.1 %select_reduce_fusion.1 = s32[8,256]{1,0:T(8,128)S(1)} fusion(s32[254]{0:T(256)S(1)} %bitcast.23, s32[8,256]{1,0:T(8,128)S(1)} %iota_add_fusion, s32[254]{0:T(256)S(1)} %bitcast.22), kind=kLoop, calls=%fused_computation.1 | loop fusion | flops 1558528 | bytes 18416 | tf_op jit(solution)/shard_map/reduce_max | solution.py:51
  32.7 0.1 slice_reduce_fusion
  32.8 0.8 select_reduce_fusion
  33.6 0.2 fusion.3
  33.8 0.1 reshape_minimum_fusion
  33.9 0.1 concatenate.3.info_ref
  34.1 0.0 collective-permute-done.5.b3_ref
  34.1 1.0 %collective-permute-done.4.b2_ref = bf16[256,256]{1,0:T(8,128)(2,1)S(1)} collective-permute-done((bf16[256,256]{1,0:T(8,128)(2,1)S(1)}, bf16[256,256]{1,0:T(8,128)(2,1)S(1)}, u32[]{:S(2)}, u32[]{:S(2)}) %collective-permute-start.4) | collective-permute-done | bytes 131104 | tf_op jit(solution)/shard_map/ppermute | solution.py:39
  35.1 4.5 %all-to-all-done.qg_ref = bf16[8,256,256]{2,1,0:T(8,128)(2,1)S(1)} async-done(((bf16[8,256,256]{2,1,0:T(8,128)(2,1)}), bf16[8,256,256]{2,1,0:T(8,128)(2,1)S(1)}, u32[]{:S(2)}, u32[]{:S(2)}) %all-to-all-start) | async-done | bytes 1048608 | tf_op jit(solution)/shard_map/all_to_all | solution.py:28
  39.5 4.0 %stats.1 = f32[4,8,2,256]{3,2,1,0:T(2,128)S(1)} custom-call(s32[24]{0:T(128)S(1)} %concatenate.3.info_ref, bf16[8,256,256]{2,1,0:T(8,128)(2,1)S(1)} %all-to-all-done.qg_ref, bf16[256,256]{1,0:T(8,128)(2,1)S(1)} %copy-done, bf16[256,256]{1,0:T(8,128)(2,1)S(1)} %collective-permute-done.a1_ref, bf16[2,256,256]{2,1,0:T(8,128)(2,1)S(1)} %collective-permute-done.1.a23_ref, ...), custom_call_target="tpu_custom_call" | custom-call | flops 536870912 | bytes 2097152 | tf_op jit(solution)/shard_map/stats/pallas_call | solution.py:236
  43.6 5.8 %all_to_all.15.stats_ref = f32[4,8,2,256]{3,2,1,0:T(2,128)S(1)} all-to-all(f32[4,8,2,256]{3,2,1,0:T(2,128)S(1)} %stats.1), channel_id=1, replica_groups={{0,4,8,12},{1,5,9,13},{2,6,10,14},{3,7,11,15},{16,20,24,28},{17,21,25,2..., dimensions={0} | all-to-all | bytes 131072 | tf_op jit(solution)/shard_map/all_to_all | solution.py:28
  49.4 6.6 %grads.1 = (bf16[8,128,256]{2,1,0:T(8,128)(2,1)}, f32[2,256,256]{2,1,0:T(8,128)S(1)}, f32[2,256,256]{2,1,0:T(8,128)S(1)}, bf16[2,256,256]{2,1,0:T(8,128)(2,1)S(1)}, bf16[2,256,256]{2,1,0:T(8,128)(2,1)}) custom-call(s32[24]{0:T(128)S(1)} %concatenate.3.info_ref, bf16[8,256,256]{2,1,0:T(8,128)(2,1)S(1)} %all-to-all-done.qg_ref, bf16[256,256]{1,0:T(8,128)(2,1)S(1)} %copy-done, ...), custom_call_target="tpu_custom_call" | custom-call | flops 1342177280 | bytes 4194304 | tf_op jit(solution)/shard_map/grads/pallas_call | solution.py:254
  56.0 2.4 %collective-permute-start.6 = (bf16[2,256,256]{2,1,0:T(8,128)(2,1)}, bf16[2,256,256]{2,1,0:T(8,128)(2,1)S(1)}, u32[]{:S(2)}, u32[]{:S(2)}) collective-permute-start(bf16[2,256,256]{2,1,0:T(8,128)(2,1)} %get-tuple-element.27), channel_id=1, source_target_pairs={{2,0},{3,1},{0,2},{1,3},{6,4},{7,5},{4,6},{5,7},{10,8},{11,9},{8,1... | collective-permute-start | bytes 786440 | tf_op jit(solution)/shard_map/ppermute | solution.py:39
  58.4 6.7 %all-to-all-start.2 = ((bf16[8,128,256]{2,1,0:T(8,128)(2,1)}), bf16[8,128,256]{2,1,0:T(8,128)(2,1)S(1)}, u32[]{:S(2)}, u32[]{:S(2)}) async-start(bf16[8,128,256]{2,1,0:T(8,128)(2,1)} %get-tuple-element.32), calls=%async_computation.2 | async-start | bytes 1048576 | tf_op jit(solution)/shard_map/all_to_all | solution.py:28
  65.1 0.0 collective-permute-done.6
  65.1 0.1 fusion.1
  65.1 1.9 %collective-permute-start.7 = (bf16[2,256,256]{2,1,0:T(8,128)(2,1)S(1)}, bf16[2,256,256]{2,1,0:T(8,128)(2,1)S(1)}, u32[]{:S(2)}, u32[]{:S(2)}) collective-permute-start(bf16[2,256,256]{2,1,0:T(8,128)(2,1)S(1)} %get-tuple-element.29), channel_id=1, source_target_pairs={{2,0},{3,1},{0,2},{1,3},{6,4},{7,5},{4,6},{5,7},{10,8},{11,9},{8,1... | collective-permute-start | bytes 786440 | tf_op jit(solution)/shard_map/ppermute | solution.py:39
  67.1 2.6 %collective-permute-start.9 = (bf16[256,256]{1,0:T(8,128)(2,1)S(1)}, bf16[256,256]{1,0:T(8,128)(2,1)S(1)}, u32[]{:S(2)}, u32[]{:S(2)}) collective-permute-start(bf16[256,256]{1,0:T(8,128)(2,1)S(1)} %get-tuple-element.30), channel_id=1, source_target_pairs={{16,0},{17,1},{18,2},{19,3},{20,4},{21,5},{22,6},{23,7},{24,8},{25... | collective-permute-start | bytes 393224 | tf_op jit(solution)/shard_map/ppermute | solution.py:35
  69.6 3.8 %all-to-all-done.2.dq_ref = bf16[8,128,256]{2,1,0:T(8,128)(2,1)S(1)} async-done(((bf16[8,128,256]{2,1,0:T(8,128)(2,1)}), bf16[8,128,256]{2,1,0:T(8,128)(2,1)S(1)}, u32[]{:S(2)}, u32[]{:S(2)}) %all-to-all-start.2) | async-done | bytes 524320 | tf_op jit(solution)/shard_map/all_to_all | solution.py:28
  73.4 3.2 %collective-permute-start.10 = (bf16[256,256]{1,0:T(8,128)(2,1)S(1)}, bf16[256,256]{1,0:T(8,128)(2,1)S(1)}, u32[]{:S(2)}, u32[]{:S(2)}) collective-permute-start(bf16[256,256]{1,0:T(8,128)(2,1)S(1)} %get-tuple-element.33), channel_id=1, source_target_pairs={{16,1},{17,0},{18,3},{19,2},{20,5},{21,4},{22,7},{23,6},{24,9},{25... | collective-permute-start | bytes 393224 | tf_op jit(solution)/shard_map/ppermute | solution.py:35
  76.6 0.0 collective-permute-done.7.got_a_ref
  76.7 3.2 %collective-permute-start.8 = (bf16[256,256]{1,0:T(8,128)(2,1)S(1)}, bf16[256,256]{1,0:T(8,128)(2,1)S(1)}, u32[]{:S(2)}, u32[]{:S(2)}) collective-permute-start(bf16[256,256]{1,0:T(8,128)(2,1)S(1)} %fusion.2), channel_id=1, source_target_pairs={{1,0},{0,1},{3,2},{2,3},{5,4},{4,5},{7,6},{6,7},{9,8},{8,9},{11,10... | collective-permute-start | bytes 393224 | tf_op jit(solution)/shard_map/ppermute | solution.py:39
  79.9 1.2 %collective-permute-done.9.next_mine_ref = bf16[256,256]{1,0:T(8,128)(2,1)S(1)} collective-permute-done((bf16[256,256]{1,0:T(8,128)(2,1)S(1)}, bf16[256,256]{1,0:T(8,128)(2,1)S(1)}, u32[]{:S(2)}, u32[]{:S(2)}) %collective-permute-start.9) | collective-permute-done | bytes 131104 | tf_op jit(solution)/shard_map/ppermute | solution.py:35
  81.2 8.5 %collective-permute-done.10.next_other_ref = bf16[256,256]{1,0:T(8,128)(2,1)S(1)} collective-permute-done((bf16[256,256]{1,0:T(8,128)(2,1)S(1)}, bf16[256,256]{1,0:T(8,128)(2,1)S(1)}, u32[]{:S(2)}, u32[]{:S(2)}) %collective-permute-start.10) | collective-permute-done | bytes 131104 | tf_op jit(solution)/shard_map/ppermute | solution.py:35
  89.6 0.9 %finish.1 = (bf16[256,256]{1,0:T(8,128)(2,1)}, bf16[256,256]{1,0:T(8,128)(2,1)}, bf16[256,256]{1,0:T(8,128)(2,1)}) custom-call(s32[1]{0:T(128)} %bitcast.info_ref, f32[2,256,256]{2,1,0:T(8,128)S(1)} %get-tuple-element.25.own_a_ref, bf16[2,256,256]{2,1,0:T(8,128)(2,1)S(1)} %collective-permute-done.7.got_a_ref, ...), custom_call_target="tpu_custom_call" | custom-call | bytes 2097152 | tf_op jit(solution)/shard_map/finish/pallas_call | solution.py:335
  (12 shorter events, 0.1 us)
Async XLA Ops:
  2.4 23.2 %collective-permute-start.3 = (bf16[256,256]{1,0:T(8,128)(2,1)}, bf16[256,256]{1,0:T(8,128)(2,1)S(1)}, u32[]{:S(2)}, u32[]{:S(2)}) collective-permute-start(bf16[256,256]{1,0:T(8,128)(2,1)} %get-tuple-element.20), channel_id=1, source_target_pairs={{0,17},{1,16},{2,19},{3,18},{4,21},{5,20},{6,23},{7,22},{8,25},{9,... | collective-permute-start | bytes 393224 | tf_op jit(solution)/shard_map/ppermute | solution.py:35
  8.3 6.4 %collective-permute-start = (bf16[256,256]{1,0:T(8,128)(2,1)}, bf16[256,256]{1,0:T(8,128)(2,1)S(1)}, u32[]{:S(2)}, u32[]{:S(2)}) collective-permute-start(bf16[256,256]{1,0:T(8,128)(2,1)} %get-tuple-element.20), channel_id=1, source_target_pairs={{1,0},{0,1},{3,2},{2,3},{5,4},{4,5},{7,6},{6,7},{9,8},{8,9},{11,10... | collective-permute-start | bytes 393224 | tf_op jit(solution)/shard_map/ppermute | solution.py:39
  10.3 18.5 %collective-permute-start.2 = (bf16[256,256]{1,0:T(8,128)(2,1)}, bf16[256,256]{1,0:T(8,128)(2,1)S(1)}, u32[]{:S(2)}, u32[]{:S(2)}) collective-permute-start(bf16[256,256]{1,0:T(8,128)(2,1)} %get-tuple-element.19.a0_ref), channel_id=1, source_target_pairs={{0,16},{1,17},{2,18},{3,19},{4,20},{5,21},{6,22},{7,23},{8,24},{9,... | collective-permute-start | bytes 393224 | tf_op jit(solution)/shard_map/ppermute | solution.py:35
  15.6 15.2 %collective-permute-start.1 = (bf16[2,256,256]{2,1,0:T(8,128)(2,1)S(1)}, bf16[2,256,256]{2,1,0:T(8,128)(2,1)S(1)}, u32[]{:S(2)}, u32[]{:S(2)}) collective-permute-start(bf16[2,256,256]{2,1,0:T(8,128)(2,1)S(1)} %pad_maximum_fusion), channel_id=1, source_target_pairs={{2,0},{3,1},{0,2},{1,3},{6,4},{7,5},{4,6},{5,7},{10,8},{11,9},{8,1... | collective-permute-start | bytes 786440 | tf_op jit(solution)/shard_map/ppermute | solution.py:39
  19.9 11.0 %copy-start.1 = (s32[256]{0:T(256)S(1)}, s32[256]{0:T(256)}, u32[]{:S(2)}) copy-start(s32[256]{0:T(256)} %param.9) | copy-start | bytes 3076
  19.9 19.7 %copy-start = (bf16[256,256]{1,0:T(8,128)(2,1)S(1)}, bf16[256,256]{1,0:T(8,128)(2,1)}, u32[]{:S(2)}) copy-start(bf16[256,256]{1,0:T(8,128)(2,1)} %get-tuple-element.19.a0_ref) | copy-start | bytes 393220
  19.9 19.7 %all-to-all-start = ((bf16[8,256,256]{2,1,0:T(8,128)(2,1)}), bf16[8,256,256]{2,1,0:T(8,128)(2,1)S(1)}, u32[]{:S(2)}, u32[]{:S(2)}) async-start(bf16[8,256,256]{2,1,0:T(8,128)(2,1)} %pack.1), calls=%async_computation | async-start | bytes 2097152 | tf_op jit(solution)/shard_map/all_to_all | solution.py:28
  25.5 8.5 %collective-permute-start.5 = (bf16[256,256]{1,0:T(8,128)(2,1)S(1)}, bf16[256,256]{1,0:T(8,128)(2,1)S(1)}, u32[]{:S(2)}, u32[]{:S(2)}) collective-permute-start(bf16[256,256]{1,0:T(8,128)(2,1)S(1)} %collective-permute-done.3.b1_ref), channel_id=1, source_target_pairs={{2,0},{3,1},{0,2},{1,3},{6,4},{7,5},{4,6},{5,7},{10,8},{11,9},{8,1... | collective-permute-start | bytes 393224 | tf_op jit(solution)/shard_map/ppermute | solution.py:39
  28.8 6.3 %collective-permute-start.4 = (bf16[256,256]{1,0:T(8,128)(2,1)S(1)}, bf16[256,256]{1,0:T(8,128)(2,1)S(1)}, u32[]{:S(2)}, u32[]{:S(2)}) collective-permute-start(bf16[256,256]{1,0:T(8,128)(2,1)S(1)} %collective-permute-done.2.b0_ref), channel_id=1, source_target_pairs={{2,0},{3,1},{0,2},{1,3},{6,4},{7,5},{4,6},{5,7},{10,8},{11,9},{8,1... | collective-permute-start | bytes 393224 | tf_op jit(solution)/shard_map/ppermute | solution.py:39
  56.0 9.1 %collective-permute-start.6 = (bf16[2,256,256]{2,1,0:T(8,128)(2,1)}, bf16[2,256,256]{2,1,0:T(8,128)(2,1)S(1)}, u32[]{:S(2)}, u32[]{:S(2)}) collective-permute-start(bf16[2,256,256]{2,1,0:T(8,128)(2,1)} %get-tuple-element.27), channel_id=1, source_target_pairs={{2,0},{3,1},{0,2},{1,3},{6,4},{7,5},{4,6},{5,7},{10,8},{11,9},{8,1... | collective-permute-start | bytes 786440 | tf_op jit(solution)/shard_map/ppermute | solution.py:39
  58.4 15.1 %all-to-all-start.2 = ((bf16[8,128,256]{2,1,0:T(8,128)(2,1)}), bf16[8,128,256]{2,1,0:T(8,128)(2,1)S(1)}, u32[]{:S(2)}, u32[]{:S(2)}) async-start(bf16[8,128,256]{2,1,0:T(8,128)(2,1)} %get-tuple-element.32), calls=%async_computation.2 | async-start | bytes 1048576 | tf_op jit(solution)/shard_map/all_to_all | solution.py:28
  65.1 11.5 %collective-permute-start.7 = (bf16[2,256,256]{2,1,0:T(8,128)(2,1)S(1)}, bf16[2,256,256]{2,1,0:T(8,128)(2,1)S(1)}, u32[]{:S(2)}, u32[]{:S(2)}) collective-permute-start(bf16[2,256,256]{2,1,0:T(8,128)(2,1)S(1)} %get-tuple-element.29), channel_id=1, source_target_pairs={{2,0},{3,1},{0,2},{1,3},{6,4},{7,5},{4,6},{5,7},{10,8},{11,9},{8,1... | collective-permute-start | bytes 786440 | tf_op jit(solution)/shard_map/ppermute | solution.py:39
  67.1 14.1 %collective-permute-start.9 = (bf16[256,256]{1,0:T(8,128)(2,1)S(1)}, bf16[256,256]{1,0:T(8,128)(2,1)S(1)}, u32[]{:S(2)}, u32[]{:S(2)}) collective-permute-start(bf16[256,256]{1,0:T(8,128)(2,1)S(1)} %get-tuple-element.30), channel_id=1, source_target_pairs={{16,0},{17,1},{18,2},{19,3},{20,4},{21,5},{22,6},{23,7},{24,8},{25... | collective-permute-start | bytes 393224 | tf_op jit(solution)/shard_map/ppermute | solution.py:35
  73.4 16.2 %collective-permute-start.10 = (bf16[256,256]{1,0:T(8,128)(2,1)S(1)}, bf16[256,256]{1,0:T(8,128)(2,1)S(1)}, u32[]{:S(2)}, u32[]{:S(2)}) collective-permute-start(bf16[256,256]{1,0:T(8,128)(2,1)S(1)} %get-tuple-element.33), channel_id=1, source_target_pairs={{16,1},{17,0},{18,3},{19,2},{20,5},{21,4},{22,7},{23,6},{24,9},{25... | collective-permute-start | bytes 393224 | tf_op jit(solution)/shard_map/ppermute | solution.py:35
  76.7 12.9 %collective-permute-start.8 = (bf16[256,256]{1,0:T(8,128)(2,1)S(1)}, bf16[256,256]{1,0:T(8,128)(2,1)S(1)}, u32[]{:S(2)}, u32[]{:S(2)}) collective-permute-start(bf16[256,256]{1,0:T(8,128)(2,1)S(1)} %fusion.2), channel_id=1, source_target_pairs={{1,0},{0,1},{3,2},{2,3},{5,4},{4,5},{7,6},{6,7},{9,8},{8,9},{11,10... | collective-permute-start | bytes 393224 | tf_op jit(solution)/shard_map/ppermute | solution.py:39

commit v5 on v3

--- a/solution.py
+++ b/solution.py
@@ -306,9 +306,8 @@
     b0, b1 = row_step(mine, 1), row_step(give, 1, 1)
     a1 = partner(give, 1)
     qg = exchange(qg, XC_GROUPS)
-    a23 = partner(jnp.stack([mine, a1]), 2)
-    b3, group_lengths = lax.optimization_barrier((partner(b1, 2), group_lengths))
-    kv = [mine, a1, a23, b0, b1, partner(b0, 2), b3]
+    a23, group_lengths = lax.optimization_barrier((partner(jnp.stack([mine, a1]), 2), group_lengths))
+    kv = [mine, a1, a23, b0, b1, partner(b0, 2), partner(b1, 2)]
 
     low, high = key_ranges(group_lengths, row, y_lo)
     lohi = jnp.stack([low, high], axis=1)

time: 90.8 us -> 88.5 us (0.975)
  the two profiles are of different devices: /device:TPU:249 before, /device:TPU:247 now
where the time goes in v5:
time: 88.5 us; the launch traced here: 87.9 us
  starting transfers between devices  49 us (55%)
  waiting for transfers between devices  15.7 us (18%)
  Pallas kernels  12.2 us (14%)
  blocking collectives  6.76 us (8%)
  other arithmetic  2.93 us (3%)
    ppermute x7, starting transfers between devices, partner(): return lax.ppermute(value, 'inner', [(i ^ flip, i) for i in range(ROW)])  19.2 us
    all_to_all x2, starting transfers between devices, exchange(): lax.all_to_all(value, 'inner', 0, 0, axis_index_groups=groups, tiled=True)  15.1 us
    ppermute x4, starting transfers between devices, row_step(): return lax.ppermute(value, ('outer', 'inner'), route)  14.7 us
    ppermute x4, waiting for transfers between devices, row_step(): return lax.ppermute(value, ('outer', 'inner'), route)  7.52 us
    all_to_all x1, blocking collectives, exchange(): lax.all_to_all(value, 'inner', 0, 0, axis_index_groups=groups, tiled=True)  6.76 us
    ppermute x7, waiting for transfers between devices, partner(): return lax.ppermute(value, 'inner', [(i ^ flip, i) for i in range(ROW)])  5.58 us
    pallas_call x1, Pallas kernels, grads_call(): pl.pallas_call(grads_kernel, out_shape=(jax.ShapeDtypeStruct((NQ, HD, BLK...  4.81 us
    pallas_call x1, Pallas kernels, stats_call(): pl.pallas_call(stats_kernel, out_shape=jax.ShapeDtypeStruct((NX, NQ, 2, B...  2.68 us
  transfers between devices with their start and end apart: 13, of which 5 were waited for; matrix products, arithmetic and copies ran while one was open for 4% of the time, Pallas kernels for 2%

profile of v5, /device:TPU:247, one launch (start us, length us, event | category | flops | bytes accessed | tf_op | source)
XLA Modules:
  0.0 87.9 jit_solution(7254904427584858017)
XLA Ops:
  0.6 1.7 %split.1 = (bf16[256,256]{1,0:T(8,128)(2,1)}, bf16[256,256]{1,0:T(8,128)(2,1)}) custom-call(s32[1]{0:T(128)} %bitcast.info_ref, bf16[256,256]{1,0:T(8,128)(2,1)} %k_ref.1, bf16[256,256]{1,0:T(8,128)(2,1)} %v_ref.1), custom_call_target="tpu_custom_call" | custom-call | bytes 524288 | tf_op jit(solution)/shard_map/split/pallas_call | solution.py:287
  2.4 5.1 %collective-permute-start.3 = (bf16[256,256]{1,0:T(8,128)(2,1)}, bf16[256,256]{1,0:T(8,128)(2,1)S(1)}, u32[]{:S(2)}, u32[]{:S(2)}) collective-permute-start(bf16[256,256]{1,0:T(8,128)(2,1)} %get-tuple-element.18), channel_id=1, source_target_pairs={{0,17},{1,16},{2,19},{3,18},{4,21},{5,20},{6,23},{7,22},{8,25},{9,... | collective-permute-start | bytes 393224 | tf_op jit(solution)/shard_map/ppermute | solution.py:35
  7.4 1.9 %collective-permute-start = (bf16[256,256]{1,0:T(8,128)(2,1)}, bf16[256,256]{1,0:T(8,128)(2,1)S(1)}, u32[]{:S(2)}, u32[]{:S(2)}) collective-permute-start(bf16[256,256]{1,0:T(8,128)(2,1)} %get-tuple-element.18), channel_id=1, source_target_pairs={{1,0},{0,1},{3,2},{2,3},{5,4},{4,5},{7,6},{6,7},{9,8},{8,9},{11,10... | collective-permute-start | bytes 393224 | tf_op jit(solution)/shard_map/ppermute | solution.py:39
  9.4 4.2 %collective-permute-start.2 = (bf16[256,256]{1,0:T(8,128)(2,1)}, bf16[256,256]{1,0:T(8,128)(2,1)S(1)}, u32[]{:S(2)}, u32[]{:S(2)}) collective-permute-start(bf16[256,256]{1,0:T(8,128)(2,1)} %get-tuple-element.17.a0_ref), channel_id=1, source_target_pairs={{0,16},{1,17},{2,18},{3,19},{4,20},{5,21},{6,22},{7,23},{8,24},{9,... | collective-permute-start | bytes 393224 | tf_op jit(solution)/shard_map/ppermute | solution.py:35
  13.6 2.1 %pack.1 = bf16[8,256,256]{2,1,0:T(8,128)(2,1)} custom-call(bf16[256,256]{1,0:T(8,128)(2,1)} %q_ref.1, bf16[256,256]{1,0:T(8,128)(2,1)} %g_ref.1), custom_call_target="tpu_custom_call" | custom-call | bytes 1048576 | tf_op jit(solution)/shard_map/pack/pallas_call | solution.py:296
  15.7 5.3 %all-to-all-start = ((bf16[8,256,256]{2,1,0:T(8,128)(2,1)}), bf16[8,256,256]{2,1,0:T(8,128)(2,1)S(1)}, u32[]{:S(2)}, u32[]{:S(2)}) async-start(bf16[8,256,256]{2,1,0:T(8,128)(2,1)} %pack.1), calls=%async_computation | async-start | bytes 2097152 | tf_op jit(solution)/shard_map/all_to_all | solution.py:28
  21.0 0.1 add_multiply_fusion
  21.1 0.1 mul.44
  21.2 0.0 collective-permute-done.a1_ref
  21.2 3.2 %collective-permute-start.1 = (bf16[2,256,256]{2,1,0:T(8,128)(2,1)S(1)}, bf16[2,256,256]{2,1,0:T(8,128)(2,1)S(1)}, u32[]{:S(2)}, u32[]{:S(2)}) collective-permute-start(bf16[2,256,256]{2,1,0:T(8,128)(2,1)S(1)} %pad_maximum_fusion), channel_id=1, source_target_pairs={{2,0},{3,1},{0,2},{1,3},{6,4},{7,5},{4,6},{5,7},{10,8},{11,9},{8,1... | collective-permute-start | bytes 786440 | tf_op jit(solution)/shard_map/ppermute | solution.py:39
  24.4 0.1 iota_add_fusion
  24.5 0.0 collective-permute-done.3.b1_ref
  24.5 2.1 %collective-permute-start.5 = (bf16[256,256]{1,0:T(8,128)(2,1)S(1)}, bf16[256,256]{1,0:T(8,128)(2,1)S(1)}, u32[]{:S(2)}, u32[]{:S(2)}) collective-permute-start(bf16[256,256]{1,0:T(8,128)(2,1)S(1)} %collective-permute-done.3.b1_ref), channel_id=1, source_target_pairs={{2,0},{3,1},{0,2},{1,3},{6,4},{7,5},{4,6},{5,7},{10,8},{11,9},{8,1... | collective-permute-start | bytes 393224 | tf_op jit(solution)/shard_map/ppermute | solution.py:39
  26.6 0.0 collective-permute-done.2.b0_ref
  26.6 3.2 %collective-permute-start.4 = (bf16[256,256]{1,0:T(8,128)(2,1)S(1)}, bf16[256,256]{1,0:T(8,128)(2,1)S(1)}, u32[]{:S(2)}, u32[]{:S(2)}) collective-permute-start(bf16[256,256]{1,0:T(8,128)(2,1)S(1)} %collective-permute-done.2.b0_ref), channel_id=1, source_target_pairs={{2,0},{3,1},{0,2},{1,3},{6,4},{7,5},{4,6},{5,7},{10,8},{11,9},{8,1... | collective-permute-start | bytes 393224 | tf_op jit(solution)/shard_map/ppermute | solution.py:39
  29.8 0.8 collective-permute-done.1.a23_ref
  30.6 0.3 reduce-window.9
  30.9 0.1 slice.37
  31.1 0.1 slice_reduce_fusion.1
  31.2 0.1 fusion.7
  31.3 0.1 broadcast_add_fusion
  31.3 0.1 fusion.6
  31.4 1.1 %select_reduce_fusion.1 = s32[8,256]{1,0:T(8,128)S(1)} fusion(s32[254]{0:T(256)S(1)} %bitcast.23, s32[8,256]{1,0:T(8,128)S(1)} %iota_add_fusion, s32[254]{0:T(256)S(1)} %bitcast.22), kind=kLoop, calls=%fused_computation.1 | loop fusion | flops 1558528 | bytes 18416 | tf_op jit(solution)/shard_map/reduce_max | solution.py:51
  32.5 0.1 slice_reduce_fusion
  32.6 0.8 select_reduce_fusion
  33.4 0.2 fusion.3
  33.6 0.1 reshape_minimum_fusion
  33.7 0.1 concatenate.3.info_ref
  33.8 0.0 collective-permute-done.5.b3_ref
  33.8 2.4 %collective-permute-done.4.b2_ref = bf16[256,256]{1,0:T(8,128)(2,1)S(1)} collective-permute-done((bf16[256,256]{1,0:T(8,128)(2,1)S(1)}, bf16[256,256]{1,0:T(8,128)(2,1)S(1)}, u32[]{:S(2)}, u32[]{:S(2)}) %collective-permute-start.4) | collective-permute-done | bytes 131104 | tf_op jit(solution)/shard_map/ppermute | solution.py:39
  36.3 0.0 all-to-all-done.qg_ref
  36.3 2.7 %stats.1 = f32[4,8,2,256]{3,2,1,0:T(2,128)S(1)} custom-call(s32[24]{0:T(128)S(1)} %concatenate.3.info_ref, bf16[8,256,256]{2,1,0:T(8,128)(2,1)S(1)} %all-to-all-done.qg_ref, bf16[256,256]{1,0:T(8,128)(2,1)S(1)} %copy-done, bf16[256,256]{1,0:T(8,128)(2,1)S(1)} %collective-permute-done.a1_ref, bf16[2,256,256]{2,1,0:T(8,128)(2,1)S(1)} %collective-permute-done.1.a23_ref, ...), custom_call_target="tpu_custom_call" | custom-call | flops 536870912 | bytes 2097152 | tf_op jit(solution)/shard_map/stats/pallas_call | solution.py:236
  39.0 6.8 %all_to_all.15.stats_ref = f32[4,8,2,256]{3,2,1,0:T(2,128)S(1)} all-to-all(f32[4,8,2,256]{3,2,1,0:T(2,128)S(1)} %stats.1), channel_id=1, replica_groups={{0,4,8,12},{1,5,9,13},{2,6,10,14},{3,7,11,15},{16,20,24,28},{17,21,25,2..., dimensions={0} | all-to-all | bytes 131072 | tf_op jit(solution)/shard_map/all_to_all | solution.py:28
  45.7 4.8 %grads.1 = (bf16[8,128,256]{2,1,0:T(8,128)(2,1)}, f32[2,256,256]{2,1,0:T(8,128)S(1)}, f32[2,256,256]{2,1,0:T(8,128)S(1)}, bf16[2,256,256]{2,1,0:T(8,128)(2,1)S(1)}, bf16[2,256,256]{2,1,0:T(8,128)(2,1)}) custom-call(s32[24]{0:T(128)S(1)} %concatenate.3.info_ref, bf16[8,256,256]{2,1,0:T(8,128)(2,1)S(1)} %all-to-all-done.qg_ref, bf16[256,256]{1,0:T(8,128)(2,1)S(1)} %copy-done, ...), custom_call_target="tpu_custom_call" | custom-call | flops 1342177280 | bytes 4194304 | tf_op jit(solution)/shard_map/grads/pallas_call | solution.py:254
  50.5 2.3 %collective-permute-start.6 = (bf16[2,256,256]{2,1,0:T(8,128)(2,1)}, bf16[2,256,256]{2,1,0:T(8,128)(2,1)S(1)}, u32[]{:S(2)}, u32[]{:S(2)}) collective-permute-start(bf16[2,256,256]{2,1,0:T(8,128)(2,1)} %get-tuple-element.23), channel_id=1, source_target_pairs={{2,0},{3,1},{0,2},{1,3},{6,4},{7,5},{4,6},{5,7},{10,8},{11,9},{8,1... | collective-permute-start | bytes 786440 | tf_op jit(solution)/shard_map/ppermute | solution.py:39
  52.9 9.8 %all-to-all-start.2 = ((bf16[8,128,256]{2,1,0:T(8,128)(2,1)}), bf16[8,128,256]{2,1,0:T(8,128)(2,1)S(1)}, u32[]{:S(2)}, u32[]{:S(2)}) async-start(bf16[8,128,256]{2,1,0:T(8,128)(2,1)} %get-tuple-element.28), calls=%async_computation.2 | async-start | bytes 1048576 | tf_op jit(solution)/shard_map/all_to_all | solution.py:28
  62.7 0.0 collective-permute-done.6
  62.7 0.1 fusion.1
  62.7 1.9 %collective-permute-start.7 = (bf16[2,256,256]{2,1,0:T(8,128)(2,1)S(1)}, bf16[2,256,256]{2,1,0:T(8,128)(2,1)S(1)}, u32[]{:S(2)}, u32[]{:S(2)}) collective-permute-start(bf16[2,256,256]{2,1,0:T(8,128)(2,1)S(1)} %get-tuple-element.25), channel_id=1, source_target_pairs={{2,0},{3,1},{0,2},{1,3},{6,4},{7,5},{4,6},{5,7},{10,8},{11,9},{8,1... | collective-permute-start | bytes 786440 | tf_op jit(solution)/shard_map/ppermute | solution.py:39
  64.7 3.2 %collective-permute-start.9 = (bf16[256,256]{1,0:T(8,128)(2,1)S(1)}, bf16[256,256]{1,0:T(8,128)(2,1)S(1)}, u32[]{:S(2)}, u32[]{:S(2)}) collective-permute-start(bf16[256,256]{1,0:T(8,128)(2,1)S(1)} %get-tuple-element.26), channel_id=1, source_target_pairs={{16,0},{17,1},{18,2},{19,3},{20,4},{21,5},{22,6},{23,7},{24,8},{25... | collective-permute-start | bytes 393224 | tf_op jit(solution)/shard_map/ppermute | solution.py:35
  67.8 2.6 %all-to-all-done.2.dq_ref = bf16[8,128,256]{2,1,0:T(8,128)(2,1)S(1)} async-done(((bf16[8,128,256]{2,1,0:T(8,128)(2,1)}), bf16[8,128,256]{2,1,0:T(8,128)(2,1)S(1)}, u32[]{:S(2)}, u32[]{:S(2)}) %all-to-all-start.2) | async-done | bytes 524320 | tf_op jit(solution)/shard_map/all_to_all | solution.py:28
  70.4 2.2 %collective-permute-start.10 = (bf16[256,256]{1,0:T(8,128)(2,1)S(1)}, bf16[256,256]{1,0:T(8,128)(2,1)S(1)}, u32[]{:S(2)}, u32[]{:S(2)}) collective-permute-start(bf16[256,256]{1,0:T(8,128)(2,1)S(1)} %get-tuple-element.29), channel_id=1, source_target_pairs={{16,1},{17,0},{18,3},{19,2},{20,5},{21,4},{22,7},{23,6},{24,9},{25... | collective-permute-start | bytes 393224 | tf_op jit(solution)/shard_map/ppermute | solution.py:35
  72.6 2.3 %collective-permute-done.7.got_a_ref = bf16[2,256,256]{2,1,0:T(8,128)(2,1)S(1)} collective-permute-done((bf16[2,256,256]{2,1,0:T(8,128)(2,1)S(1)}, bf16[2,256,256]{2,1,0:T(8,128)(2,1)S(1)}, u32[]{:S(2)}, u32[]{:S(2)}) %collective-permute-start.7) | collective-permute-done | bytes 262176 | tf_op jit(solution)/shard_map/ppermute | solution.py:39
  75.0 4.5 %collective-permute-start.8 = (bf16[256,256]{1,0:T(8,128)(2,1)S(1)}, bf16[256,256]{1,0:T(8,128)(2,1)S(1)}, u32[]{:S(2)}, u32[]{:S(2)}) collective-permute-start(bf16[256,256]{1,0:T(8,128)(2,1)S(1)} %fusion.2), channel_id=1, source_target_pairs={{1,0},{0,1},{3,2},{2,3},{5,4},{4,5},{7,6},{6,7},{9,8},{8,9},{11,10... | collective-permute-start | bytes 393224 | tf_op jit(solution)/shard_map/ppermute | solution.py:39
  79.5 0.0 collective-permute-done.9.next_mine_ref
  79.5 7.5 %collective-permute-done.10.next_other_ref = bf16[256,256]{1,0:T(8,128)(2,1)S(1)} collective-permute-done((bf16[256,256]{1,0:T(8,128)(2,1)S(1)}, bf16[256,256]{1,0:T(8,128)(2,1)S(1)}, u32[]{:S(2)}, u32[]{:S(2)}) %collective-permute-start.10) | collective-permute-done | bytes 131104 | tf_op jit(solution)/shard_map/ppermute | solution.py:35
  87.0 0.0 collective-permute-done.8.mate_a_ref
  87.0 0.9 %finish.1 = (bf16[256,256]{1,0:T(8,128)(2,1)}, bf16[256,256]{1,0:T(8,128)(2,1)}, bf16[256,256]{1,0:T(8,128)(2,1)}) custom-call(s32[1]{0:T(128)} %bitcast.info_ref, f32[2,256,256]{2,1,0:T(8,128)S(1)} %get-tuple-element.21.own_a_ref, bf16[2,256,256]{2,1,0:T(8,128)(2,1)S(1)} %collective-permute-done.7.got_a_ref, ...), custom_call_target="tpu_custom_call" | custom-call | bytes 2097152 | tf_op jit(solution)/shard_map/finish/pallas_call | solution.py:335
  (12 shorter events, 0.1 us)
Async XLA Ops:
  2.4 22.1 %collective-permute-start.3 = (bf16[256,256]{1,0:T(8,128)(2,1)}, bf16[256,256]{1,0:T(8,128)(2,1)S(1)}, u32[]{:S(2)}, u32[]{:S(2)}) collective-permute-start(bf16[256,256]{1,0:T(8,128)(2,1)} %get-tuple-element.18), channel_id=1, source_target_pairs={{0,17},{1,16},{2,19},{3,18},{4,21},{5,20},{6,23},{7,22},{8,25},{9,... | collective-permute-start | bytes 393224 | tf_op jit(solution)/shard_map/ppermute | solution.py:35
  7.4 13.7 %collective-permute-start = (bf16[256,256]{1,0:T(8,128)(2,1)}, bf16[256,256]{1,0:T(8,128)(2,1)S(1)}, u32[]{:S(2)}, u32[]{:S(2)}) collective-permute-start(bf16[256,256]{1,0:T(8,128)(2,1)} %get-tuple-element.18), channel_id=1, source_target_pairs={{1,0},{0,1},{3,2},{2,3},{5,4},{4,5},{7,6},{6,7},{9,8},{8,9},{11,10... | collective-permute-start | bytes 393224 | tf_op jit(solution)/shard_map/ppermute | solution.py:39
  9.4 17.2 %collective-permute-start.2 = (bf16[256,256]{1,0:T(8,128)(2,1)}, bf16[256,256]{1,0:T(8,128)(2,1)S(1)}, u32[]{:S(2)}, u32[]{:S(2)}) collective-permute-start(bf16[256,256]{1,0:T(8,128)(2,1)} %get-tuple-element.17.a0_ref), channel_id=1, source_target_pairs={{0,16},{1,17},{2,18},{3,19},{4,20},{5,21},{6,22},{7,23},{8,24},{9,... | collective-permute-start | bytes 393224 | tf_op jit(solution)/shard_map/ppermute | solution.py:35
  15.7 5.5 %copy-start = (bf16[256,256]{1,0:T(8,128)(2,1)S(1)}, bf16[256,256]{1,0:T(8,128)(2,1)}, u32[]{:S(2)}) copy-start(bf16[256,256]{1,0:T(8,128)(2,1)} %get-tuple-element.17.a0_ref) | copy-start | bytes 393220
  15.7 15.0 %copy-start.1 = (s32[256]{0:T(256)S(1)}, s32[256]{0:T(256)}, u32[]{:S(2)}) copy-start(s32[256]{0:T(256)} %param.9) | copy-start | bytes 3076
  15.7 20.6 %all-to-all-start = ((bf16[8,256,256]{2,1,0:T(8,128)(2,1)}), bf16[8,256,256]{2,1,0:T(8,128)(2,1)S(1)}, u32[]{:S(2)}, u32[]{:S(2)}) async-start(bf16[8,256,256]{2,1,0:T(8,128)(2,1)} %pack.1), calls=%async_computation | async-start | bytes 2097152 | tf_op jit(solution)/shard_map/all_to_all | solution.py:28
  21.2 9.4 %collective-permute-start.1 = (bf16[2,256,256]{2,1,0:T(8,128)(2,1)S(1)}, bf16[2,256,256]{2,1,0:T(8,128)(2,1)S(1)}, u32[]{:S(2)}, u32[]{:S(2)}) collective-permute-start(bf16[2,256,256]{2,1,0:T(8,128)(2,1)S(1)} %pad_maximum_fusion), channel_id=1, source_target_pairs={{2,0},{3,1},{0,2},{1,3},{6,4},{7,5},{4,6},{5,7},{10,8},{11,9},{8,1... | collective-permute-start | bytes 786440 | tf_op jit(solution)/shard_map/ppermute | solution.py:39
  24.5 9.3 %collective-permute-start.5 = (bf16[256,256]{1,0:T(8,128)(2,1)S(1)}, bf16[256,256]{1,0:T(8,128)(2,1)S(1)}, u32[]{:S(2)}, u32[]{:S(2)}) collective-permute-start(bf16[256,256]{1,0:T(8,128)(2,1)S(1)} %collective-permute-done.3.b1_ref), channel_id=1, source_target_pairs={{2,0},{3,1},{0,2},{1,3},{6,4},{7,5},{4,6},{5,7},{10,8},{11,9},{8,1... | collective-permute-start | bytes 393224 | tf_op jit(solution)/shard_map/ppermute | solution.py:39
  26.6 9.7 %collective-permute-start.4 = (bf16[256,256]{1,0:T(8,128)(2,1)S(1)}, bf16[256,256]{1,0:T(8,128)(2,1)S(1)}, u32[]{:S(2)}, u32[]{:S(2)}) collective-permute-start(bf16[256,256]{1,0:T(8,128)(2,1)S(1)} %collective-permute-done.2.b0_ref), channel_id=1, source_target_pairs={{2,0},{3,1},{0,2},{1,3},{6,4},{7,5},{4,6},{5,7},{10,8},{11,9},{8,1... | collective-permute-start | bytes 393224 | tf_op jit(solution)/shard_map/ppermute | solution.py:39
  50.5 12.1 %collective-permute-start.6 = (bf16[2,256,256]{2,1,0:T(8,128)(2,1)}, bf16[2,256,256]{2,1,0:T(8,128)(2,1)S(1)}, u32[]{:S(2)}, u32[]{:S(2)}) collective-permute-start(bf16[2,256,256]{2,1,0:T(8,128)(2,1)} %get-tuple-element.23), channel_id=1, source_target_pairs={{2,0},{3,1},{0,2},{1,3},{6,4},{7,5},{4,6},{5,7},{10,8},{11,9},{8,1... | collective-permute-start | bytes 786440 | tf_op jit(solution)/shard_map/ppermute | solution.py:39
  52.9 17.5 %all-to-all-start.2 = ((bf16[8,128,256]{2,1,0:T(8,128)(2,1)}), bf16[8,128,256]{2,1,0:T(8,128)(2,1)S(1)}, u32[]{:S(2)}, u32[]{:S(2)}) async-start(bf16[8,128,256]{2,1,0:T(8,128)(2,1)} %get-tuple-element.28), calls=%async_computation.2 | async-start | bytes 1048576 | tf_op jit(solution)/shard_map/all_to_all | solution.py:28
  62.7 12.2 %collective-permute-start.7 = (bf16[2,256,256]{2,1,0:T(8,128)(2,1)S(1)}, bf16[2,256,256]{2,1,0:T(8,128)(2,1)S(1)}, u32[]{:S(2)}, u32[]{:S(2)}) collective-permute-start(bf16[2,256,256]{2,1,0:T(8,128)(2,1)S(1)} %get-tuple-element.25), channel_id=1, source_target_pairs={{2,0},{3,1},{0,2},{1,3},{6,4},{7,5},{4,6},{5,7},{10,8},{11,9},{8,1... | collective-permute-start | bytes 786440 | tf_op jit(solution)/shard_map/ppermute | solution.py:39
  64.7 14.9 %collective-permute-start.9 = (bf16[256,256]{1,0:T(8,128)(2,1)S(1)}, bf16[256,256]{1,0:T(8,128)(2,1)S(1)}, u32[]{:S(2)}, u32[]{:S(2)}) collective-permute-start(bf16[256,256]{1,0:T(8,128)(2,1)S(1)} %get-tuple-element.26), channel_id=1, source_target_pairs={{16,0},{17,1},{18,2},{19,3},{20,4},{21,5},{22,6},{23,7},{24,8},{25... | collective-permute-start | bytes 393224 | tf_op jit(solution)/shard_map/ppermute | solution.py:35
  70.4 16.6 %collective-permute-start.10 = (bf16[256,256]{1,0:T(8,128)(2,1)S(1)}, bf16[256,256]{1,0:T(8,128)(2,1)S(1)}, u32[]{:S(2)}, u32[]{:S(2)}) collective-permute-start(bf16[256,256]{1,0:T(8,128)(2,1)S(1)} %get-tuple-element.29), channel_id=1, source_target_pairs={{16,1},{17,0},{18,3},{19,2},{20,5},{21,4},{22,7},{23,6},{24,9},{25... | collective-permute-start | bytes 393224 | tf_op jit(solution)/shard_map/ppermute | solution.py:35
  75.0 12.0 %collective-permute-start.8 = (bf16[256,256]{1,0:T(8,128)(2,1)S(1)}, bf16[256,256]{1,0:T(8,128)(2,1)S(1)}, u32[]{:S(2)}, u32[]{:S(2)}) collective-permute-start(bf16[256,256]{1,0:T(8,128)(2,1)S(1)} %fusion.2), channel_id=1, source_target_pairs={{1,0},{0,1},{3,2},{2,3},{5,4},{4,5},{7,6},{6,7},{9,8},{8,9},{11,10... | collective-permute-start | bytes 393224 | tf_op jit(solution)/shard_map/ppermute | solution.py:39

commit v6 on v5

--- a/solution.py
+++ b/solution.py
@@ -53,12 +53,12 @@
     return low, jnp.minimum(high, last)
 
 
-def list_tiles(info_ref, tiles_ref):
+def list_tiles(info_ref, tiles_ref, wanted=(False, True), start=0):
     x = info_ref[0]
     count = jnp.int32(0)
     for n in range(NQ):
         before = n // NC < x
-        row = jnp.where(before, COL * BLK, 0)
+        row = jnp.where(before, start, 0)
         pos = jnp.where(before, info_ref[2], info_ref[1])
 
         def put(t, i, n=n, row=row, pos=pos):
@@ -67,7 +67,10 @@
             tiles_ref[2, i] = pos + t * BLK
             return i + 1
 
-        count = lax.fori_loop(info_ref[8 + n], info_ref[16 + n], put, count)
+        first, last = info_ref[8 + n], info_ref[16 + n]
+        if len(wanted) == 1:
+            last = jnp.where(before == wanted[0], last, first)
+        count = lax.fori_loop(first, last, put, count)
     for i in range(UNROLL - 1):
         tiles_ref[0, count + i] = 0
         tiles_ref[1, count + i] = 0
@@ -123,7 +126,7 @@
     out_ref, tiles_ref, kv_ref, m_ref, l_ref, u_ref,
 ):
     y_lo, core = info_ref[3], info_ref[4]
-    pairs = list_tiles(info_ref, tiles_ref)
+    pairs = list_tiles(info_ref, tiles_ref, start=COL * BLK)
     blocks = (a0_ref, a1_ref, a23_ref.at[0], a23_ref.at[1], b0_ref, b1_ref, b2_ref, b3_ref)
     assemble(y_lo, core, blocks, kv_ref)
     m_ref[...] = jnp.full_like(m_ref, NEG)
@@ -157,15 +160,17 @@
 
 
 def grads_kernel(
-    info_ref, qg_ref, a0_ref, a1_ref, a23_ref, b0_ref, b1_ref, b2_ref, b3_ref, lohi_ref, stats_ref,
-    dq_ref, own_a_ref, own_b_ref, away_a_ref, away_b_ref,
-    tiles_ref, kv_ref, kt_ref, acc_ref, dqt_ref, sums_ref,
+    before, info_ref, qg_ref, lohi_ref, stats_ref, *refs
 ):
+    block_refs, refs = refs[: 4 if before else 3], refs[4 if before else 3 :]
+    dq_in_ref, refs = (refs[0], refs[1:]) if before else (None, refs)
+    dq_ref, own_ref, away_ref, tiles_ref, kv_ref, kt_ref, acc_ref, dqt_ref, sums_ref = refs
     y_lo, core = info_ref[3], info_ref[4]
     scale = 1.0 / math.sqrt(HD)
-    pairs = list_tiles(info_ref, tiles_ref)
-    blocks = (a0_ref, a1_ref, a23_ref.at[0], a23_ref.at[1], b0_ref, b1_ref, b2_ref, b3_ref)
-    assemble(y_lo, core, blocks, kv_ref)
+    pairs = list_tiles(info_ref, tiles_ref, (before,))
+    if not before:
+        block_refs = (block_refs[0], block_refs[1], block_refs[2].at[0], block_refs[2].at[1])
+    assemble(y_lo, core, block_refs, kv_ref)
     kt_ref[...] = kv_ref[:, :HD].T
     acc_ref[...] = jnp.zeros_like(acc_ref)
     dqt_ref[...] = jnp.zeros_like(dqt_ref)
@@ -197,13 +202,15 @@
 
     lax.fori_loop(0, pairs, step, 0)
     for n in range(NQ):
-        dq_ref[n] = (dqt_ref[n] * scale).astype(jnp.bfloat16)
+        dq = dqt_ref[n] * scale
+        if before:
+            dq += dq_in_ref[n].astype(jnp.float32)
+        dq_ref[n] = dq.astype(jnp.bfloat16)
     for i in range(NC):
-        for start, own_ref, away_ref in ((0, own_a_ref, away_a_ref), (COL * BLK, own_b_ref, away_b_ref)):
-            for y, out_ref in ((y_lo, own_ref), (1 - y_lo, away_ref)):
-                rows = pl.ds(pl.multiple_of(start + (y * NC + (core ^ i)) * BLK, BLK), BLK)
-                out_ref[i, :, :HD] = (acc_ref[rows, :HD] * scale).astype(out_ref.dtype)
-                out_ref[i, :, HD:] = acc_ref[rows, HD:].astype(out_ref.dtype)
+        for y, out_ref in ((y_lo, own_ref), (1 - y_lo, away_ref)):
+            rows = pl.ds(pl.multiple_of((y * NC + (core ^ i)) * BLK, BLK), BLK)
+            out_ref[i, :, :HD] = (acc_ref[rows, :HD] * scale).astype(out_ref.dtype)
+            out_ref[i, :, HD:] = acc_ref[rows, HD:].astype(out_ref.dtype)
 
 
 def finish_kernel(
@@ -249,31 +256,29 @@
     )(info, qg, *kv, lohi)
 
 
-def grads_call(info, qg, kv, lohi, stats):
+def grads_call(before, info, qg, lohi, stats, *more):
     part = (NC, BLK, 2 * HD)
     return pl.pallas_call(
-        grads_kernel,
+        functools.partial(grads_kernel, before),
         out_shape=(
             jax.ShapeDtypeStruct((NQ, HD, BLK), jnp.bfloat16),
             jax.ShapeDtypeStruct(part, jnp.float32),
-            jax.ShapeDtypeStruct(part, jnp.float32),
-            jax.ShapeDtypeStruct(part, jnp.bfloat16),
             jax.ShapeDtypeStruct(part, jnp.bfloat16),
         ),
-        in_specs=[SMEM] + [VMEM] * 10,
-        out_specs=(VMEM,) * 5,
+        in_specs=[SMEM] + [VMEM] * (3 + len(more)),
+        out_specs=(VMEM,) * 3,
         scratch_shapes=[
             pltpu.SMEM((3, NQ * COL + UNROLL), jnp.int32),
-            pltpu.VMEM((2 * COL * BLK, 2 * HD), jnp.bfloat16),
-            pltpu.VMEM((HD, 2 * COL * BLK), jnp.bfloat16),
-            pltpu.VMEM((2 * COL * BLK, 2 * HD), jnp.float32),
+            pltpu.VMEM((COL * BLK, 2 * HD), jnp.bfloat16),
+            pltpu.VMEM((HD, COL * BLK), jnp.bfloat16),
+            pltpu.VMEM((COL * BLK, 2 * HD), jnp.float32),
             pltpu.VMEM((NQ, HD, BLK), jnp.float32),
             pltpu.VMEM((NQ, 2, BLK), jnp.float32),
         ],
         compiler_params=PARAMS,
-        cost_estimate=pl.CostEstimate(flops=16 * 5 * 2 * BLK * BLK * HD, bytes_accessed=4 << 20, transcendentals=16 * BLK * BLK),
-        name="grads",
-    )(info, qg, *kv, lohi, stats)
+        cost_estimate=pl.CostEstimate(flops=8 * 5 * 2 * BLK * BLK * HD, bytes_accessed=4 << 20, transcendentals=8 * BLK * BLK),
+        name="grads_before" if before else "grads_own",
+    )(info, qg, lohi, stats, *more)
 
 
 def per_device(queries, keys, values, grad_out, group_lengths):
@@ -321,16 +326,15 @@
     stats = stats_call(info, qg, kv, lohi)
     stats = exchange(stats, X_GROUPS)
 
-    dq, own_a, own_b, away_a, away_b = grads_call(info, qg, kv, lohi, stats)
+    dq, own_a, away_a = grads_call(False, info, qg, lohi, stats, *kv[:3])
+    got_a = partner(away_a, 2)
+    dq, own_b, away_b = grads_call(True, info, qg, lohi, stats, *kv[3:], dq)
+    away_b, got_a = lax.optimization_barrier((away_b, got_a))
 
     got_b = partner(away_b, 2)
     dq = exchange(dq, XC_GROUPS)
     mine_b, other_b = [(own_b[i] + got_b[i].astype(jnp.float32)).astype(bf16) for i in range(NC)]
-    mine_b, other_b, away_a = lax.optimization_barrier((mine_b, other_b, away_a))
-    next_mine = row_step(mine_b, -1)
-    other_b, dq = lax.optimization_barrier((other_b, dq))
-    next_other = row_step(other_b, -1, 1)
-    got_a = partner(away_a, 2)
+    next_mine, next_other = row_step(mine_b, -1), row_step(other_b, -1, 1)
     mate_a = partner((own_a[1] + got_a[1].astype(jnp.float32)).astype(bf16), 1)
     return pl.pallas_call(
         finish_kernel,

time: 88.5 us -> 94.6 us (1.069)
  the two profiles are of different devices: /device:TPU:247 before, /device:TPU:243 now
where the time goes in v6:
time: 94.6 us; the launch traced here: 94 us
  starting transfers between devices  48.4 us (51%)
  waiting for transfers between devices  20 us (21%)
  Pallas kernels  13 us (14%)
  blocking collectives  8.36 us (9%)
  other arithmetic  2.93 us (3%)
    ppermute x7, starting transfers between devices, partner(): return lax.ppermute(value, 'inner', [(i ^ flip, i) for i in range(ROW)])  19 us
    all_to_all x2, starting transfers between devices, exchange(): lax.all_to_all(value, 'inner', 0, 0, axis_index_groups=groups, tiled=True)  14.8 us
    ppermute x4, starting transfers between devices, row_step(): return lax.ppermute(value, ('outer', 'inner'), route)  14.5 us
    ppermute x4, waiting for transfers between devices, row_step(): return lax.ppermute(value, ('outer', 'inner'), route)  13.9 us
    all_to_all x1, blocking collectives, exchange(): lax.all_to_all(value, 'inner', 0, 0, axis_index_groups=groups, tiled=True)  8.36 us
    pallas_call x2, Pallas kernels, grads_call(): pl.pallas_call(functools.partial(grads_kernel, before), out_shape=(jax.Sh...  5.58 us
    ppermute x7, waiting for transfers between devices, partner(): return lax.ppermute(value, 'inner', [(i ^ flip, i) for i in range(ROW)])  5.3 us
    pallas_call x1, Pallas kernels, stats_call(): pl.pallas_call(stats_kernel, out_shape=jax.ShapeDtypeStruct((NX, NQ, 2, B...  2.71 us
  transfers between devices with their start and end apart: 13, of which 6 were waited for; matrix products, arithmetic and copies ran while one was open for 4% of the time, Pallas kernels for 4%

profile of v6, /device:TPU:243, one launch (start us, length us, event | category | flops | bytes accessed | tf_op | source)
XLA Modules:
  0.0 94.0 jit_solution(16293720594759908496)
XLA Ops:
  0.6 1.7 %split.1 = (bf16[256,256]{1,0:T(8,128)(2,1)}, bf16[256,256]{1,0:T(8,128)(2,1)}) custom-call(s32[1]{0:T(128)} %bitcast.info_ref, bf16[256,256]{1,0:T(8,128)(2,1)} %k_ref.1, bf16[256,256]{1,0:T(8,128)(2,1)} %v_ref.1), custom_call_target="tpu_custom_call" | custom-call | bytes 524288 | tf_op jit(solution)/shard_map/split/pallas_call | solution.py:292
  2.4 5.1 %collective-permute-start.3 = (bf16[256,256]{1,0:T(8,128)(2,1)}, bf16[256,256]{1,0:T(8,128)(2,1)S(1)}, u32[]{:S(2)}, u32[]{:S(2)}) collective-permute-start(bf16[256,256]{1,0:T(8,128)(2,1)} %get-tuple-element.16), channel_id=1, source_target_pairs={{0,17},{1,16},{2,19},{3,18},{4,21},{5,20},{6,23},{7,22},{8,25},{9,... | collective-permute-start | bytes 393224 | tf_op jit(solution)/shard_map/ppermute | solution.py:35
  7.4 1.9 %collective-permute-start = (bf16[256,256]{1,0:T(8,128)(2,1)}, bf16[256,256]{1,0:T(8,128)(2,1)S(1)}, u32[]{:S(2)}, u32[]{:S(2)}) collective-permute-start(bf16[256,256]{1,0:T(8,128)(2,1)} %get-tuple-element.16), channel_id=1, source_target_pairs={{1,0},{0,1},{3,2},{2,3},{5,4},{4,5},{7,6},{6,7},{9,8},{8,9},{11,10... | collective-permute-start | bytes 393224 | tf_op jit(solution)/shard_map/ppermute | solution.py:39
  9.4 4.2 %collective-permute-start.2 = (bf16[256,256]{1,0:T(8,128)(2,1)}, bf16[256,256]{1,0:T(8,128)(2,1)S(1)}, u32[]{:S(2)}, u32[]{:S(2)}) collective-permute-start(bf16[256,256]{1,0:T(8,128)(2,1)} %get-tuple-element.15.a0_ref.refs_0_), channel_id=1, source_target_pairs={{0,16},{1,17},{2,18},{3,19},{4,20},{5,21},{6,22},{7,23},{8,24},{9,... | collective-permute-start | bytes 393224 | tf_op jit(solution)/shard_map/ppermute | solution.py:35
  13.6 2.1 %pack.1 = bf16[8,256,256]{2,1,0:T(8,128)(2,1)} custom-call(bf16[256,256]{1,0:T(8,128)(2,1)} %q_ref.1, bf16[256,256]{1,0:T(8,128)(2,1)} %g_ref.1), custom_call_target="tpu_custom_call" | custom-call | bytes 1048576 | tf_op jit(solution)/shard_map/pack/pallas_call | solution.py:301
  15.7 5.4 %all-to-all-start = ((bf16[8,256,256]{2,1,0:T(8,128)(2,1)}), bf16[8,256,256]{2,1,0:T(8,128)(2,1)S(1)}, u32[]{:S(2)}, u32[]{:S(2)}) async-start(bf16[8,256,256]{2,1,0:T(8,128)(2,1)} %pack.1), calls=%async_computation | async-start | bytes 2097152 | tf_op jit(solution)/shard_map/all_to_all | solution.py:28
  21.1 0.1 add_multiply_fusion
  21.1 0.1 mul.44
  21.2 0.0 collective-permute-done.a1_ref.refs_1_
  21.3 3.2 %collective-permute-start.1 = (bf16[2,256,256]{2,1,0:T(8,128)(2,1)S(1)}, bf16[2,256,256]{2,1,0:T(8,128)(2,1)S(1)}, u32[]{:S(2)}, u32[]{:S(2)}) collective-permute-start(bf16[2,256,256]{2,1,0:T(8,128)(2,1)S(1)} %pad_maximum_fusion), channel_id=1, source_target_pairs={{2,0},{3,1},{0,2},{1,3},{6,4},{7,5},{4,6},{5,7},{10,8},{11,9},{8,1... | collective-permute-start | bytes 786440 | tf_op jit(solution)/shard_map/ppermute | solution.py:39
  24.5 0.1 iota_add_fusion
  24.5 0.0 collective-permute-done.3.b1_ref.refs_1_
  24.6 2.1 %collective-permute-start.5 = (bf16[256,256]{1,0:T(8,128)(2,1)S(1)}, bf16[256,256]{1,0:T(8,128)(2,1)S(1)}, u32[]{:S(2)}, u32[]{:S(2)}) collective-permute-start(bf16[256,256]{1,0:T(8,128)(2,1)S(1)} %collective-permute-done.3.b1_ref.refs_1_), channel_id=1, source_target_pairs={{2,0},{3,1},{0,2},{1,3},{6,4},{7,5},{4,6},{5,7},{10,8},{11,9},{8,1... | collective-permute-start | bytes 393224 | tf_op jit(solution)/shard_map/ppermute | solution.py:39
  26.6 0.0 collective-permute-done.2.b0_ref.refs_0_
  26.6 3.2 %collective-permute-start.4 = (bf16[256,256]{1,0:T(8,128)(2,1)S(1)}, bf16[256,256]{1,0:T(8,128)(2,1)S(1)}, u32[]{:S(2)}, u32[]{:S(2)}) collective-permute-start(bf16[256,256]{1,0:T(8,128)(2,1)S(1)} %collective-permute-done.2.b0_ref.refs_0_), channel_id=1, source_target_pairs={{2,0},{3,1},{0,2},{1,3},{6,4},{7,5},{4,6},{5,7},{10,8},{11,9},{8,1... | collective-permute-start | bytes 393224 | tf_op jit(solution)/shard_map/ppermute | solution.py:39
  29.9 0.8 collective-permute-done.1.a23_ref.refs_2_
  30.7 0.3 reduce-window.9
  31.0 0.1 slice.37
  31.1 0.1 slice_reduce_fusion.1
  31.2 0.1 fusion.7
  31.3 0.1 broadcast_add_fusion
  31.4 0.1 fusion.6
  31.4 1.1 %select_reduce_fusion.1 = s32[8,256]{1,0:T(8,128)S(1)} fusion(s32[254]{0:T(256)S(1)} %bitcast.23, s32[8,256]{1,0:T(8,128)S(1)} %iota_add_fusion, s32[254]{0:T(256)S(1)} %bitcast.22), kind=kLoop, calls=%fused_computation.1 | loop fusion | flops 1558528 | bytes 18416 | tf_op jit(solution)/shard_map/reduce_max | solution.py:51
  32.5 0.1 slice_reduce_fusion
  32.6 0.8 select_reduce_fusion
  33.5 0.2 fusion.3
  33.7 0.1 reshape_minimum_fusion
  33.8 0.1 concatenate.3.info_ref
  33.9 0.0 collective-permute-done.5.b3_ref.refs_3_
  33.9 2.4 %collective-permute-done.4.b2_ref.refs_2_ = bf16[256,256]{1,0:T(8,128)(2,1)S(1)} collective-permute-done((bf16[256,256]{1,0:T(8,128)(2,1)S(1)}, bf16[256,256]{1,0:T(8,128)(2,1)S(1)}, u32[]{:S(2)}, u32[]{:S(2)}) %collective-permute-start.4) | collective-permute-done | bytes 131104 | tf_op jit(solution)/shard_map/ppermute | solution.py:39
  36.3 0.0 all-to-all-done.qg_ref
  36.3 2.7 %stats.1 = f32[4,8,2,256]{3,2,1,0:T(2,128)S(1)} custom-call(s32[24]{0:T(128)S(1)} %concatenate.3.info_ref, bf16[8,256,256]{2,1,0:T(8,128)(2,1)S(1)} %all-to-all-done.qg_ref, bf16[256,256]{1,0:T(8,128)(2,1)S(1)} %copy-done, bf16[256,256]{1,0:T(8,128)(2,1)S(1)} %collective-permute-done.a1_ref.refs_1_, ...), custom_call_target="tpu_custom_call" | custom-call | flops 536870912 | bytes 2097152 | tf_op jit(solution)/shard_map/stats/pallas_call | solution.py:243
  39.0 8.4 %all_to_all.15.stats_ref = f32[4,8,2,256]{3,2,1,0:T(2,128)S(1)} all-to-all(f32[4,8,2,256]{3,2,1,0:T(2,128)S(1)} %stats.1), channel_id=1, replica_groups={{0,4,8,12},{1,5,9,13},{2,6,10,14},{3,7,11,15},{16,20,24,28},{17,21,25,2..., dimensions={0} | all-to-all | bytes 131072 | tf_op jit(solution)/shard_map/all_to_all | solution.py:28
  47.4 3.7 %grads_own.1 = (bf16[8,128,256]{2,1,0:T(8,128)(2,1)S(1)}, f32[2,256,256]{2,1,0:T(8,128)S(1)}, bf16[2,256,256]{2,1,0:T(8,128)(2,1)S(1)}) custom-call(s32[24]{0:T(128)S(1)} %concatenate.3.info_ref, bf16[8,256,256]{2,1,0:T(8,128)(2,1)S(1)} %all-to-all-done.qg_ref, s32[8,2,256]{2,1,0:T(2,128)S(1)} %pad_add_fusion.lohi_ref, ...), custom_call_target="tpu_custom_call" | custom-call | flops 671088640 | bytes 4194304 | tf_op jit(solution)/shard_map/grads_own/pallas_call | solution.py:261
  51.1 3.2 %collective-permute-start.6 = (bf16[2,256,256]{2,1,0:T(8,128)(2,1)S(1)}, bf16[2,256,256]{2,1,0:T(8,128)(2,1)S(1)}, u32[]{:S(2)}, u32[]{:S(2)}) collective-permute-start(bf16[2,256,256]{2,1,0:T(8,128)(2,1)S(1)} %get-tuple-element.22), channel_id=1, source_target_pairs={{2,0},{3,1},{0,2},{1,3},{6,4},{7,5},{4,6},{5,7},{10,8},{11,9},{8,1... | collective-permute-start | bytes 786440 | tf_op jit(solution)/shard_map/ppermute | solution.py:39
  54.3 1.9 %grads_before.1 = (bf16[8,128,256]{2,1,0:T(8,128)(2,1)}, f32[2,256,256]{2,1,0:T(8,128)S(1)}, bf16[2,256,256]{2,1,0:T(8,128)(2,1)S(1)}) custom-call(s32[24]{0:T(128)S(1)} %concatenate.3.info_ref, bf16[8,256,256]{2,1,0:T(8,128)(2,1)S(1)} %all-to-all-done.qg_ref, s32[8,2,256]{2,1,0:T(2,128)S(1)} %pad_add_fusion.lohi_ref, ...), custom_call_target="tpu_custom_call" | custom-call | flops 671088640 | bytes 4194304 | tf_op jit(solution)/shard_map/grads_before/pallas_call | solution.py:261
  56.1 2.1 %collective-permute-done.6.got_a_ref = bf16[2,256,256]{2,1,0:T(8,128)(2,1)S(1)} collective-permute-done((bf16[2,256,256]{2,1,0:T(8,128)(2,1)S(1)}, bf16[2,256,256]{2,1,0:T(8,128)(2,1)S(1)}, u32[]{:S(2)}, u32[]{:S(2)}) %collective-permute-start.6) | collective-permute-done | bytes 262176 | tf_op jit(solution)/shard_map/ppermute | solution.py:39
  58.2 3.2 %collective-permute-start.8 = (bf16[2,256,256]{2,1,0:T(8,128)(2,1)S(1)}, bf16[2,256,256]{2,1,0:T(8,128)(2,1)S(1)}, u32[]{:S(2)}, u32[]{:S(2)}) collective-permute-start(bf16[2,256,256]{2,1,0:T(8,128)(2,1)S(1)} %get-tuple-element.25), channel_id=1, source_target_pairs={{2,0},{3,1},{0,2},{1,3},{6,4},{7,5},{4,6},{5,7},{10,8},{11,9},{8,1... | collective-permute-start | bytes 786440 | tf_op jit(solution)/shard_map/ppermute | solution.py:39
  61.4 9.5 %all-to-all-start.2 = ((bf16[8,128,256]{2,1,0:T(8,128)(2,1)}), bf16[8,128,256]{2,1,0:T(8,128)(2,1)S(1)}, u32[]{:S(2)}, u32[]{:S(2)}) async-start(bf16[8,128,256]{2,1,0:T(8,128)(2,1)} %get-tuple-element.26), calls=%async_computation.2 | async-start | bytes 1048576 | tf_op jit(solution)/shard_map/all_to_all | solution.py:28
  70.9 2.3 %collective-permute-start.7 = (bf16[256,256]{1,0:T(8,128)(2,1)S(1)}, bf16[256,256]{1,0:T(8,128)(2,1)S(1)}, u32[]{:S(2)}, u32[]{:S(2)}) collective-permute-start(bf16[256,256]{1,0:T(8,128)(2,1)S(1)} %fusion), channel_id=1, source_target_pairs={{1,0},{0,1},{3,2},{2,3},{5,4},{4,5},{7,6},{6,7},{9,8},{8,9},{11,10... | collective-permute-start | bytes 393224 | tf_op jit(solution)/shard_map/ppermute | solution.py:39
  73.1 0.0 collective-permute-done.8
  73.2 0.1 fusion.2
  73.2 1.9 %collective-permute-start.10 = (bf16[256,256]{1,0:T(8,128)(2,1)S(1)}, bf16[256,256]{1,0:T(8,128)(2,1)S(1)}, u32[]{:S(2)}, u32[]{:S(2)}) collective-permute-start(bf16[256,256]{1,0:T(8,128)(2,1)S(1)} %get-tuple-element.27), channel_id=1, source_target_pairs={{16,1},{17,0},{18,3},{19,2},{20,5},{21,4},{22,7},{23,6},{24,9},{25... | collective-permute-start | bytes 393224 | tf_op jit(solution)/shard_map/ppermute | solution.py:35
  75.1 3.3 %collective-permute-start.9 = (bf16[256,256]{1,0:T(8,128)(2,1)S(1)}, bf16[256,256]{1,0:T(8,128)(2,1)S(1)}, u32[]{:S(2)}, u32[]{:S(2)}) collective-permute-start(bf16[256,256]{1,0:T(8,128)(2,1)S(1)} %get-tuple-element.28), channel_id=1, source_target_pairs={{16,0},{17,1},{18,2},{19,3},{20,4},{21,5},{22,6},{23,7},{24,8},{25... | collective-permute-start | bytes 393224 | tf_op jit(solution)/shard_map/ppermute | solution.py:35
  78.5 0.8 all-to-all-done.2.dq_ref
  79.2 10.3 %collective-permute-done.10.next_other_ref = bf16[256,256]{1,0:T(8,128)(2,1)S(1)} collective-permute-done((bf16[256,256]{1,0:T(8,128)(2,1)S(1)}, bf16[256,256]{1,0:T(8,128)(2,1)S(1)}, u32[]{:S(2)}, u32[]{:S(2)}) %collective-permute-start.10) | collective-permute-done | bytes 131104 | tf_op jit(solution)/shard_map/ppermute | solution.py:35
  89.5 3.6 %collective-permute-done.9.next_mine_ref = bf16[256,256]{1,0:T(8,128)(2,1)S(1)} collective-permute-done((bf16[256,256]{1,0:T(8,128)(2,1)S(1)}, bf16[256,256]{1,0:T(8,128)(2,1)S(1)}, u32[]{:S(2)}, u32[]{:S(2)}) %collective-permute-start.9) | collective-permute-done | bytes 131104 | tf_op jit(solution)/shard_map/ppermute | solution.py:35
  93.1 0.9 finish.1
  (13 shorter events, 0.2 us)
Async XLA Ops:
  2.4 22.2 %collective-permute-start.3 = (bf16[256,256]{1,0:T(8,128)(2,1)}, bf16[256,256]{1,0:T(8,128)(2,1)S(1)}, u32[]{:S(2)}, u32[]{:S(2)}) collective-permute-start(bf16[256,256]{1,0:T(8,128)(2,1)} %get-tuple-element.16), channel_id=1, source_target_pairs={{0,17},{1,16},{2,19},{3,18},{4,21},{5,20},{6,23},{7,22},{8,25},{9,... | collective-permute-start | bytes 393224 | tf_op jit(solution)/shard_map/ppermute | solution.py:35
  7.4 13.8 %collective-permute-start = (bf16[256,256]{1,0:T(8,128)(2,1)}, bf16[256,256]{1,0:T(8,128)(2,1)S(1)}, u32[]{:S(2)}, u32[]{:S(2)}) collective-permute-start(bf16[256,256]{1,0:T(8,128)(2,1)} %get-tuple-element.16), channel_id=1, source_target_pairs={{1,0},{0,1},{3,2},{2,3},{5,4},{4,5},{7,6},{6,7},{9,8},{8,9},{11,10... | collective-permute-start | bytes 393224 | tf_op jit(solution)/shard_map/ppermute | solution.py:39
  9.4 17.3 %collective-permute-start.2 = (bf16[256,256]{1,0:T(8,128)(2,1)}, bf16[256,256]{1,0:T(8,128)(2,1)S(1)}, u32[]{:S(2)}, u32[]{:S(2)}) collective-permute-start(bf16[256,256]{1,0:T(8,128)(2,1)} %get-tuple-element.15.a0_ref.refs_0_), channel_id=1, source_target_pairs={{0,16},{1,17},{2,18},{3,19},{4,20},{5,21},{6,22},{7,23},{8,24},{9,... | collective-permute-start | bytes 393224 | tf_op jit(solution)/shard_map/ppermute | solution.py:35
  15.7 5.6 %copy-start = (bf16[256,256]{1,0:T(8,128)(2,1)S(1)}, bf16[256,256]{1,0:T(8,128)(2,1)}, u32[]{:S(2)}) copy-start(bf16[256,256]{1,0:T(8,128)(2,1)} %get-tuple-element.15.a0_ref.refs_0_) | copy-start | bytes 393220
  15.7 15.0 %copy-start.1 = (s32[256]{0:T(256)S(1)}, s32[256]{0:T(256)}, u32[]{:S(2)}) copy-start(s32[256]{0:T(256)} %param.9) | copy-start | bytes 3076
  15.7 20.6 %all-to-all-start = ((bf16[8,256,256]{2,1,0:T(8,128)(2,1)}), bf16[8,256,256]{2,1,0:T(8,128)(2,1)S(1)}, u32[]{:S(2)}, u32[]{:S(2)}) async-start(bf16[8,256,256]{2,1,0:T(8,128)(2,1)} %pack.1), calls=%async_computation | async-start | bytes 2097152 | tf_op jit(solution)/shard_map/all_to_all | solution.py:28
  21.3 9.4 %collective-permute-start.1 = (bf16[2,256,256]{2,1,0:T(8,128)(2,1)S(1)}, bf16[2,256,256]{2,1,0:T(8,128)(2,1)S(1)}, u32[]{:S(2)}, u32[]{:S(2)}) collective-permute-start(bf16[2,256,256]{2,1,0:T(8,128)(2,1)S(1)} %pad_maximum_fusion), channel_id=1, source_target_pairs={{2,0},{3,1},{0,2},{1,3},{6,4},{7,5},{4,6},{5,7},{10,8},{11,9},{8,1... | collective-permute-start | bytes 786440 | tf_op jit(solution)/shard_map/ppermute | solution.py:39
  24.6 9.3 %collective-permute-start.5 = (bf16[256,256]{1,0:T(8,128)(2,1)S(1)}, bf16[256,256]{1,0:T(8,128)(2,1)S(1)}, u32[]{:S(2)}, u32[]{:S(2)}) collective-permute-start(bf16[256,256]{1,0:T(8,128)(2,1)S(1)} %collective-permute-done.3.b1_ref.refs_1_), channel_id=1, source_target_pairs={{2,0},{3,1},{0,2},{1,3},{6,4},{7,5},{4,6},{5,7},{10,8},{11,9},{8,1... | collective-permute-start | bytes 393224 | tf_op jit(solution)/shard_map/ppermute | solution.py:39
  26.6 9.7 %collective-permute-start.4 = (bf16[256,256]{1,0:T(8,128)(2,1)S(1)}, bf16[256,256]{1,0:T(8,128)(2,1)S(1)}, u32[]{:S(2)}, u32[]{:S(2)}) collective-permute-start(bf16[256,256]{1,0:T(8,128)(2,1)S(1)} %collective-permute-done.2.b0_ref.refs_0_), channel_id=1, source_target_pairs={{2,0},{3,1},{0,2},{1,3},{6,4},{7,5},{4,6},{5,7},{10,8},{11,9},{8,1... | collective-permute-start | bytes 393224 | tf_op jit(solution)/shard_map/ppermute | solution.py:39
  51.1 7.1 %collective-permute-start.6 = (bf16[2,256,256]{2,1,0:T(8,128)(2,1)S(1)}, bf16[2,256,256]{2,1,0:T(8,128)(2,1)S(1)}, u32[]{:S(2)}, u32[]{:S(2)}) collective-permute-start(bf16[2,256,256]{2,1,0:T(8,128)(2,1)S(1)} %get-tuple-element.22), channel_id=1, source_target_pairs={{2,0},{3,1},{0,2},{1,3},{6,4},{7,5},{4,6},{5,7},{10,8},{11,9},{8,1... | collective-permute-start | bytes 786440 | tf_op jit(solution)/shard_map/ppermute | solution.py:39
  58.2 14.9 %collective-permute-start.8 = (bf16[2,256,256]{2,1,0:T(8,128)(2,1)S(1)}, bf16[2,256,256]{2,1,0:T(8,128)(2,1)S(1)}, u32[]{:S(2)}, u32[]{:S(2)}) collective-permute-start(bf16[2,256,256]{2,1,0:T(8,128)(2,1)S(1)} %get-tuple-element.25), channel_id=1, source_target_pairs={{2,0},{3,1},{0,2},{1,3},{6,4},{7,5},{4,6},{5,7},{10,8},{11,9},{8,1... | collective-permute-start | bytes 786440 | tf_op jit(solution)/shard_map/ppermute | solution.py:39
  61.4 17.9 %all-to-all-start.2 = ((bf16[8,128,256]{2,1,0:T(8,128)(2,1)}), bf16[8,128,256]{2,1,0:T(8,128)(2,1)S(1)}, u32[]{:S(2)}, u32[]{:S(2)}) async-start(bf16[8,128,256]{2,1,0:T(8,128)(2,1)} %get-tuple-element.26), calls=%async_computation.2 | async-start | bytes 1048576 | tf_op jit(solution)/shard_map/all_to_all | solution.py:28
  70.9 7.6 %collective-permute-start.7 = (bf16[256,256]{1,0:T(8,128)(2,1)S(1)}, bf16[256,256]{1,0:T(8,128)(2,1)S(1)}, u32[]{:S(2)}, u32[]{:S(2)}) collective-permute-start(bf16[256,256]{1,0:T(8,128)(2,1)S(1)} %fusion), channel_id=1, source_target_pairs={{1,0},{0,1},{3,2},{2,3},{5,4},{4,5},{7,6},{6,7},{9,8},{8,9},{11,10... | collective-permute-start | bytes 393224 | tf_op jit(solution)/shard_map/ppermute | solution.py:39
  73.2 16.3 %collective-permute-start.10 = (bf16[256,256]{1,0:T(8,128)(2,1)S(1)}, bf16[256,256]{1,0:T(8,128)(2,1)S(1)}, u32[]{:S(2)}, u32[]{:S(2)}) collective-permute-start(bf16[256,256]{1,0:T(8,128)(2,1)S(1)} %get-tuple-element.27), channel_id=1, source_target_pairs={{16,1},{17,0},{18,3},{19,2},{20,5},{21,4},{22,7},{23,6},{24,9},{25... | collective-permute-start | bytes 393224 | tf_op jit(solution)/shard_map/ppermute | solution.py:35
  75.1 18.0 %collective-permute-start.9 = (bf16[256,256]{1,0:T(8,128)(2,1)S(1)}, bf16[256,256]{1,0:T(8,128)(2,1)S(1)}, u32[]{:S(2)}, u32[]{:S(2)}) collective-permute-start(bf16[256,256]{1,0:T(8,128)(2,1)S(1)} %get-tuple-element.28), channel_id=1, source_target_pairs={{16,0},{17,1},{18,2},{19,3},{20,4},{21,5},{22,6},{23,7},{24,8},{25... | collective-permute-start | bytes 393224 | tf_op jit(solution)/shard_map/ppermute | solution.py:35

commit v7 on v3

--- a/solution.py
+++ b/solution.py
@@ -92,8 +92,8 @@
     return n, rows, q, g, jnp.where(allowed, s, NEG), dp
 
 
-def split_kernel(info_ref, k_ref, v_ref, mine_ref, give_ref):
-    core = info_ref[0]
+def split_kernel(k_ref, v_ref, mine_ref, give_ref):
+    core = lax.rem(lax.axis_index("inner"), NC)
     for c in range(NC):
 
         @pl.when(core == c)
@@ -211,7 +211,7 @@
 ):
     core = info_ref[0]
     f32 = jnp.float32
-    mine = own_a_ref[0] + got_a_ref[0].astype(f32) + next_mine_ref[...].astype(f32)
+    mine = own_a_ref[0].astype(f32) + got_a_ref[0].astype(f32) + next_mine_ref[...].astype(f32)
     other = mate_a_ref[...].astype(f32) + next_other_ref[...].astype(f32)
     for c in range(NC):
 
@@ -255,8 +255,8 @@
         grads_kernel,
         out_shape=(
             jax.ShapeDtypeStruct((NQ, HD, BLK), jnp.bfloat16),
-            jax.ShapeDtypeStruct(part, jnp.float32),
-            jax.ShapeDtypeStruct(part, jnp.float32),
+            jax.ShapeDtypeStruct(part, jnp.bfloat16),
+            jax.ShapeDtypeStruct(part, jnp.bfloat16),
             jax.ShapeDtypeStruct(part, jnp.bfloat16),
             jax.ShapeDtypeStruct(part, jnp.bfloat16),
         ),
@@ -287,12 +287,12 @@
     mine, give = pl.pallas_call(
         split_kernel,
         out_shape=(jax.ShapeDtypeStruct((BLK, 2 * HD), bf16),) * 2,
-        in_specs=[SMEM] + [VMEM] * 2,
+        in_specs=[VMEM] * 2,
         out_specs=(VMEM,) * 2,
         compiler_params=big,
         cost_estimate=pl.CostEstimate(flops=0, bytes_accessed=1 << 19, transcendentals=0),
         name="split",
-    )(me, keys, values)
+    )(keys, values)
     qg = pl.pallas_call(
         pack_kernel,
         out_shape=jax.ShapeDtypeStruct((NQ, BLK, 2 * HD), bf16),
@@ -326,13 +326,13 @@
 
     got_b = partner(away_b, 2)
     dq = exchange(dq, XC_GROUPS)
-    mine_b, other_b = [(own_b[i] + got_b[i].astype(jnp.float32)).astype(bf16) for i in range(NC)]
+    mine_b, other_b = [(own_b[i].astype(jnp.float32) + got_b[i].astype(jnp.float32)).astype(bf16) for i in range(NC)]
     mine_b, other_b, away_a = lax.optimization_barrier((mine_b, other_b, away_a))
     next_mine = row_step(mine_b, -1)
     other_b, dq = lax.optimization_barrier((other_b, dq))
     next_other = row_step(other_b, -1, 1)
     got_a = partner(away_a, 2)
-    mate_a = partner((own_a[1] + got_a[1].astype(jnp.float32)).astype(bf16), 1)
+    mate_a = partner((own_a[1].astype(jnp.float32) + got_a[1].astype(jnp.float32)).astype(bf16), 1)
     return pl.pallas_call(
         finish_kernel,
         out_shape=(jax.ShapeDtypeStruct((BLK, HEADS * HD), bf16),) * 3,

time: 90.8 us -> 90.6 us (level)
  the two profiles are of different devices: /device:TPU:249 before, /device:TPU:241 now
where the time goes in v7:
time: 90.6 us; the launch traced here: 90.1 us
  starting transfers between devices  47.6 us (53%)
  waiting for transfers between devices  15.4 us (17%)
  Pallas kernels  15.2 us (17%)
  blocking collectives  7.39 us (8%)
  other arithmetic  2.96 us (3%)
    ppermute x7, starting transfers between devices, partner(): return lax.ppermute(value, 'inner', [(i ^ flip, i) for i in range(ROW)])  23.9 us
    ppermute x4, starting transfers between devices, row_step(): return lax.ppermute(value, ('outer', 'inner'), route)  12.5 us
    all_to_all x2, starting transfers between devices, exchange(): lax.all_to_all(value, 'inner', 0, 0, axis_index_groups=groups, tiled=True)  11.3 us
    all_to_all x1, blocking collectives, exchange(): lax.all_to_all(value, 'inner', 0, 0, axis_index_groups=groups, tiled=True)  7.39 us
    ppermute x4, waiting for transfers between devices, row_step(): return lax.ppermute(value, ('outer', 'inner'), route)  6.64 us
    pallas_call x1, Pallas kernels, grads_call(): pl.pallas_call(grads_kernel, out_shape=(jax.ShapeDtypeStruct((NQ, HD, BLK...  6.49 us
    all_to_all x2, waiting for transfers between devices, exchange(): lax.all_to_all(value, 'inner', 0, 0, axis_index_groups=groups, tiled=True)  4.93 us
    pallas_call x1, Pallas kernels, stats_call(): pl.pallas_call(stats_kernel, out_shape=jax.ShapeDtypeStruct((NX, NQ, 2, B...  4.01 us
  transfers between devices with their start and end apart: 13, of which 3 were waited for; matrix products, arithmetic and copies ran while one was open for 4% of the time, Pallas kernels for 2%

profile of v7, /device:TPU:241, one launch (start us, length us, event | category | flops | bytes accessed | tf_op | source)
XLA Modules:
  0.0 90.1 jit_solution(5401909946466464328)
XLA Ops:
  0.6 1.7 %split.1 = (bf16[256,256]{1,0:T(8,128)(2,1)}, bf16[256,256]{1,0:T(8,128)(2,1)}) custom-call(bf16[256,256]{1,0:T(8,128)(2,1)} %k_ref.1, bf16[256,256]{1,0:T(8,128)(2,1)} %v_ref.1), custom_call_target="tpu_custom_call" | custom-call | bytes 524288 | tf_op jit(solution)/shard_map/split/pallas_call | solution.py:287
  2.3 2.6 %collective-permute-start.2 = (bf16[256,256]{1,0:T(8,128)(2,1)}, bf16[256,256]{1,0:T(8,128)(2,1)S(1)}, u32[]{:S(2)}, u32[]{:S(2)}) collective-permute-start(bf16[256,256]{1,0:T(8,128)(2,1)} %get-tuple-element.17), channel_id=1, source_target_pairs={{1,0},{0,1},{3,2},{2,3},{5,4},{4,5},{7,6},{6,7},{9,8},{8,9},{11,10... | collective-permute-start | bytes 393224 | tf_op jit(solution)/shard_map/ppermute | solution.py:39
  4.9 4.4 %collective-permute-start = (bf16[256,256]{1,0:T(8,128)(2,1)}, bf16[256,256]{1,0:T(8,128)(2,1)S(1)}, u32[]{:S(2)}, u32[]{:S(2)}) collective-permute-start(bf16[256,256]{1,0:T(8,128)(2,1)} %get-tuple-element.17), channel_id=1, source_target_pairs={{0,17},{1,16},{2,19},{3,18},{4,21},{5,20},{6,23},{7,22},{8,25},{9,... | collective-permute-start | bytes 393224 | tf_op jit(solution)/shard_map/ppermute | solution.py:35
  9.4 4.2 %collective-permute-start.4 = (bf16[256,256]{1,0:T(8,128)(2,1)}, bf16[256,256]{1,0:T(8,128)(2,1)S(1)}, u32[]{:S(2)}, u32[]{:S(2)}) collective-permute-start(bf16[256,256]{1,0:T(8,128)(2,1)} %get-tuple-element.19.a0_ref), channel_id=1, source_target_pairs={{0,16},{1,17},{2,18},{3,19},{4,20},{5,21},{6,22},{7,23},{8,24},{9,... | collective-permute-start | bytes 393224 | tf_op jit(solution)/shard_map/ppermute | solution.py:35
  13.6 2.1 %pack.1 = bf16[8,256,256]{2,1,0:T(8,128)(2,1)} custom-call(bf16[256,256]{1,0:T(8,128)(2,1)} %q_ref.1, bf16[256,256]{1,0:T(8,128)(2,1)} %g_ref.1), custom_call_target="tpu_custom_call" | custom-call | bytes 1048576 | tf_op jit(solution)/shard_map/pack/pallas_call | solution.py:296
  15.7 5.2 %all-to-all-start = ((bf16[8,256,256]{2,1,0:T(8,128)(2,1)}), bf16[8,256,256]{2,1,0:T(8,128)(2,1)S(1)}, u32[]{:S(2)}, u32[]{:S(2)}) async-start(bf16[8,256,256]{2,1,0:T(8,128)(2,1)} %pack.1), calls=%async_computation | async-start | bytes 2097152 | tf_op jit(solution)/shard_map/all_to_all | solution.py:28
  20.9 0.1 add_multiply_fusion
  21.0 0.1 mul.44
  21.0 0.1 iota_add_fusion
  21.1 0.0 collective-permute-done.b1_ref
  21.1 3.2 %collective-permute-start.1 = (bf16[256,256]{1,0:T(8,128)(2,1)S(1)}, bf16[256,256]{1,0:T(8,128)(2,1)S(1)}, u32[]{:S(2)}, u32[]{:S(2)}) collective-permute-start(bf16[256,256]{1,0:T(8,128)(2,1)S(1)} %collective-permute-done.b1_ref), channel_id=1, source_target_pairs={{2,0},{3,1},{0,2},{1,3},{6,4},{7,5},{4,6},{5,7},{10,8},{11,9},{8,1... | collective-permute-start | bytes 393224 | tf_op jit(solution)/shard_map/ppermute | solution.py:39
  24.4 0.0 collective-permute-done.2.a1_ref
  24.4 2.1 %collective-permute-start.3 = (bf16[2,256,256]{2,1,0:T(8,128)(2,1)S(1)}, bf16[2,256,256]{2,1,0:T(8,128)(2,1)S(1)}, u32[]{:S(2)}, u32[]{:S(2)}) collective-permute-start(bf16[2,256,256]{2,1,0:T(8,128)(2,1)S(1)} %pad_maximum_fusion), channel_id=1, source_target_pairs={{2,0},{3,1},{0,2},{1,3},{6,4},{7,5},{4,6},{5,7},{10,8},{11,9},{8,1... | collective-permute-start | bytes 786440 | tf_op jit(solution)/shard_map/ppermute | solution.py:39
  26.5 0.0 collective-permute-done.4.b0_ref
  26.5 3.2 %collective-permute-start.5 = (bf16[256,256]{1,0:T(8,128)(2,1)S(1)}, bf16[256,256]{1,0:T(8,128)(2,1)S(1)}, u32[]{:S(2)}, u32[]{:S(2)}) collective-permute-start(bf16[256,256]{1,0:T(8,128)(2,1)S(1)} %collective-permute-done.4.b0_ref), channel_id=1, source_target_pairs={{2,0},{3,1},{0,2},{1,3},{6,4},{7,5},{4,6},{5,7},{10,8},{11,9},{8,1... | collective-permute-start | bytes 393224 | tf_op jit(solution)/shard_map/ppermute | solution.py:39
  29.7 0.0 collective-permute-done.1.b3_ref
  29.7 0.3 reduce-window.9
  30.1 0.1 slice.37
  30.2 0.1 slice_reduce_fusion.1
  30.3 0.1 fusion.7
  30.4 0.1 broadcast_add_fusion
  30.4 0.1 fusion.6
  30.5 1.1 %select_reduce_fusion.1 = s32[8,256]{1,0:T(8,128)S(1)} fusion(s32[254]{0:T(256)S(1)} %bitcast.23, s32[8,256]{1,0:T(8,128)S(1)} %iota_add_fusion, s32[254]{0:T(256)S(1)} %bitcast.22), kind=kLoop, calls=%fused_computation.1 | loop fusion | flops 1558528 | bytes 18416 | tf_op jit(solution)/shard_map/reduce_max | solution.py:51
  31.6 0.1 slice_reduce_fusion
  31.7 0.8 select_reduce_fusion
  32.5 0.2 fusion.3
  32.7 0.1 reshape_minimum_fusion
  32.8 0.1 concatenate.3.info_ref
  32.9 3.8 %collective-permute-done.5.b2_ref = bf16[256,256]{1,0:T(8,128)(2,1)S(1)} collective-permute-done((bf16[256,256]{1,0:T(8,128)(2,1)S(1)}, bf16[256,256]{1,0:T(8,128)(2,1)S(1)}, u32[]{:S(2)}, u32[]{:S(2)}) %collective-permute-start.5) | collective-permute-done | bytes 131104 | tf_op jit(solution)/shard_map/ppermute | solution.py:39
  36.7 0.0 collective-permute-done.3.a23_ref
  36.7 0.0 all-to-all-done.qg_ref
  36.7 4.0 %stats.1 = f32[4,8,2,256]{3,2,1,0:T(2,128)S(1)} custom-call(s32[24]{0:T(128)S(1)} %concatenate.3.info_ref, bf16[8,256,256]{2,1,0:T(8,128)(2,1)S(1)} %all-to-all-done.qg_ref, bf16[256,256]{1,0:T(8,128)(2,1)S(1)} %copy-done, bf16[256,256]{1,0:T(8,128)(2,1)S(1)} %collective-permute-done.2.a1_ref, bf16[2,256,256]{2,1,0:T(8,128)(2,1)S(1)} %collective-permute-done.3.a23_ref, ...), custom_call_target="tpu_custom_call" | custom-call | flops 536870912 | bytes 2097152 | tf_op jit(solution)/shard_map/stats/pallas_call | solution.py:236
  40.8 7.4 %all_to_all.15.stats_ref = f32[4,8,2,256]{3,2,1,0:T(2,128)S(1)} all-to-all(f32[4,8,2,256]{3,2,1,0:T(2,128)S(1)} %stats.1), channel_id=1, replica_groups={{0,4,8,12},{1,5,9,13},{2,6,10,14},{3,7,11,15},{16,20,24,28},{17,21,25,2..., dimensions={0} | all-to-all | bytes 131072 | tf_op jit(solution)/shard_map/all_to_all | solution.py:28
  48.2 6.5 %grads.1 = (bf16[8,128,256]{2,1,0:T(8,128)(2,1)}, bf16[2,256,256]{2,1,0:T(8,128)(2,1)S(1)}, bf16[2,256,256]{2,1,0:T(8,128)(2,1)S(1)}, bf16[2,256,256]{2,1,0:T(8,128)(2,1)S(1)}, bf16[2,256,256]{2,1,0:T(8,128)(2,1)S(1)}) custom-call(s32[24]{0:T(128)S(1)} %concatenate.3.info_ref, bf16[8,256,256]{2,1,0:T(8,128)(2,1)S(1)} %all-to-all-done.qg_ref, ...), custom_call_target="tpu_custom_call" | custom-call | flops 1342177280 | bytes 4194304 | tf_op jit(solution)/shard_map/grads/pallas_call | solution.py:254
  54.6 3.2 %collective-permute-start.6 = (bf16[2,256,256]{2,1,0:T(8,128)(2,1)S(1)}, bf16[2,256,256]{2,1,0:T(8,128)(2,1)S(1)}, u32[]{:S(2)}, u32[]{:S(2)}) collective-permute-start(bf16[2,256,256]{2,1,0:T(8,128)(2,1)S(1)} %get-tuple-element.23), channel_id=1, source_target_pairs={{2,0},{3,1},{0,2},{1,3},{6,4},{7,5},{4,6},{5,7},{10,8},{11,9},{8,1... | collective-permute-start | bytes 786440 | tf_op jit(solution)/shard_map/ppermute | solution.py:39
  57.9 6.1 %all-to-all-start.2 = ((bf16[8,128,256]{2,1,0:T(8,128)(2,1)}), bf16[8,128,256]{2,1,0:T(8,128)(2,1)S(1)}, u32[]{:S(2)}, u32[]{:S(2)}) async-start(bf16[8,128,256]{2,1,0:T(8,128)(2,1)} %get-tuple-element.28), calls=%async_computation.2 | async-start | bytes 1048576 | tf_op jit(solution)/shard_map/all_to_all | solution.py:28
  64.0 0.0 collective-permute-done.6
  64.0 0.1 fusion.1
  64.1 2.6 %collective-permute-start.7 = (bf16[2,256,256]{2,1,0:T(8,128)(2,1)S(1)}, bf16[2,256,256]{2,1,0:T(8,128)(2,1)S(1)}, u32[]{:S(2)}, u32[]{:S(2)}) collective-permute-start(bf16[2,256,256]{2,1,0:T(8,128)(2,1)S(1)} %get-tuple-element.25), channel_id=1, source_target_pairs={{2,0},{3,1},{0,2},{1,3},{6,4},{7,5},{4,6},{5,7},{10,8},{11,9},{8,1... | collective-permute-start | bytes 786440 | tf_op jit(solution)/shard_map/ppermute | solution.py:39
  66.6 1.9 %collective-permute-start.9 = (bf16[256,256]{1,0:T(8,128)(2,1)S(1)}, bf16[256,256]{1,0:T(8,128)(2,1)S(1)}, u32[]{:S(2)}, u32[]{:S(2)}) collective-permute-start(bf16[256,256]{1,0:T(8,128)(2,1)S(1)} %get-tuple-element.26), channel_id=1, source_target_pairs={{16,0},{17,1},{18,2},{19,3},{20,4},{21,5},{22,6},{23,7},{24,8},{25... | collective-permute-start | bytes 393224 | tf_op jit(solution)/shard_map/ppermute | solution.py:35
  68.6 4.9 %all-to-all-done.2.dq_ref = bf16[8,128,256]{2,1,0:T(8,128)(2,1)S(1)} async-done(((bf16[8,128,256]{2,1,0:T(8,128)(2,1)}), bf16[8,128,256]{2,1,0:T(8,128)(2,1)S(1)}, u32[]{:S(2)}, u32[]{:S(2)}) %all-to-all-start.2) | async-done | bytes 524320 | tf_op jit(solution)/shard_map/all_to_all | solution.py:28
  73.5 1.9 %collective-permute-start.10 = (bf16[256,256]{1,0:T(8,128)(2,1)S(1)}, bf16[256,256]{1,0:T(8,128)(2,1)S(1)}, u32[]{:S(2)}, u32[]{:S(2)}) collective-permute-start(bf16[256,256]{1,0:T(8,128)(2,1)S(1)} %get-tuple-element.29), channel_id=1, source_target_pairs={{16,1},{17,0},{18,3},{19,2},{20,5},{21,4},{22,7},{23,6},{24,9},{25... | collective-permute-start | bytes 393224 | tf_op jit(solution)/shard_map/ppermute | solution.py:35
  75.4 0.0 collective-permute-done.7.got_a_ref
  75.5 7.0 %collective-permute-start.8 = (bf16[256,256]{1,0:T(8,128)(2,1)S(1)}, bf16[256,256]{1,0:T(8,128)(2,1)S(1)}, u32[]{:S(2)}, u32[]{:S(2)}) collective-permute-start(bf16[256,256]{1,0:T(8,128)(2,1)S(1)} %fusion.2), channel_id=1, source_target_pairs={{1,0},{0,1},{3,2},{2,3},{5,4},{4,5},{7,6},{6,7},{9,8},{8,9},{11,10... | collective-permute-start | bytes 393224 | tf_op jit(solution)/shard_map/ppermute | solution.py:39
  82.5 0.0 collective-permute-done.9.next_mine_ref
  82.5 6.6 %collective-permute-done.10.next_other_ref = bf16[256,256]{1,0:T(8,128)(2,1)S(1)} collective-permute-done((bf16[256,256]{1,0:T(8,128)(2,1)S(1)}, bf16[256,256]{1,0:T(8,128)(2,1)S(1)}, u32[]{:S(2)}, u32[]{:S(2)}) %collective-permute-start.10) | collective-permute-done | bytes 131104 | tf_op jit(solution)/shard_map/ppermute | solution.py:35
  89.1 0.0 collective-permute-done.8.mate_a_ref
  89.1 0.9 %finish.1 = (bf16[256,256]{1,0:T(8,128)(2,1)}, bf16[256,256]{1,0:T(8,128)(2,1)}, bf16[256,256]{1,0:T(8,128)(2,1)}) custom-call(s32[1]{0:T(128)} %bitcast.info_ref, bf16[2,256,256]{2,1,0:T(8,128)(2,1)S(1)} %get-tuple-element.21.own_a_ref, bf16[2,256,256]{2,1,0:T(8,128)(2,1)S(1)} %collective-permute-done.7.got_a_ref, ...), custom_call_target="tpu_custom_call" | custom-call | bytes 2097152 | tf_op jit(solution)/shard_map/finish/pallas_call | solution.py:336
  (12 shorter events, 0.2 us)
Async XLA Ops:
  2.3 22.0 %collective-permute-start.2 = (bf16[256,256]{1,0:T(8,128)(2,1)}, bf16[256,256]{1,0:T(8,128)(2,1)S(1)}, u32[]{:S(2)}, u32[]{:S(2)}) collective-permute-start(bf16[256,256]{1,0:T(8,128)(2,1)} %get-tuple-element.17), channel_id=1, source_target_pairs={{1,0},{0,1},{3,2},{2,3},{5,4},{4,5},{7,6},{6,7},{9,8},{8,9},{11,10... | collective-permute-start | bytes 393224 | tf_op jit(solution)/shard_map/ppermute | solution.py:39
  4.9 16.2 %collective-permute-start = (bf16[256,256]{1,0:T(8,128)(2,1)}, bf16[256,256]{1,0:T(8,128)(2,1)S(1)}, u32[]{:S(2)}, u32[]{:S(2)}) collective-permute-start(bf16[256,256]{1,0:T(8,128)(2,1)} %get-tuple-element.17), channel_id=1, source_target_pairs={{0,17},{1,16},{2,19},{3,18},{4,21},{5,20},{6,23},{7,22},{8,25},{9,... | collective-permute-start | bytes 393224 | tf_op jit(solution)/shard_map/ppermute | solution.py:35
  9.4 17.1 %collective-permute-start.4 = (bf16[256,256]{1,0:T(8,128)(2,1)}, bf16[256,256]{1,0:T(8,128)(2,1)S(1)}, u32[]{:S(2)}, u32[]{:S(2)}) collective-permute-start(bf16[256,256]{1,0:T(8,128)(2,1)} %get-tuple-element.19.a0_ref), channel_id=1, source_target_pairs={{0,16},{1,17},{2,18},{3,19},{4,20},{5,21},{6,22},{7,23},{8,24},{9,... | collective-permute-start | bytes 393224 | tf_op jit(solution)/shard_map/ppermute | solution.py:35
  15.7 8.7 %copy-start = (bf16[256,256]{1,0:T(8,128)(2,1)S(1)}, bf16[256,256]{1,0:T(8,128)(2,1)}, u32[]{:S(2)}) copy-start(bf16[256,256]{1,0:T(8,128)(2,1)} %get-tuple-element.19.a0_ref) | copy-start | bytes 393220
  15.7 14.1 %copy-start.1 = (s32[256]{0:T(256)S(1)}, s32[256]{0:T(256)}, u32[]{:S(2)}) copy-start(s32[256]{0:T(256)} %param.9) | copy-start | bytes 3076
  15.7 21.1 %all-to-all-start = ((bf16[8,256,256]{2,1,0:T(8,128)(2,1)}), bf16[8,256,256]{2,1,0:T(8,128)(2,1)S(1)}, u32[]{:S(2)}, u32[]{:S(2)}) async-start(bf16[8,256,256]{2,1,0:T(8,128)(2,1)} %pack.1), calls=%async_computation | async-start | bytes 2097152 | tf_op jit(solution)/shard_map/all_to_all | solution.py:28
  21.1 8.6 %collective-permute-start.1 = (bf16[256,256]{1,0:T(8,128)(2,1)S(1)}, bf16[256,256]{1,0:T(8,128)(2,1)S(1)}, u32[]{:S(2)}, u32[]{:S(2)}) collective-permute-start(bf16[256,256]{1,0:T(8,128)(2,1)S(1)} %collective-permute-done.b1_ref), channel_id=1, source_target_pairs={{2,0},{3,1},{0,2},{1,3},{6,4},{7,5},{4,6},{5,7},{10,8},{11,9},{8,1... | collective-permute-start | bytes 393224 | tf_op jit(solution)/shard_map/ppermute | solution.py:39
  24.4 12.3 %collective-permute-start.3 = (bf16[2,256,256]{2,1,0:T(8,128)(2,1)S(1)}, bf16[2,256,256]{2,1,0:T(8,128)(2,1)S(1)}, u32[]{:S(2)}, u32[]{:S(2)}) collective-permute-start(bf16[2,256,256]{2,1,0:T(8,128)(2,1)S(1)} %pad_maximum_fusion), channel_id=1, source_target_pairs={{2,0},{3,1},{0,2},{1,3},{6,4},{7,5},{4,6},{5,7},{10,8},{11,9},{8,1... | collective-permute-start | bytes 786440 | tf_op jit(solution)/shard_map/ppermute | solution.py:39
  26.5 10.2 %collective-permute-start.5 = (bf16[256,256]{1,0:T(8,128)(2,1)S(1)}, bf16[256,256]{1,0:T(8,128)(2,1)S(1)}, u32[]{:S(2)}, u32[]{:S(2)}) collective-permute-start(bf16[256,256]{1,0:T(8,128)(2,1)S(1)} %collective-permute-done.4.b0_ref), channel_id=1, source_target_pairs={{2,0},{3,1},{0,2},{1,3},{6,4},{7,5},{4,6},{5,7},{10,8},{11,9},{8,1... | collective-permute-start | bytes 393224 | tf_op jit(solution)/shard_map/ppermute | solution.py:39
  54.6 9.3 %collective-permute-start.6 = (bf16[2,256,256]{2,1,0:T(8,128)(2,1)S(1)}, bf16[2,256,256]{2,1,0:T(8,128)(2,1)S(1)}, u32[]{:S(2)}, u32[]{:S(2)}) collective-permute-start(bf16[2,256,256]{2,1,0:T(8,128)(2,1)S(1)} %get-tuple-element.23), channel_id=1, source_target_pairs={{2,0},{3,1},{0,2},{1,3},{6,4},{7,5},{4,6},{5,7},{10,8},{11,9},{8,1... | collective-permute-start | bytes 786440 | tf_op jit(solution)/shard_map/ppermute | solution.py:39
  57.9 15.6 %all-to-all-start.2 = ((bf16[8,128,256]{2,1,0:T(8,128)(2,1)}), bf16[8,128,256]{2,1,0:T(8,128)(2,1)S(1)}, u32[]{:S(2)}, u32[]{:S(2)}) async-start(bf16[8,128,256]{2,1,0:T(8,128)(2,1)} %get-tuple-element.28), calls=%async_computation.2 | async-start | bytes 1048576 | tf_op jit(solution)/shard_map/all_to_all | solution.py:28
  64.1 11.3 %collective-permute-start.7 = (bf16[2,256,256]{2,1,0:T(8,128)(2,1)S(1)}, bf16[2,256,256]{2,1,0:T(8,128)(2,1)S(1)}, u32[]{:S(2)}, u32[]{:S(2)}) collective-permute-start(bf16[2,256,256]{2,1,0:T(8,128)(2,1)S(1)} %get-tuple-element.25), channel_id=1, source_target_pairs={{2,0},{3,1},{0,2},{1,3},{6,4},{7,5},{4,6},{5,7},{10,8},{11,9},{8,1... | collective-permute-start | bytes 786440 | tf_op jit(solution)/shard_map/ppermute | solution.py:39
  66.6 15.9 %collective-permute-start.9 = (bf16[256,256]{1,0:T(8,128)(2,1)S(1)}, bf16[256,256]{1,0:T(8,128)(2,1)S(1)}, u32[]{:S(2)}, u32[]{:S(2)}) collective-permute-start(bf16[256,256]{1,0:T(8,128)(2,1)S(1)} %get-tuple-element.26), channel_id=1, source_target_pairs={{16,0},{17,1},{18,2},{19,3},{20,4},{21,5},{22,6},{23,7},{24,8},{25... | collective-permute-start | bytes 393224 | tf_op jit(solution)/shard_map/ppermute | solution.py:35
  73.5 15.6 %collective-permute-start.10 = (bf16[256,256]{1,0:T(8,128)(2,1)S(1)}, bf16[256,256]{1,0:T(8,128)(2,1)S(1)}, u32[]{:S(2)}, u32[]{:S(2)}) collective-permute-start(bf16[256,256]{1,0:T(8,128)(2,1)S(1)} %get-tuple-element.29), channel_id=1, source_target_pairs={{16,1},{17,0},{18,3},{19,2},{20,5},{21,4},{22,7},{23,6},{24,9},{25... | collective-permute-start | bytes 393224 | tf_op jit(solution)/shard_map/ppermute | solution.py:35
  75.5 13.7 %collective-permute-start.8 = (bf16[256,256]{1,0:T(8,128)(2,1)S(1)}, bf16[256,256]{1,0:T(8,128)(2,1)S(1)}, u32[]{:S(2)}, u32[]{:S(2)}) collective-permute-start(bf16[256,256]{1,0:T(8,128)(2,1)S(1)} %fusion.2), channel_id=1, source_target_pairs={{1,0},{0,1},{3,2},{2,3},{5,4},{4,5},{7,6},{6,7},{9,8},{8,9},{11,10... | collective-permute-start | bytes 393224 | tf_op jit(solution)/shard_map/ppermute | solution.py:39

commit v8 on v3

--- a/solution.py
+++ b/solution.py
@@ -206,8 +206,14 @@
                 out_ref[i, :, HD:] = acc_ref[rows, HD:].astype(out_ref.dtype)
 
 
-def finish_kernel(
-    info_ref, own_a_ref, got_a_ref, mate_a_ref, next_mine_ref, next_other_ref, dq_ref, grad_q_ref, grad_k_ref, grad_v_ref
+def finish_q_kernel(dq_ref, grad_q_ref):
+    for h in range(HEADS):
+        dq = sum(dq_ref[i * HEADS + h].astype(jnp.float32) for i in range(NX))
+        grad_q_ref[:, h * HD : (h + 1) * HD] = dq.T.astype(jnp.bfloat16)
+
+
+def finish_kv_kernel(
+    info_ref, own_a_ref, got_a_ref, mate_a_ref, next_mine_ref, next_other_ref, grad_k_ref, grad_v_ref
 ):
     core = info_ref[0]
     f32 = jnp.float32
@@ -221,10 +227,6 @@
                 cols = slice(h * HD, (h + 1) * HD)
                 grad_k_ref[:, cols] = part[:, :HD].astype(jnp.bfloat16)
                 grad_v_ref[:, cols] = part[:, HD:].astype(jnp.bfloat16)
-
-    for h in range(HEADS):
-        dq = sum(dq_ref[i * HEADS + h].astype(f32) for i in range(NX))
-        grad_q_ref[:, h * HD : (h + 1) * HD] = dq.T.astype(jnp.bfloat16)
 
 
 SMEM = pl.BlockSpec(memory_space=pltpu.SMEM)
@@ -333,15 +335,26 @@
     next_other = row_step(other_b, -1, 1)
     got_a = partner(away_a, 2)
     mate_a = partner((own_a[1] + got_a[1].astype(jnp.float32)).astype(bf16), 1)
-    return pl.pallas_call(
-        finish_kernel,
-        out_shape=(jax.ShapeDtypeStruct((BLK, HEADS * HD), bf16),) * 3,
-        in_specs=[SMEM] + [VMEM] * 6,
-        out_specs=(VMEM,) * 3,
+    whole = jax.ShapeDtypeStruct((BLK, HEADS * HD), bf16)
+    grad_q = pl.pallas_call(
+        finish_q_kernel,
+        out_shape=whole,
+        in_specs=[VMEM],
+        out_specs=VMEM,
+        compiler_params=PARAMS,
+        cost_estimate=pl.CostEstimate(flops=0, bytes_accessed=1 << 20, transcendentals=0),
+        name="finish_q",
+    )(dq)
+    grad_k, grad_v = pl.pallas_call(
+        finish_kv_kernel,
+        out_shape=(whole, whole),
+        in_specs=[SMEM] + [VMEM] * 5,
+        out_specs=(VMEM,) * 2,
         compiler_params=PARAMS,
         cost_estimate=pl.CostEstimate(flops=0, bytes_accessed=2 << 20, transcendentals=0),
-        name="finish",
-    )(me, own_a, got_a, mate_a, next_mine, next_other, dq)
+        name="finish_kv",
+    )(me, own_a, got_a, mate_a, next_mine, next_other)
+    return grad_q, grad_k, grad_v
 
 
 def solution(mesh):

time: 90.8 us -> 88.9 us (0.979)
  the two profiles are of different devices: /device:TPU:249 before, /device:TPU:241 now
where the time goes in v8:
time: 88.9 us; the launch traced here: 88.4 us
  starting transfers between devices  47.1 us (53%)
  waiting for transfers between devices  15.5 us (17%)
  Pallas kernels  13 us (15%)
  blocking collectives  8.39 us (9%)
  other arithmetic  2.94 us (3%)
  between operations  0.89 us (1%)
    ppermute x7, starting transfers between devices, partner(): return lax.ppermute(value, 'inner', [(i ^ flip, i) for i in range(ROW)])  22.6 us
    ppermute x4, starting transfers between devices, row_step(): return lax.ppermute(value, ('outer', 'inner'), route)  13.2 us
    all_to_all x2, starting transfers between devices, exchange(): lax.all_to_all(value, 'inner', 0, 0, axis_index_groups=groups, tiled=True)  11.3 us
    all_to_all x1, blocking collectives, exchange(): lax.all_to_all(value, 'inner', 0, 0, axis_index_groups=groups, tiled=True)  8.39 us
    ppermute x4, waiting for transfers between devices, row_step(): return lax.ppermute(value, ('outer', 'inner'), route)  6.57 us
    all_to_all x2, waiting for transfers between devices, exchange(): lax.all_to_all(value, 'inner', 0, 0, axis_index_groups=groups, tiled=True)  5.17 us
    pallas_call x1, Pallas kernels, grads_call(): pl.pallas_call(grads_kernel, out_shape=(jax.ShapeDtypeStruct((NQ, HD, BLK...  4.86 us
    ppermute x7, waiting for transfers between devices, partner(): return lax.ppermute(value, 'inner', [(i ^ flip, i) for i in range(ROW)])  3.81 us
  transfers between devices with their start and end apart: 13, of which 3 were waited for; matrix products, arithmetic and copies ran while one was open for 4% of the time, Pallas kernels for 3%

profile of v8, /device:TPU:241, one launch (start us, length us, event | category | flops | bytes accessed | tf_op | source)
XLA Modules:
  0.0 88.4 jit_solution(3308492320280241286)
XLA Ops:
  0.6 1.7 %split.1 = (bf16[256,256]{1,0:T(8,128)(2,1)}, bf16[256,256]{1,0:T(8,128)(2,1)}) custom-call(s32[1]{0:T(128)} %bitcast.4.info_ref, bf16[256,256]{1,0:T(8,128)(2,1)} %k_ref.1, bf16[256,256]{1,0:T(8,128)(2,1)} %v_ref.1), custom_call_target="tpu_custom_call" | custom-call | bytes 524288 | tf_op jit(solution)/shard_map/split/pallas_call | solution.py:289
  2.4 2.6 %collective-permute-start.2 = (bf16[256,256]{1,0:T(8,128)(2,1)}, bf16[256,256]{1,0:T(8,128)(2,1)S(1)}, u32[]{:S(2)}, u32[]{:S(2)}) collective-permute-start(bf16[256,256]{1,0:T(8,128)(2,1)} %get-tuple-element.19), channel_id=1, source_target_pairs={{1,0},{0,1},{3,2},{2,3},{5,4},{4,5},{7,6},{6,7},{9,8},{8,9},{11,10... | collective-permute-start | bytes 393224 | tf_op jit(solution)/shard_map/ppermute | solution.py:39
  4.9 4.4 %collective-permute-start = (bf16[256,256]{1,0:T(8,128)(2,1)}, bf16[256,256]{1,0:T(8,128)(2,1)S(1)}, u32[]{:S(2)}, u32[]{:S(2)}) collective-permute-start(bf16[256,256]{1,0:T(8,128)(2,1)} %get-tuple-element.19), channel_id=1, source_target_pairs={{0,17},{1,16},{2,19},{3,18},{4,21},{5,20},{6,23},{7,22},{8,25},{9,... | collective-permute-start | bytes 393224 | tf_op jit(solution)/shard_map/ppermute | solution.py:35
  9.4 4.2 %collective-permute-start.4 = (bf16[256,256]{1,0:T(8,128)(2,1)}, bf16[256,256]{1,0:T(8,128)(2,1)S(1)}, u32[]{:S(2)}, u32[]{:S(2)}) collective-permute-start(bf16[256,256]{1,0:T(8,128)(2,1)} %get-tuple-element.21.a0_ref), channel_id=1, source_target_pairs={{0,16},{1,17},{2,18},{3,19},{4,20},{5,21},{6,22},{7,23},{8,24},{9,... | collective-permute-start | bytes 393224 | tf_op jit(solution)/shard_map/ppermute | solution.py:35
  13.6 2.1 %pack.1 = bf16[8,256,256]{2,1,0:T(8,128)(2,1)} custom-call(bf16[256,256]{1,0:T(8,128)(2,1)} %q_ref.1, bf16[256,256]{1,0:T(8,128)(2,1)} %g_ref.1), custom_call_target="tpu_custom_call" | custom-call | bytes 1048576 | tf_op jit(solution)/shard_map/pack/pallas_call | solution.py:298
  15.7 5.2 %all-to-all-start = ((bf16[8,256,256]{2,1,0:T(8,128)(2,1)}), bf16[8,256,256]{2,1,0:T(8,128)(2,1)S(1)}, u32[]{:S(2)}, u32[]{:S(2)}) async-start(bf16[8,256,256]{2,1,0:T(8,128)(2,1)} %pack.1), calls=%async_computation | async-start | bytes 2097152 | tf_op jit(solution)/shard_map/all_to_all | solution.py:28
  20.9 0.1 add_multiply_fusion
  21.0 0.1 mul.44
  21.0 0.1 iota_add_fusion
  21.1 0.0 collective-permute-done.b1_ref
  21.1 3.2 %collective-permute-start.1 = (bf16[256,256]{1,0:T(8,128)(2,1)S(1)}, bf16[256,256]{1,0:T(8,128)(2,1)S(1)}, u32[]{:S(2)}, u32[]{:S(2)}) collective-permute-start(bf16[256,256]{1,0:T(8,128)(2,1)S(1)} %collective-permute-done.b1_ref), channel_id=1, source_target_pairs={{2,0},{3,1},{0,2},{1,3},{6,4},{7,5},{4,6},{5,7},{10,8},{11,9},{8,1... | collective-permute-start | bytes 393224 | tf_op jit(solution)/shard_map/ppermute | solution.py:39
  24.4 0.0 collective-permute-done.2.a1_ref
  24.4 2.1 %collective-permute-start.3 = (bf16[2,256,256]{2,1,0:T(8,128)(2,1)S(1)}, bf16[2,256,256]{2,1,0:T(8,128)(2,1)S(1)}, u32[]{:S(2)}, u32[]{:S(2)}) collective-permute-start(bf16[2,256,256]{2,1,0:T(8,128)(2,1)S(1)} %pad_maximum_fusion), channel_id=1, source_target_pairs={{2,0},{3,1},{0,2},{1,3},{6,4},{7,5},{4,6},{5,7},{10,8},{11,9},{8,1... | collective-permute-start | bytes 786440 | tf_op jit(solution)/shard_map/ppermute | solution.py:39
  26.5 0.0 collective-permute-done.4.b0_ref
  26.5 3.2 %collective-permute-start.5 = (bf16[256,256]{1,0:T(8,128)(2,1)S(1)}, bf16[256,256]{1,0:T(8,128)(2,1)S(1)}, u32[]{:S(2)}, u32[]{:S(2)}) collective-permute-start(bf16[256,256]{1,0:T(8,128)(2,1)S(1)} %collective-permute-done.4.b0_ref), channel_id=1, source_target_pairs={{2,0},{3,1},{0,2},{1,3},{6,4},{7,5},{4,6},{5,7},{10,8},{11,9},{8,1... | collective-permute-start | bytes 393224 | tf_op jit(solution)/shard_map/ppermute | solution.py:39
  29.7 0.0 collective-permute-done.1.b3_ref
  29.7 0.3 reduce-window.9
  30.1 0.1 slice.37
  30.2 0.1 slice_reduce_fusion.1
  30.3 0.1 fusion.7
  30.4 0.1 broadcast_add_fusion
  30.4 0.1 fusion.6
  30.5 1.1 %select_reduce_fusion.1 = s32[8,256]{1,0:T(8,128)S(1)} fusion(s32[254]{0:T(256)S(1)} %bitcast.23, s32[8,256]{1,0:T(8,128)S(1)} %iota_add_fusion, s32[254]{0:T(256)S(1)} %bitcast.22), kind=kLoop, calls=%fused_computation.1 | loop fusion | flops 1558528 | bytes 18416 | tf_op jit(solution)/shard_map/reduce_max | solution.py:51
  31.6 0.1 slice_reduce_fusion
  31.7 0.8 select_reduce_fusion
  32.5 0.2 fusion.3
  32.7 0.1 reshape_minimum_fusion
  32.8 0.1 concatenate.3.info_ref
  32.9 3.8 %collective-permute-done.5.b2_ref = bf16[256,256]{1,0:T(8,128)(2,1)S(1)} collective-permute-done((bf16[256,256]{1,0:T(8,128)(2,1)S(1)}, bf16[256,256]{1,0:T(8,128)(2,1)S(1)}, u32[]{:S(2)}, u32[]{:S(2)}) %collective-permute-start.5) | collective-permute-done | bytes 131104 | tf_op jit(solution)/shard_map/ppermute | solution.py:39
  36.7 0.0 collective-permute-done.3.a23_ref
  36.7 0.0 all-to-all-done.qg_ref
  36.7 2.7 %stats.1 = f32[4,8,2,256]{3,2,1,0:T(2,128)S(1)} custom-call(s32[24]{0:T(128)S(1)} %concatenate.3.info_ref, bf16[8,256,256]{2,1,0:T(8,128)(2,1)S(1)} %all-to-all-done.qg_ref, bf16[256,256]{1,0:T(8,128)(2,1)S(1)} %copy-done, bf16[256,256]{1,0:T(8,128)(2,1)S(1)} %collective-permute-done.2.a1_ref, bf16[2,256,256]{2,1,0:T(8,128)(2,1)S(1)} %collective-permute-done.3.a23_ref, ...), custom_call_target="tpu_custom_call" | custom-call | flops 536870912 | bytes 2097152 | tf_op jit(solution)/shard_map/stats/pallas_call | solution.py:238
  39.5 8.4 %all_to_all.15.stats_ref = f32[4,8,2,256]{3,2,1,0:T(2,128)S(1)} all-to-all(f32[4,8,2,256]{3,2,1,0:T(2,128)S(1)} %stats.1), channel_id=1, replica_groups={{0,4,8,12},{1,5,9,13},{2,6,10,14},{3,7,11,15},{16,20,24,28},{17,21,25,2..., dimensions={0} | all-to-all | bytes 131072 | tf_op jit(solution)/shard_map/all_to_all | solution.py:28
  47.9 4.9 %grads.1 = (bf16[8,128,256]{2,1,0:T(8,128)(2,1)}, f32[2,256,256]{2,1,0:T(8,128)S(1)}, f32[2,256,256]{2,1,0:T(8,128)S(1)}, bf16[2,256,256]{2,1,0:T(8,128)(2,1)S(1)}, bf16[2,256,256]{2,1,0:T(8,128)(2,1)}) custom-call(s32[24]{0:T(128)S(1)} %concatenate.3.info_ref, bf16[8,256,256]{2,1,0:T(8,128)(2,1)S(1)} %all-to-all-done.qg_ref, bf16[256,256]{1,0:T(8,128)(2,1)S(1)} %copy-done, ...), custom_call_target="tpu_custom_call" | custom-call | flops 1342177280 | bytes 4194304 | tf_op jit(solution)/shard_map/grads/pallas_call | solution.py:256
  52.7 4.1 %collective-permute-start.6 = (bf16[2,256,256]{2,1,0:T(8,128)(2,1)}, bf16[2,256,256]{2,1,0:T(8,128)(2,1)S(1)}, u32[]{:S(2)}, u32[]{:S(2)}) collective-permute-start(bf16[2,256,256]{2,1,0:T(8,128)(2,1)} %get-tuple-element.24), channel_id=1, source_target_pairs={{2,0},{3,1},{0,2},{1,3},{6,4},{7,5},{4,6},{5,7},{10,8},{11,9},{8,1... | collective-permute-start | bytes 786440 | tf_op jit(solution)/shard_map/ppermute | solution.py:39
  56.8 6.1 %all-to-all-start.2 = ((bf16[8,128,256]{2,1,0:T(8,128)(2,1)}), bf16[8,128,256]{2,1,0:T(8,128)(2,1)S(1)}, u32[]{:S(2)}, u32[]{:S(2)}) async-start(bf16[8,128,256]{2,1,0:T(8,128)(2,1)} %get-tuple-element.27), calls=%async_computation.2 | async-start | bytes 1048576 | tf_op jit(solution)/shard_map/all_to_all | solution.py:28
  62.9 0.0 collective-permute-done.6
  63.0 0.1 fusion.1
  63.0 1.9 %collective-permute-start.7 = (bf16[2,256,256]{2,1,0:T(8,128)(2,1)S(1)}, bf16[2,256,256]{2,1,0:T(8,128)(2,1)S(1)}, u32[]{:S(2)}, u32[]{:S(2)}) collective-permute-start(bf16[2,256,256]{2,1,0:T(8,128)(2,1)S(1)} %get-tuple-element.30), channel_id=1, source_target_pairs={{2,0},{3,1},{0,2},{1,3},{6,4},{7,5},{4,6},{5,7},{10,8},{11,9},{8,1... | collective-permute-start | bytes 786440 | tf_op jit(solution)/shard_map/ppermute | solution.py:39
  64.9 2.3 %collective-permute-start.9 = (bf16[256,256]{1,0:T(8,128)(2,1)S(1)}, bf16[256,256]{1,0:T(8,128)(2,1)S(1)}, u32[]{:S(2)}, u32[]{:S(2)}) collective-permute-start(bf16[256,256]{1,0:T(8,128)(2,1)S(1)} %get-tuple-element.31), channel_id=1, source_target_pairs={{16,0},{17,1},{18,2},{19,3},{20,4},{21,5},{22,6},{23,7},{24,8},{25... | collective-permute-start | bytes 393224 | tf_op jit(solution)/shard_map/ppermute | solution.py:35
  67.3 5.2 %all-to-all-done.2.dq_ref = bf16[8,128,256]{2,1,0:T(8,128)(2,1)S(1)} async-done(((bf16[8,128,256]{2,1,0:T(8,128)(2,1)}), bf16[8,128,256]{2,1,0:T(8,128)(2,1)S(1)}, u32[]{:S(2)}, u32[]{:S(2)}) %all-to-all-start.2) | async-done | bytes 524320 | tf_op jit(solution)/shard_map/all_to_all | solution.py:28
  72.5 2.2 %collective-permute-start.10 = (bf16[256,256]{1,0:T(8,128)(2,1)S(1)}, bf16[256,256]{1,0:T(8,128)(2,1)S(1)}, u32[]{:S(2)}, u32[]{:S(2)}) collective-permute-start(bf16[256,256]{1,0:T(8,128)(2,1)S(1)} %get-tuple-element.32), channel_id=1, source_target_pairs={{16,1},{17,0},{18,3},{19,2},{20,5},{21,4},{22,7},{23,6},{24,9},{25... | collective-permute-start | bytes 393224 | tf_op jit(solution)/shard_map/ppermute | solution.py:35
  74.7 0.0 collective-permute-done.7.got_a_ref
  74.7 5.5 %collective-permute-start.8 = (bf16[256,256]{1,0:T(8,128)(2,1)S(1)}, bf16[256,256]{1,0:T(8,128)(2,1)S(1)}, u32[]{:S(2)}, u32[]{:S(2)}) collective-permute-start(bf16[256,256]{1,0:T(8,128)(2,1)S(1)} %fusion.2), channel_id=1, source_target_pairs={{1,0},{0,1},{3,2},{2,3},{5,4},{4,5},{7,6},{6,7},{9,8},{8,9},{11,10... | collective-permute-start | bytes 393224 | tf_op jit(solution)/shard_map/ppermute | solution.py:39
  80.2 0.8 finish_q.1
  81.0 6.6 %collective-permute-done.10.next_other_ref = bf16[256,256]{1,0:T(8,128)(2,1)S(1)} collective-permute-done((bf16[256,256]{1,0:T(8,128)(2,1)S(1)}, bf16[256,256]{1,0:T(8,128)(2,1)S(1)}, u32[]{:S(2)}, u32[]{:S(2)}) %collective-permute-start.10) | collective-permute-done | bytes 131104 | tf_op jit(solution)/shard_map/ppermute | solution.py:35
  87.6 0.0 collective-permute-done.8.mate_a_ref
  87.6 0.8 finish_kv.1
  (13 shorter events, 0.2 us)
Async XLA Ops:
  2.4 22.0 %collective-permute-start.2 = (bf16[256,256]{1,0:T(8,128)(2,1)}, bf16[256,256]{1,0:T(8,128)(2,1)S(1)}, u32[]{:S(2)}, u32[]{:S(2)}) collective-permute-start(bf16[256,256]{1,0:T(8,128)(2,1)} %get-tuple-element.19), channel_id=1, source_target_pairs={{1,0},{0,1},{3,2},{2,3},{5,4},{4,5},{7,6},{6,7},{9,8},{8,9},{11,10... | collective-permute-start | bytes 393224 | tf_op jit(solution)/shard_map/ppermute | solution.py:39
  4.9 16.2 %collective-permute-start = (bf16[256,256]{1,0:T(8,128)(2,1)}, bf16[256,256]{1,0:T(8,128)(2,1)S(1)}, u32[]{:S(2)}, u32[]{:S(2)}) collective-permute-start(bf16[256,256]{1,0:T(8,128)(2,1)} %get-tuple-element.19), channel_id=1, source_target_pairs={{0,17},{1,16},{2,19},{3,18},{4,21},{5,20},{6,23},{7,22},{8,25},{9,... | collective-permute-start | bytes 393224 | tf_op jit(solution)/shard_map/ppermute | solution.py:35
  9.4 17.1 %collective-permute-start.4 = (bf16[256,256]{1,0:T(8,128)(2,1)}, bf16[256,256]{1,0:T(8,128)(2,1)S(1)}, u32[]{:S(2)}, u32[]{:S(2)}) collective-permute-start(bf16[256,256]{1,0:T(8,128)(2,1)} %get-tuple-element.21.a0_ref), channel_id=1, source_target_pairs={{0,16},{1,17},{2,18},{3,19},{4,20},{5,21},{6,22},{7,23},{8,24},{9,... | collective-permute-start | bytes 393224 | tf_op jit(solution)/shard_map/ppermute | solution.py:35
  15.7 8.7 %copy-start = (bf16[256,256]{1,0:T(8,128)(2,1)S(1)}, bf16[256,256]{1,0:T(8,128)(2,1)}, u32[]{:S(2)}) copy-start(bf16[256,256]{1,0:T(8,128)(2,1)} %get-tuple-element.21.a0_ref) | copy-start | bytes 393220
  15.7 14.1 %copy-start.1 = (s32[256]{0:T(256)S(1)}, s32[256]{0:T(256)}, u32[]{:S(2)}) copy-start(s32[256]{0:T(256)} %param.9) | copy-start | bytes 3076
  15.7 21.1 %all-to-all-start = ((bf16[8,256,256]{2,1,0:T(8,128)(2,1)}), bf16[8,256,256]{2,1,0:T(8,128)(2,1)S(1)}, u32[]{:S(2)}, u32[]{:S(2)}) async-start(bf16[8,256,256]{2,1,0:T(8,128)(2,1)} %pack.1), calls=%async_computation | async-start | bytes 2097152 | tf_op jit(solution)/shard_map/all_to_all | solution.py:28
  21.1 8.6 %collective-permute-start.1 = (bf16[256,256]{1,0:T(8,128)(2,1)S(1)}, bf16[256,256]{1,0:T(8,128)(2,1)S(1)}, u32[]{:S(2)}, u32[]{:S(2)}) collective-permute-start(bf16[256,256]{1,0:T(8,128)(2,1)S(1)} %collective-permute-done.b1_ref), channel_id=1, source_target_pairs={{2,0},{3,1},{0,2},{1,3},{6,4},{7,5},{4,6},{5,7},{10,8},{11,9},{8,1... | collective-permute-start | bytes 393224 | tf_op jit(solution)/shard_map/ppermute | solution.py:39
  24.4 12.3 %collective-permute-start.3 = (bf16[2,256,256]{2,1,0:T(8,128)(2,1)S(1)}, bf16[2,256,256]{2,1,0:T(8,128)(2,1)S(1)}, u32[]{:S(2)}, u32[]{:S(2)}) collective-permute-start(bf16[2,256,256]{2,1,0:T(8,128)(2,1)S(1)} %pad_maximum_fusion), channel_id=1, source_target_pairs={{2,0},{3,1},{0,2},{1,3},{6,4},{7,5},{4,6},{5,7},{10,8},{11,9},{8,1... | collective-permute-start | bytes 786440 | tf_op jit(solution)/shard_map/ppermute | solution.py:39
  26.5 10.2 %collective-permute-start.5 = (bf16[256,256]{1,0:T(8,128)(2,1)S(1)}, bf16[256,256]{1,0:T(8,128)(2,1)S(1)}, u32[]{:S(2)}, u32[]{:S(2)}) collective-permute-start(bf16[256,256]{1,0:T(8,128)(2,1)S(1)} %collective-permute-done.4.b0_ref), channel_id=1, source_target_pairs={{2,0},{3,1},{0,2},{1,3},{6,4},{7,5},{4,6},{5,7},{10,8},{11,9},{8,1... | collective-permute-start | bytes 393224 | tf_op jit(solution)/shard_map/ppermute | solution.py:39
  52.7 10.2 %collective-permute-start.6 = (bf16[2,256,256]{2,1,0:T(8,128)(2,1)}, bf16[2,256,256]{2,1,0:T(8,128)(2,1)S(1)}, u32[]{:S(2)}, u32[]{:S(2)}) collective-permute-start(bf16[2,256,256]{2,1,0:T(8,128)(2,1)} %get-tuple-element.24), channel_id=1, source_target_pairs={{2,0},{3,1},{0,2},{1,3},{6,4},{7,5},{4,6},{5,7},{10,8},{11,9},{8,1... | collective-permute-start | bytes 786440 | tf_op jit(solution)/shard_map/ppermute | solution.py:39
  56.8 15.6 %all-to-all-start.2 = ((bf16[8,128,256]{2,1,0:T(8,128)(2,1)}), bf16[8,128,256]{2,1,0:T(8,128)(2,1)S(1)}, u32[]{:S(2)}, u32[]{:S(2)}) async-start(bf16[8,128,256]{2,1,0:T(8,128)(2,1)} %get-tuple-element.27), calls=%async_computation.2 | async-start | bytes 1048576 | tf_op jit(solution)/shard_map/all_to_all | solution.py:28
  63.0 11.7 %collective-permute-start.7 = (bf16[2,256,256]{2,1,0:T(8,128)(2,1)S(1)}, bf16[2,256,256]{2,1,0:T(8,128)(2,1)S(1)}, u32[]{:S(2)}, u32[]{:S(2)}) collective-permute-start(bf16[2,256,256]{2,1,0:T(8,128)(2,1)S(1)} %get-tuple-element.30), channel_id=1, source_target_pairs={{2,0},{3,1},{0,2},{1,3},{6,4},{7,5},{4,6},{5,7},{10,8},{11,9},{8,1... | collective-permute-start | bytes 786440 | tf_op jit(solution)/shard_map/ppermute | solution.py:39
  64.9 16.1 %collective-permute-start.9 = (bf16[256,256]{1,0:T(8,128)(2,1)S(1)}, bf16[256,256]{1,0:T(8,128)(2,1)S(1)}, u32[]{:S(2)}, u32[]{:S(2)}) collective-permute-start(bf16[256,256]{1,0:T(8,128)(2,1)S(1)} %get-tuple-element.31), channel_id=1, source_target_pairs={{16,0},{17,1},{18,2},{19,3},{20,4},{21,5},{22,6},{23,7},{24,8},{25... | collective-permute-start | bytes 393224 | tf_op jit(solution)/shard_map/ppermute | solution.py:35
  72.5 15.2 %collective-permute-start.10 = (bf16[256,256]{1,0:T(8,128)(2,1)S(1)}, bf16[256,256]{1,0:T(8,128)(2,1)S(1)}, u32[]{:S(2)}, u32[]{:S(2)}) collective-permute-start(bf16[256,256]{1,0:T(8,128)(2,1)S(1)} %get-tuple-element.32), channel_id=1, source_target_pairs={{16,1},{17,0},{18,3},{19,2},{20,5},{21,4},{22,7},{23,6},{24,9},{25... | collective-permute-start | bytes 393224 | tf_op jit(solution)/shard_map/ppermute | solution.py:35
  74.7 12.9 %collective-permute-start.8 = (bf16[256,256]{1,0:T(8,128)(2,1)S(1)}, bf16[256,256]{1,0:T(8,128)(2,1)S(1)}, u32[]{:S(2)}, u32[]{:S(2)}) collective-permute-start(bf16[256,256]{1,0:T(8,128)(2,1)S(1)} %fusion.2), channel_id=1, source_target_pairs={{1,0},{0,1},{3,2},{2,3},{5,4},{4,5},{7,6},{6,7},{9,8},{8,9},{11,10... | collective-permute-start | bytes 393224 | tf_op jit(solution)/shard_map/ppermute | solution.py:39
